TPU v7x, 128 devices: a whole 4x4x4 slice. The times are simulated.
128 devices in a mesh: loader: 4 (over z_hi, core), centers: 32 (over y, z_lo, x).
Axes of the slice: x: 4, y: 4, z: 4 (z_hi: 2, z_lo: 2; z = z_hi * 2 + z_lo), core: 2. Of those that a mesh axis runs over, the one named last changes fastest.
Arguments:
- pool: bfloat16 [32768, 256], P('loader'), may hold values from -6 to 6
- batch_index: int32 [2048], replicated, may hold values from 0 to 32767
- targets: float32 [16, 2048], replicated, may hold values from -6 to 6
- centers: bfloat16 [1048576, 256], P(('loader', 'centers')), may hold values from -6 to 6
- weights: float32 [16, 1048576], P(None, ('loader', 'centers')), may hold values from -1.8 to 1.8
- nys_index: int32 [8192], P(('loader', 'centers')), may hold values from 0 to 8191, as said below
- eigvecs: float32 [8192, 128], P(('loader', 'centers')), may hold values from -0.0625 to 0.0625
- damping: float32 [128], replicated, may hold values from 1 to 30
Outputs:
- new_weights: float32 [16, 1048576], P(None, ('loader', 'centers'))
- predictions: float32 [16, 2048], replicated
Inputs may be any that keep to these rules, and one draw needn't show every extreme that they name: `nys_index`: each device's block of 64 entries names distinct local rows of that device's own 8192 centers; entry k lies in [k * 128, (k + 1) * 128); the first is 0 and the last 8191.
All inputs are finite; a program needn't handle non-finite values.
Results may differ from a plain program's by a relative error of at most 0.0049.
Values may be sent and summed in bfloat16 or wider, within the bound.
No kernel may reach another device: no remote copies, remote signals or barrier semaphores. Data moves between devices by JAX's collectives and lax.ppermute only.
A program may use at most 256 MiB of HBM per device.

v0:
```python
import math

import jax
import jax.numpy as jnp
from jax import lax
from jax.sharding import PartitionSpec as P

D = 256


def pick_rows(pool, wanted):
    held = pool.shape[0]
    local = wanted - lax.axis_index("loader") * held
    owned = (local >= 0) & (local < held)
    rows = pool[jnp.clip(local, 0, held - 1)]
    return jnp.where(owned[:, None], rows, jnp.zeros_like(rows))


def body(pool, batch_index, targets, centers, weights, nys_index, eigvecs, damping):
    total_rows = batch_index.shape[0]
    share = total_rows // lax.axis_size("centers")
    mine = lax.dynamic_slice_in_dim(batch_index, lax.axis_index("centers") * share, share)
    summed = lax.psum(pick_rows(pool, mine), "loader").astype(jnp.float32).astype(jnp.bfloat16)
    batch = lax.all_gather(summed, "centers", axis=0, tiled=True)
    cen_sq = jnp.sum(centers.astype(jnp.float32) * centers.astype(jnp.float32), axis=1)
    width = min(512, total_rows)

    def tile(rows):
        row_sq = jnp.sum(rows.astype(jnp.float32) * rows.astype(jnp.float32), axis=1)
        cross = jnp.dot(rows, centers.T, preferred_element_type=jnp.float32)
        dist_sq = row_sq[:, None] + cen_sq[None, :] - 2.0 * cross
        return jnp.exp(-4.0 * jnp.sqrt(dist_sq) / math.sqrt(D)).astype(jnp.bfloat16)

    kern = lax.map(tile, batch.reshape(total_rows // width, width, batch.shape[1]))
    kern = kern.reshape(total_rows, centers.shape[0])
    w_half = weights.astype(jnp.bfloat16)
    partial_value = lax.dot_general(
        w_half, kern, (((1,), (1,)), ((), ())), preferred_element_type=jnp.float32
    )
    predictions = lax.psum(partial_value, ("loader", "centers"))
    resid = (predictions - targets).astype(jnp.bfloat16)
    grad = jnp.dot(resid, kern, preferred_element_type=jnp.float32)
    grad_nys = grad[:, nys_index]
    local_coeff = jnp.dot(
        grad_nys, eigvecs, precision=lax.Precision.HIGHEST, preferred_element_type=jnp.float32
    )
    coeff = lax.psum(local_coeff, ("loader", "centers"))
    delta = jnp.dot(
        coeff * damping[None, :],
        eigvecs.T,
        precision=lax.Precision.HIGHEST,
        preferred_element_type=jnp.float32,
    )
    fresh = weights - 2.0 * grad
    fresh = fresh.at[:, nys_index].add(2.0 * delta)
    return (fresh, predictions)


def solution(mesh):
    return jax.shard_map(
        body,
        mesh=mesh,
        in_specs=(
            P("loader", None),
            P(),
            P(),
            P(("loader", "centers"), None),
            P(None, ("loader", "centers")),
            P(("loader", "centers")),
            P(("loader", "centers"), None),
            P(),
        ),
        out_specs=(P(None, ("loader", "centers")), P()),
        check_vma=False,
    )
```

profile of v0, /device:TPU:1, one launch (start us, length us, event | category | flops | bytes accessed | tf_op | source)
XLA Modules:
  0.0 498.1 jit_solution(4399989665971109694)
XLA Ops:
  7.2 0.0 all-gather.2.cloned.1.call-start
  7.2 0.8 compare_select_fusion.1
  8.0 0.8 compare_and_fusion
  8.8 3.4 gather_fusion
  12.2 0.1 broadcast_select_fusion
  12.2 15.6 %psum.21 = bf16[64,256]{1,0:T(8,128)(2,1)} all-reduce(bf16[64,256]{1,0:T(8,128)(2,1)S(1)} %broadcast_select_fusion), channel_id=1, replica_groups=mesh['loader'=4,'centers'=32] {'loader'}, use_global_device_ids=true, to_apply=%region_0.1 | all-reduce | flops 16384 | bytes 65536 | tf_op jit(solution)/shard_map/psum | solution.py:23
  27.9 0.0 all-reduce.2.cloned.1.call-start
  28.0 0.7 compare_select_fusion
  28.6 3.3 multiply_reduce_fusion.1
  32.0 127.5 %all-gather.2.cloned.1.call-done = bf16[2048,256]{1,0:T(8,128)(2,1)} async-done(((bf16[64,256]{1,0:T(8,128)(2,1)}), bf16[2048,256]{1,0:T(8,128)(2,1)}) %all-gather.2.cloned.1.call-update) | async-done | bytes 1048592 | tf_op jit(solution)/shard_map/all_gather | solution.py:24
  159.5 58.4 %while.12 = (s32[]{:T(128)}, bf16[4,512,8192]{2,1,0:T(8,128)(2,1)}, bf16[4,512,256]{2,1,0:T(8,128)(2,1)}, f32[8192]{0:T(1024)S(1)}, bf16[8192,256]{1,0:T(8,128)(2,1)}, /*index=5*/s32[]{:T(128)}) while((s32[]{:T(128)}, bf16[4,512,8192]{2,1,0:T(8,128)(2,1)}, bf16[4,512,256]{2,1,0:T(8,128)(2,1)}, f32[8192]{0:T(1024)S(1)}, ...), condition=%wide.region_4.5_spmd, body=%wide.region_2.4_spmd.sunk | while | flops 2168847872 | bytes 13145161 | solution.py:34
  159.5 1.2 multiply_reduce_fusion.3
  160.6 13.5 %fusion.22 = bf16[4,512,8192]{2,1,0:T(8,128)(2,1)} fusion(bf16[4,512,8192]{2,1,0:T(8,128)(2,1)} %get-tuple-element.120, s32[]{:T(128)} %get-tuple-element.119, bf16[8192,256]{1,0:T(8,128)(2,1)} %get-tuple-element.129, f32[8192]{0:T(1024)S(1)} %get-tuple-element.128, f32[512]{0:T(512)S(1)} %multiply_reduce_fusion.3, ...), kind=kOutput, calls=%fused_computation.5.clone.1 | convolution fusion | flops 2168455168 | bytes 12880896 | tf_op jit(solution)/shard_map/while/body/eval_jaxpr/dot_general | solution.py:30
  174.1 1.1 multiply_reduce_fusion.3
  175.2 13.5 %fusion.22 = bf16[4,512,8192]{2,1,0:T(8,128)(2,1)} fusion(bf16[4,512,8192]{2,1,0:T(8,128)(2,1)} %get-tuple-element.120, s32[]{:T(128)} %get-tuple-element.119, bf16[8192,256]{1,0:T(8,128)(2,1)} %get-tuple-element.129, f32[8192]{0:T(1024)S(1)} %get-tuple-element.128, f32[512]{0:T(512)S(1)} %multiply_reduce_fusion.3, ...), kind=kOutput, calls=%fused_computation.5.clone.1 | convolution fusion | flops 2168455168 | bytes 12880896 | tf_op jit(solution)/shard_map/while/body/eval_jaxpr/dot_general | solution.py:30
  188.7 1.1 multiply_reduce_fusion.3
  189.8 13.5 %fusion.22 = bf16[4,512,8192]{2,1,0:T(8,128)(2,1)} fusion(bf16[4,512,8192]{2,1,0:T(8,128)(2,1)} %get-tuple-element.120, s32[]{:T(128)} %get-tuple-element.119, bf16[8192,256]{1,0:T(8,128)(2,1)} %get-tuple-element.129, f32[8192]{0:T(1024)S(1)} %get-tuple-element.128, f32[512]{0:T(512)S(1)} %multiply_reduce_fusion.3, ...), kind=kOutput, calls=%fused_computation.5.clone.1 | convolution fusion | flops 2168455168 | bytes 12880896 | tf_op jit(solution)/shard_map/while/body/eval_jaxpr/dot_general | solution.py:30
  203.3 1.1 multiply_reduce_fusion.3
  204.4 13.5 %fusion.22 = bf16[4,512,8192]{2,1,0:T(8,128)(2,1)} fusion(bf16[4,512,8192]{2,1,0:T(8,128)(2,1)} %get-tuple-element.120, s32[]{:T(128)} %get-tuple-element.119, bf16[8192,256]{1,0:T(8,128)(2,1)} %get-tuple-element.129, f32[8192]{0:T(1024)S(1)} %get-tuple-element.128, f32[512]{0:T(512)S(1)} %multiply_reduce_fusion.3, ...), kind=kOutput, calls=%fused_computation.5.clone.1 | convolution fusion | flops 2168455168 | bytes 12880896 | tf_op jit(solution)/shard_map/while/body/eval_jaxpr/dot_general | solution.py:30
  217.9 15.7 %convolution_bitcast_fusion = f32[16,2048]{1,0:T(8,128)} fusion(bf16[2048,8192]{1,0:T(8,128)(2,1)} %bitcast.28, f32[16,8192]{1,0:T(8,128)S(1)} %copy-done.1), kind=kOutput, calls=%fused_computation.11 | convolution fusion | flops 537001984 | bytes 34209792 | tf_op jit(solution)/shard_map/dot_general | solution.py:37
  233.6 161.8 %all-reduce.2.cloned.1.call-done = f32[16,2048]{1,0:T(8,128)} async-done(((f32[16,2048]{1,0:T(8,128)}), f32[16,2048]{1,0:T(8,128)}) %all-reduce.2.cloned.1.call-update) | async-done | bytes 131088 | tf_op jit(solution)/shard_map/psum | solution.py:40
  395.4 14.8 %multiply_subtract_fusion = (f32[16,8192]{1,0:T(8,128)S(1)}, f32[16,8192]{1,0:T(8,128)S(1)}) fusion(f32[16,8192]{1,0:T(8,128)S(1)} %copy-done.1, bf16[2048,8192]{1,0:T(8,128)(2,1)} %bitcast.29, f32[16,2048]{1,0:T(8,128)} %all-reduce.2.cloned.1.call-done, f32[16,2048]{1,0:T(8,128)S(1)} %copy-done.3), kind=kOutput, calls=%fused_computation.14 | convolution fusion | flops 537198592 | bytes 35389440 | tf_op jit(solution)/shard_map/dot_general | solution.py:42
  410.3 2.6 copy.10
  412.9 2.8 gather_fusion.1
  415.7 0.2 fusion.10
  415.9 63.4 %psum.23 = f32[16,128]{1,0:T(8,128)S(1)} all-reduce(f32[16,128]{1,0:T(8,128)S(1)} %fusion.10), channel_id=1, replica_groups=mesh['loader'=4,'centers'=32] {'loader','centers'}, use_global_device_ids=true, to_apply=%region_6.7 | all-reduce | flops 2048 | bytes 16384 | tf_op jit(solution)/shard_map/psum | solution.py:47
  479.3 0.1 fusion.5
  479.4 0.1 copy.12
  479.5 2.6 copy.11
  482.1 4.9 scatter_fusion
  487.1 3.5 copy.13
  490.6 0.7 copy.25
  (15 shorter events, 0.1 us)
Async XLA Ops:
  7.2 408.5 %copy-start = (f32[64,128]{1,0:T(8,128)S(1)}, f32[64,128]{1,0:T(8,128)}, u32[]{:S(2)}) copy-start(f32[64,128]{1,0:T(8,128)} %param.16) | copy-start | bytes 98308
  7.2 152.3 %all-gather.2.cloned.1.call-start = ((), (), s32[]{:S(2)}) async-start(), calls=%async_computation | async-start | bytes 1081344 | tf_op jit(solution)/shard_map/all_gather | solution.py:24
  27.9 367.5 %all-reduce.2.cloned.1.call-start = ((), (), s32[]{:S(2)}) async-start(), calls=%async_computation.1 | async-start | bytes 262144 | tf_op jit(solution)/shard_map/psum | solution.py:40
  159.5 58.4 %copy-start.1 = (f32[16,8192]{1,0:T(8,128)S(1)}, f32[16,8192]{1,0:T(8,128)}, u32[]{:S(2)}) copy-start(f32[16,8192]{1,0:T(8,128)} %param.14) | copy-start | bytes 1572868
  217.9 177.5 %copy-start.3 = (f32[16,2048]{1,0:T(8,128)S(1)}, f32[16,2048]{1,0:T(8,128)}, u32[]{:S(2)}) copy-start(f32[16,2048]{1,0:T(8,128)} %param.12) | copy-start | bytes 393220
  233.6 245.7 %copy-start.4 = (f32[128]{0:T(128)S(1)}, f32[128]{0:T(128)}, u32[]{:S(2)}) copy-start(f32[128]{0:T(128)} %param.17) | copy-start | bytes 1540
  395.4 95.2 %copy-start.2 = (f32[16,2048]{1,0:T(8,128)S(1)}, f32[16,2048]{1,0:T(8,128)}, u32[]{:S(2)}) copy-start(f32[16,2048]{1,0:T(8,128)} %all-reduce.2.cloned.1.call-done) | copy-start | bytes 393220
Sparse Core Ops, SparseCore 0:
  28.0 131.4 all-gather.1
  233.7 161.6 all-reduce.1
where the time goes:
time: 499 us; the launch traced here: 498 us
  waiting for transfers between devices  289 us (58%)
  matrix products  84.8 us (17%)
  blocking collectives  79.1 us (16%)
  local copies, waits for them, and re-layouts  15.7 us (3%)
  other arithmetic  15 us (3%)
  between operations  14.1 us (3%)
    psum x1, waiting for transfers between devices, body(): predictions = lax.psum(partial_value, ('loader', 'centers'))  162 us
    all_gather x1, waiting for transfers between devices, body(): batch = lax.all_gather(summed, 'centers', axis=0, tiled=True)  128 us
    psum x1, blocking collectives, body(): coeff = lax.psum(local_coeff, ('loader', 'centers'))  63.4 us
    dot_general x4, matrix products, tile(): cross = jnp.dot(rows, centers.T, preferred_element_type=jnp.float32)  54 us
    dot_general x1, matrix products, body(): lax.dot_general(w_half, kern, (((1,), (1,)), ((), ())), preferred_element...  15.7 us
    psum x1, blocking collectives, body(): lax.psum(pick_rows(pool, mine), 'loader').astype(jnp.float32)  15.6 us
    dot_general x1, matrix products, body(): grad = jnp.dot(resid, kern, preferred_element_type=jnp.float32)  14.8 us
  transfers between devices with their start and end apart: 2, of which 2 were waited for; matrix products, arithmetic and copies ran while one was open for 1% of the time, Pallas kernels for 0%

commit v1 on v0

v1 whole, which is shorter than its diff:
```python
import math

import jax
import jax.numpy as jnp
from jax import lax
from jax.experimental import pallas as pl
from jax.experimental.pallas import tpu as pltpu
from jax.sharding import Mesh
from jax.sharding import PartitionSpec as P

f32, bf16 = jnp.float32, jnp.bfloat16
MIB = 2**20
LOADER = ("zh", "core")
CENTERS = ("y", "zl", "x")
ALL = LOADER + CENTERS
D = 256
CHUNKS = 2
LANES = 128
RATE = -4.0 / math.sqrt(D) * math.log2(math.e)
VMEM = pl.BlockSpec(memory_space=pltpu.VMEM)
SMEM = pl.BlockSpec(memory_space=pltpu.SMEM)
NT = (((1,), (1,)), ((), ()))


def laplacian(dist_sq):
    safe = jnp.maximum(dist_sq, 1e-30)
    return jnp.exp2(safe * lax.rsqrt(safe) * RATE).astype(bf16)


def load_rows(core_ref, own_ref, other_ref, rows_ref, sq_ref):
    half = own_ref.shape[0]
    for ref, place in ((own_ref, core_ref[0]), (other_ref, 1 - core_ref[0])):
        at = pl.ds(pl.multiple_of(place * half, half), half)
        rows = ref[...]
        wide = rows.astype(f32)
        rows_ref[at, :] = rows * (-2)
        sq_ref[at, :] = jnp.broadcast_to(jnp.sum(wide * wide, axis=1, keepdims=True), (half, LANES))


def values_kernel(core_ref, w_ref, cen_ref, own_ref, other_ref, cen_sq_ref, kern_ref, pred_ref, rows_ref, sq_ref, acc_ref):
    batch, count = kern_ref.shape
    col, row = 2048, 256
    load_rows(core_ref, own_ref, other_ref, rows_ref, sq_ref)
    acc_ref[...] = jnp.zeros_like(acc_ref)

    def step(i, carry):
        cols = pl.ds(pl.multiple_of(i * col, col), col)
        cen = cen_ref[cols, :]
        w = w_ref[:, cols]
        cen_sq = cen_sq_ref[:, cols]
        for j in range(batch // row):
            at = slice(j * row, (j + 1) * row)
            cross = lax.dot_general(rows_ref[at, :], cen, NT, preferred_element_type=f32)
            row_sq = jnp.concatenate([sq_ref[at, :]] * (col // LANES), axis=1)
            kern = laplacian((cross + row_sq) + cen_sq)
            kern_ref[at, cols] = kern
            acc_ref[:, at] += lax.dot_general(w, kern, NT, preferred_element_type=f32)
        return carry

    lax.fori_loop(0, count // col, step, 0)
    for r in range(batch // LANES):
        pred_ref[:, r, :] = acc_ref[:, r * LANES : (r + 1) * LANES]


def kernel_values(core, w_half, centers, own, other, cen_sq):
    batch, count = 2 * own.shape[0], centers.shape[0]
    return pl.pallas_call(
        values_kernel,
        in_specs=[SMEM] + [VMEM] * 5,
        out_specs=[VMEM, VMEM],
        out_shape=[
            pltpu.VMEM((batch, count), bf16),
            jax.ShapeDtypeStruct((w_half.shape[0], batch // LANES, LANES), f32),
        ],
        scratch_shapes=[
            pltpu.VMEM((batch, D), bf16),
            pltpu.VMEM((batch, LANES), f32),
            pltpu.VMEM((w_half.shape[0], batch), f32),
        ],
        compiler_params=pltpu.CompilerParams(vmem_limit_bytes=16 * MIB),
        cost_estimate=pl.CostEstimate(
            flops=8 * batch * count * D, bytes_accessed=2 * batch * count, transcendentals=2 * batch * count
        ),
        name="kernel_values",
    )(core, w_half, centers, own, other, cen_sq)


def nystrom_kernel(core_ref, cen_ref, sq_ref, hi_ref, lo_ref, *refs):
    pieces, (out_ref, acc_ref) = refs[:-2], refs[-2:]
    cen = cen_ref[...]
    half = pieces[0].shape[0]
    for n, ref in enumerate(pieces):
        place = core_ref[0] if n % 2 == 0 else 1 - core_ref[0]
        first = (n // 2 * 2 + place) * (half // LANES)
        rows = ref[...]
        wide = rows.astype(f32)
        cross = lax.dot_general(rows * (-2), cen, NT, preferred_element_type=f32)
        kern = laplacian((cross + jnp.sum(wide * wide, axis=1, keepdims=True)) + sq_ref[...])
        part = lax.dot_general(hi_ref[...], kern, NT, preferred_element_type=f32)
        part += lax.dot_general(lo_ref[...], kern, NT, preferred_element_type=f32)
        for r in range(half // LANES):
            acc_ref[:, pl.ds(first + r, 1), :] = part[:, None, r * LANES : (r + 1) * LANES]
    out_ref[...] = acc_ref[...].astype(bf16)


def nystrom_terms(core, nys_cen, eigvecs, pieces):
    wide = nys_cen.astype(f32)
    nys_sq = jnp.sum(wide * wide, axis=1)[None, :]
    eig_t = eigvecs.T
    hi = eig_t.astype(bf16)
    lo = (eig_t - hi.astype(f32)).astype(bf16)
    blocks = sum(p.shape[0] for p in pieces) // LANES
    shape = (eig_t.shape[0], blocks, LANES)
    return pl.pallas_call(
        nystrom_kernel,
        in_specs=[SMEM] + [VMEM] * (4 + len(pieces)),
        out_specs=VMEM,
        out_shape=jax.ShapeDtypeStruct(shape, bf16),
        scratch_shapes=[pltpu.VMEM(shape, f32)],
        compiler_params=pltpu.CompilerParams(vmem_limit_bytes=12 * MIB),
        cost_estimate=pl.CostEstimate(flops=2 * 10**9, bytes_accessed=2**20, transcendentals=2**18),
        name="nystrom_terms",
    )(core, nys_cen, nys_sq, hi, lo, *pieces)


def grad_kernel(pred_ref, tgt_ref, kern_ref, out_pred_ref, resid_ref, out_ref):
    count = kern_ref.shape[1]
    col = 1024
    for r in range(pred_ref.shape[1]):
        at = slice(r * LANES, (r + 1) * LANES)
        pred = pred_ref[:, r, :]
        out_pred_ref[:, at] = pred
        resid_ref[:, at] = (pred - tgt_ref[:, at]).astype(bf16)
    resid = resid_ref[...]
    for i in range(count // col):
        at = slice(i * col, (i + 1) * col)
        out_ref[:, at] = jnp.dot(resid, kern_ref[:, at], preferred_element_type=f32)


def grad_terms(pred, targets, kern):
    outs, count = targets.shape[0], kern.shape[1]
    return pl.pallas_call(
        grad_kernel,
        in_specs=[VMEM] * 3,
        out_specs=[VMEM] * 3,
        out_shape=[
            jax.ShapeDtypeStruct(targets.shape, f32),
            jax.ShapeDtypeStruct(targets.shape, bf16),
            jax.ShapeDtypeStruct((outs, count), f32),
        ],
        compiler_params=pltpu.CompilerParams(vmem_limit_bytes=8 * MIB),
        cost_estimate=pl.CostEstimate(flops=32 * kern.size, bytes_accessed=2 * kern.size, transcendentals=0),
        name="grad_terms",
    )(pred, targets, kern)


def update_kernel(idx_ref, damp_ref, eig_ref, w_ref, *refs):
    n = (len(refs) - 1) // 3
    grads, resids, moments, out_ref = refs[:n], refs[n : 2 * n], refs[2 * n : 3 * n], refs[-1]
    coeff = 0.0
    for resid_ref, moment_ref in zip(resids, moments):
        for r in range(moment_ref.shape[0]):
            at = slice(r * LANES, (r + 1) * LANES)
            coeff += lax.dot_general(resid_ref[:, at], moment_ref[r], NT, preferred_element_type=f32)
    delta = lax.dot_general(
        coeff * damp_ref[...], eig_ref[...], NT, precision=lax.Precision.HIGHEST, preferred_element_type=f32
    )
    lane = lax.broadcasted_iota(jnp.int32, (w_ref.shape[0], LANES), 1)
    for k in range(delta.shape[1]):
        at = slice(k * LANES, (k + 1) * LANES)
        total = grads[0][:, at]
        for grad_ref in grads[1:]:
            total += grad_ref[:, at]
        shift = jnp.where(lane == idx_ref[k] - k * LANES, 2.0 * delta[:, k : k + 1], 0.0)
        out_ref[:, at] = (w_ref[:, at] - 2.0 * total) + shift


def update(nys_index, damping, eigvecs, weights, grads, resids, moments):
    return pl.pallas_call(
        update_kernel,
        in_specs=[SMEM] + [VMEM] * (3 + 3 * len(grads)),
        out_specs=VMEM,
        out_shape=jax.ShapeDtypeStruct(weights.shape, f32),
        compiler_params=pltpu.CompilerParams(vmem_limit_bytes=12 * MIB),
        name="update",
    )(nys_index, damping[None, :], eigvecs, weights, *grads, *resids, *moments)


def pick_rows(pool, wanted):
    held = pool.shape[0]
    local = wanted - lax.axis_index(LOADER) * held
    owned = (local >= 0) & (local < held)
    rows = pool[jnp.clip(local, 0, held - 1)]
    return jnp.where(owned[:, None], rows, jnp.zeros_like(rows))


def swap(x, axis):
    return lax.ppermute(x, axis, [(0, 1), (1, 0)])


def exchange(x, axes):
    return lax.all_to_all(x, axes, split_axis=0, concat_axis=0, tiled=True)


def spread(x, axes):
    return exchange(jnp.broadcast_to(x[None], (lax.axis_size(axes),) + x.shape), axes)


def body(pool, batch_index, targets, centers, weights, nys_index, eigvecs, damping):
    outs, total = targets.shape
    core = lax.axis_index("core")
    groups = lax.axis_size(CENTERS)
    share = total // (CHUNKS * 2 * groups)
    mine = lax.dynamic_index_in_dim(
        batch_index.reshape(CHUNKS * 2, groups, share), lax.axis_index(CENTERS), 1, keepdims=False
    )
    rows = pick_rows(pool, mine.reshape(-1)).reshape(CHUNKS, 2, share, D)
    keep = lax.dynamic_index_in_dim(rows, core, 1, keepdims=False)
    give = lax.dynamic_index_in_dim(rows, 1 - core, 1, keepdims=False)
    rows = keep + swap(give, "core")
    rows = rows + swap(rows, "zh")
    own = [spread(rows[q], CENTERS).reshape(groups * share, D) for q in range(CHUNKS)]
    other = [swap(x, "core") for x in own]

    wide = centers.astype(f32)
    cen_sq = jnp.sum(wide * wide, axis=1)[None, :]
    w_half = weights.astype(bf16)
    where = core.astype(jnp.int32)[None]

    pieces = [p for pair in zip(own, other) for p in pair]
    moment = nystrom_terms(where, centers[nys_index], eigvecs, pieces)
    moment = jnp.sum(exchange(moment, ALL).astype(f32), axis=0).astype(bf16)
    moment = jnp.transpose(spread(moment, ALL), (1, 0, 2))

    preds, grads, resids, moments = [], [], [], []
    width = total // CHUNKS
    for q in range(CHUNKS):
        kern, pred = kernel_values(where, w_half, centers, own[q], other[q], cen_sq)
        shape = pred.shape
        pred = jnp.sum(exchange(pred.reshape(-1, 1, LANES), ALL), axis=0)
        pred = spread(pred, ALL).reshape(shape)
        pred, resid, grad = grad_terms(pred, targets[:, q * width : (q + 1) * width], kern)
        preds.append(pred)
        resids.append(resid)
        grads.append(grad)
        moments.append(moment[q * (width // LANES) : (q + 1) * (width // LANES)])
    fresh = update(nys_index, damping, eigvecs, weights, grads, resids, moments)
    return fresh, jnp.concatenate(preds, axis=1)


def solution(mesh):
    fine = Mesh(mesh.devices.reshape(2, 2, 4, 2, 4), ALL)
    return jax.shard_map(
        body,
        mesh=fine,
        in_specs=(
            P(LOADER, None),
            P(),
            P(),
            P(ALL, None),
            P(None, ALL),
            P(ALL),
            P(ALL, None),
            P(),
        ),
        out_specs=(P(None, ALL), P()),
        check_vma=False,
    )
```

time: 499 us -> 184 us (0.37)
  waiting for transfers between devices: 289 us -> 48.2 us
  matrix products: 84.8 us -> 0 us
  blocking collectives: 79.1 us -> 0 us
  starting transfers between devices: 0.08 us -> 57.1 us
  Pallas kernels: 0 us -> 35.1 us
  local copies, waits for them, and re-layouts: 15.7 us -> 36.7 us
  between operations: 14.1 us -> 0.93 us
  other arithmetic: 15 us -> 4.8 us
    psum x1 -> x0, waiting for transfers between devices: 162 us -> none  [body(): predictions = lax.psum(partial_value, ('loader', 'centers'))]
    all_gather x1 -> x0, waiting for transfers between devices: 128 us -> none  [body(): batch = lax.all_gather(summed, 'centers', axis=0, tiled=True)]
    dot_general x8 -> x0, matrix products: 84.8 us -> none  [the longest x4 54 us: tile(): cross = jnp.dot(rows, centers.T, preferred_element_type=jnp.float32)]
    psum x2 -> x0, blocking collectives: 79.1 us -> none  [the longest x1 63.4 us: body(): coeff = lax.psum(local_coeff, ('loader', 'centers'))]
    all_to_all x0 -> x8, waiting for transfers between devices: none -> 46.3 us  [exchange(): return lax.all_to_all(x, axes, split_axis=0, concat_axis=0, tiled=True)]
    all_to_all x0 -> x8, starting transfers between devices: none -> 44.9 us  [exchange(): return lax.all_to_all(x, axes, split_axis=0, concat_axis=0, tiled=True)]
    pallas_call x0 -> x6, Pallas kernels: none -> 35.1 us  [the longest x2 26 us: kernel_values(): pl.pallas_call(values_kernel, in_specs=[SMEM] + [VMEM] * 5, out_specs=[VM...]
    unnamed x12 -> x23, local copies, waits for them, and re-layouts: 4.18 us -> 25.2 us
  transfers between devices with their start and end apart: 2 -> 12, of which waited for: 2 -> 8; matrix products, arithmetic and copies ran while one was open for 1% -> 4% of each run, Pallas kernels for 0% -> 18%
where the time goes in v1:
time: 184 us; the launch traced here: 183 us
  starting transfers between devices  57.1 us (31%)
  waiting for transfers between devices  48.2 us (26%)
  local copies, waits for them, and re-layouts  36.7 us (20%)
  Pallas kernels  35.1 us (19%)
  other arithmetic  4.8 us (3%)
    all_to_all x8, waiting for transfers between devices, exchange(): return lax.all_to_all(x, axes, split_axis=0, concat_axis=0, tiled=True)  46.3 us
    all_to_all x8, starting transfers between devices, exchange(): return lax.all_to_all(x, axes, split_axis=0, concat_axis=0, tiled=True)  44.9 us
    pallas_call x2, Pallas kernels, kernel_values(): pl.pallas_call(values_kernel, in_specs=[SMEM] + [VMEM] * 5, out_specs=[VM...  26 us
    unnamed x23, local copies, waits for them, and re-layouts  25.2 us
    ppermute x4, starting transfers between devices, swap(): return lax.ppermute(x, axis, [(0, 1), (1, 0)])  12.2 us
    pallas_call x2, Pallas kernels, grad_terms(): pl.pallas_call(grad_kernel, in_specs=[VMEM] * 3, out_specs=[VMEM] * 3, ou...  4.6 us
  transfers between devices with their start and end apart: 12, of which 8 were waited for; matrix products, arithmetic and copies ran while one was open for 4% of the time, Pallas kernels for 18%

profile of v1, /device:TPU:1, one launch (start us, length us, event | category | flops | bytes accessed | tf_op | source)
XLA Modules:
  0.0 182.8 jit_solution(17402886697526358032)
XLA Ops:
  1.7 3.4 %gather_fusion = bf16[64,256]{1,0:T(8,128)(2,1)S(1)} fusion(bf16[8192,256]{1,0:T(8,128)(2,1)} %param.8, s32[1024]{0:T(1024)S(1)} %pad_clamp_fusion.1), kind=kCustom, calls=%fused_computation | custom fusion | bytes 65792 | tf_op jit(solution)/shard_map/gather | solution.py:193
  7.5 3.7 %collective-permute-start.1 = (bf16[2,16,256]{2,1,0:T(8,128)(2,1)S(1)}, bf16[2,16,256]{2,1,0:T(8,128)(2,1)S(1)}, u32[]{:S(2)}, u32[]{:S(2)}) collective-permute-start(bf16[2,16,256]{2,1,0:T(8,128)(2,1)S(1)} %bitcast_add_fusion), channel_id=1, source_target_pairs={{0,64},{64,0},{1,65},{65,1},{2,66},{66,2},{3,67},{67,3},{4,68},{68... | collective-permute-start | bytes 49160 | tf_op jit(solution)/shard_map/ppermute | solution.py:198
  13.1 7.8 %all-to-all-start.3 = ((bf16[32,16,256]{2,1,0:T(8,128)(2,1)}), bf16[32,16,256]{2,1,0:T(8,128)(2,1)S(1)}, u32[]{:S(2)}, u32[]{:S(2)}) async-start(bf16[32,16,256]{2,1,0:T(8,128)(2,1)} %broadcast_in_dim.69), calls=%async_computation.3 | async-start | bytes 524288 | tf_op jit(solution)/shard_map/all_to_all | solution.py:202
  20.9 3.3 %multiply_reduce_fusion = f32[8192]{0:T(1024)S(1)} fusion(bf16[8192,256]{1,0:T(8,128)(2,1)} %cen_ref.3), kind=kLoop, calls=%fused_computation.2 | loop fusion | flops 6283264 | bytes 4227072 | tf_op jit(solution)/shard_map/reduce_sum | solution.py:226
  24.2 4.7 %all-to-all-done.3 = bf16[32,16,256]{2,1,0:T(8,128)(2,1)S(1)} async-done(((bf16[32,16,256]{2,1,0:T(8,128)(2,1)}), bf16[32,16,256]{2,1,0:T(8,128)(2,1)S(1)}, u32[]{:S(2)}, u32[]{:S(2)}) %all-to-all-start.3) | async-done | bytes 262176 | tf_op jit(solution)/shard_map/all_to_all | solution.py:202
  29.7 3.9 %all-to-all-start = ((bf16[32,16,256]{2,1,0:T(8,128)(2,1)}), bf16[32,16,256]{2,1,0:T(8,128)(2,1)S(1)}, u32[]{:S(2)}, u32[]{:S(2)}) async-start(bf16[32,16,256]{2,1,0:T(8,128)(2,1)} %broadcast_in_dim.65), calls=%async_computation | async-start | bytes 524288 | tf_op jit(solution)/shard_map/all_to_all | solution.py:202
  33.6 3.0 %collective-permute-start.3 = (bf16[512,256]{1,0:T(8,128)(2,1)S(1)}, bf16[512,256]{1,0:T(8,128)(2,1)S(1)}, u32[]{:S(2)}, u32[]{:S(2)}) collective-permute-start(bf16[512,256]{1,0:T(8,128)(2,1)S(1)} %bitcast.36), channel_id=1, source_target_pairs={{0,32},{32,0},{1,33},{33,1},{2,34},{34,2},{3,35},{35,3},{4,36},{36... | collective-permute-start | bytes 786440 | tf_op jit(solution)/shard_map/ppermute | solution.py:198
  36.5 3.4 %gather_fusion.1 = bf16[64,256]{1,0:T(8,128)(2,1)S(1)} fusion(bf16[8192,256]{1,0:T(8,128)(2,1)} %cen_ref.3, s32[1024]{0:T(1024)S(1)} %pad_clamp_fusion), kind=kCustom, calls=%fused_computation.1 | custom fusion | bytes 65792 | tf_op jit(solution)/shard_map/gather | solution.py:231
  40.1 1.6 all-to-all-done
  41.7 4.0 %collective-permute-start.2 = (bf16[512,256]{1,0:T(8,128)(2,1)S(1)}, bf16[512,256]{1,0:T(8,128)(2,1)S(1)}, u32[]{:S(2)}, u32[]{:S(2)}) collective-permute-start(bf16[512,256]{1,0:T(8,128)(2,1)S(1)} %bitcast.39), channel_id=1, source_target_pairs={{0,32},{32,0},{1,33},{33,1},{2,34},{34,2},{3,35},{35,3},{4,36},{36... | collective-permute-start | bytes 786440 | tf_op jit(solution)/shard_map/ppermute | solution.py:198
  45.7 2.2 %copy-done.4 = bf16[8192,256]{1,0:T(8,128)(2,1)S(1)} copy-done((bf16[8192,256]{1,0:T(8,128)(2,1)S(1)}, bf16[8192,256]{1,0:T(8,128)(2,1)}, u32[]{:S(2)}) %copy-start.4) | copy-done | bytes 4194328
  47.9 13.0 %kernel_values.3 = (bf16[1024,8192]{1,0:T(8,128)(2,1)S(1)}, f32[16,8,128]{2,1,0:T(8,128)}) custom-call(s32[1]{0:T(128)} %bitcast.1.core_ref, bf16[16,8192]{1,0:T(8,128)(2,1)S(1)} %convert_element_type.20.w_ref, bf16[8192,256]{1,0:T(8,128)(2,1)S(1)} %copy-done.4, bf16[512,256]{1,0:T(8,128)(2,1)S(1)} %bitcast.37, ...), custom_call_target="tpu_custom_call" | custom-call | flops 17179869184 | bytes 16777216 | tf_op jit(solution)/shard_map/kernel_values/pallas_call | solution.py:67
  60.9 5.7 %copy-done = bf16[1024,8192]{1,0:T(8,128)(2,1)} copy-done((bf16[1024,8192]{1,0:T(8,128)(2,1)}, bf16[1024,8192]{1,0:T(8,128)(2,1)S(1)}, u32[]{:S(2)}) %copy-start) | copy-done | bytes 16777240
  66.6 5.7 %all-to-all-start.4 = ((f32[128,1,128]{2,1,0:T(1,128)}), f32[128,1,128]{2,1,0:T(1,128)S(1)}, u32[]{:S(2)}, u32[]{:S(2)}) async-start(f32[128,1,128]{2,1,0:T(1,128)} %bitcast.15), calls=%async_computation.4 | async-start | bytes 131072 | tf_op jit(solution)/shard_map/all_to_all | solution.py:202
  72.3 2.2 %copy-done.5 = bf16[8192,256]{1,0:T(8,128)(2,1)S(1)} copy-done((bf16[8192,256]{1,0:T(8,128)(2,1)S(1)}, bf16[8192,256]{1,0:T(8,128)(2,1)}, u32[]{:S(2)}) %copy-start.5) | copy-done | bytes 4194328
  74.5 13.0 %kernel_values.2 = (bf16[1024,8192]{1,0:T(8,128)(2,1)S(1)}, f32[16,8,128]{2,1,0:T(8,128)}) custom-call(s32[1]{0:T(128)} %bitcast.1.core_ref, bf16[16,8192]{1,0:T(8,128)(2,1)S(1)} %convert_element_type.20.w_ref, bf16[8192,256]{1,0:T(8,128)(2,1)S(1)} %copy-done.5, bf16[512,256]{1,0:T(8,128)(2,1)S(1)} %bitcast.40, ...), custom_call_target="tpu_custom_call" | custom-call | flops 17179869184 | bytes 16777216 | tf_op jit(solution)/shard_map/kernel_values/pallas_call | solution.py:67
  87.5 5.7 %copy-done.2 = bf16[1024,8192]{1,0:T(8,128)(2,1)} copy-done((bf16[1024,8192]{1,0:T(8,128)(2,1)}, bf16[1024,8192]{1,0:T(8,128)(2,1)S(1)}, u32[]{:S(2)}) %copy-start.2) | copy-done | bytes 16777240
  93.2 9.8 %all-to-all-start.1 = ((f32[128,1,128]{2,1,0:T(1,128)}), f32[128,1,128]{2,1,0:T(1,128)S(1)}, u32[]{:S(2)}, u32[]{:S(2)}) async-start(f32[128,1,128]{2,1,0:T(1,128)} %bitcast.10), calls=%async_computation.1 | async-start | bytes 131072 | tf_op jit(solution)/shard_map/all_to_all | solution.py:202
  103.3 9.4 %all-to-all-done.1 = f32[128,1,128]{2,1,0:T(1,128)S(1)} async-done(((f32[128,1,128]{2,1,0:T(1,128)}), f32[128,1,128]{2,1,0:T(1,128)S(1)}, u32[]{:S(2)}, u32[]{:S(2)}) %all-to-all-start.1) | async-done | bytes 65568 | tf_op jit(solution)/shard_map/all_to_all | solution.py:202
  113.4 4.4 %all-to-all-start.5 = ((f32[128,1,128]{2,1,0:T(1,128)}), f32[128,1,128]{2,1,0:T(1,128)S(1)}, u32[]{:S(2)}, u32[]{:S(2)}) async-start(f32[128,1,128]{2,1,0:T(1,128)} %broadcast_in_dim.70), calls=%async_computation.5 | async-start | bytes 131072 | tf_op jit(solution)/shard_map/all_to_all | solution.py:202
  117.8 2.2 %nystrom_terms.1 = bf16[128,16,128]{2,1,0:T(8,128)(2,1)} custom-call(s32[1]{0:T(128)} %bitcast.1.core_ref, bf16[64,256]{1,0:T(8,128)(2,1)S(1)} %gather_fusion.1, f32[1,64]{1,0:T(1,128)S(1)} %bitcast.45, bf16[128,64]{1,0:T(8,128)(2,1)S(1)} %get-tuple-element.23.hi_ref, bf16[128,64]{1,0:T(8,128)(2,1)S(1)} %get-tuple-element.22.lo_ref, ...), custom_call_target="tpu_custom_call" | custom-call | flops 2000000000 | bytes 1048576 | tf_op jit(solution)/shard_map/nystrom_terms/pallas_call | solution.py:114
  120.0 7.5 %all-to-all-done.5 = f32[128,1,128]{2,1,0:T(1,128)S(1)} async-done(((f32[128,1,128]{2,1,0:T(1,128)}), f32[128,1,128]{2,1,0:T(1,128)S(1)}, u32[]{:S(2)}, u32[]{:S(2)}) %all-to-all-start.5) | async-done | bytes 65568 | tf_op jit(solution)/shard_map/all_to_all | solution.py:202
  127.4 4.4 %all-to-all-start.6 = ((bf16[128,16,128]{2,1,0:T(8,128)(2,1)}), bf16[128,16,128]{2,1,0:T(8,128)(2,1)S(1)}, u32[]{:S(2)}, u32[]{:S(2)}) async-start(bf16[128,16,128]{2,1,0:T(8,128)(2,1)} %nystrom_terms.1), calls=%async_computation.6 | async-start | bytes 1048576 | tf_op jit(solution)/shard_map/all_to_all | solution.py:202
  132.0 13.6 %all-to-all-done.6 = bf16[128,16,128]{2,1,0:T(8,128)(2,1)S(1)} async-done(((bf16[128,16,128]{2,1,0:T(8,128)(2,1)}), bf16[128,16,128]{2,1,0:T(8,128)(2,1)S(1)}, u32[]{:S(2)}, u32[]{:S(2)}) %all-to-all-start.6) | async-done | bytes 524320 | tf_op jit(solution)/shard_map/all_to_all | solution.py:202
  146.2 4.6 %all-to-all-start.2 = ((f32[128,1,128]{2,1,0:T(1,128)}), f32[128,1,128]{2,1,0:T(1,128)S(1)}, u32[]{:S(2)}, u32[]{:S(2)}) async-start(f32[128,1,128]{2,1,0:T(1,128)} %broadcast_in_dim.67), calls=%async_computation.2 | async-start | bytes 131072 | tf_op jit(solution)/shard_map/all_to_all | solution.py:202
  151.0 9.5 %all-to-all-done.2 = f32[128,1,128]{2,1,0:T(1,128)S(1)} async-done(((f32[128,1,128]{2,1,0:T(1,128)}), f32[128,1,128]{2,1,0:T(1,128)S(1)}, u32[]{:S(2)}, u32[]{:S(2)}) %all-to-all-start.2) | async-done | bytes 65568 | tf_op jit(solution)/shard_map/all_to_all | solution.py:202
  161.4 4.4 %all-to-all-start.7 = ((bf16[128,16,128]{2,1,0:T(8,128)(2,1)}), bf16[128,16,128]{2,1,0:T(8,128)(2,1)S(1)}, u32[]{:S(2)}, u32[]{:S(2)}) async-start(bf16[128,16,128]{2,1,0:T(8,128)(2,1)} %broadcast_in_dim.73), calls=%async_computation.7 | async-start | bytes 1048576 | tf_op jit(solution)/shard_map/all_to_all | solution.py:202
  165.9 5.8 %copy-done.1 = bf16[1024,8192]{1,0:T(8,128)(2,1)S(1)} copy-done((bf16[1024,8192]{1,0:T(8,128)(2,1)S(1)}, bf16[1024,8192]{1,0:T(8,128)(2,1)}, u32[]{:S(2)}) %copy-start.1) | copy-done | bytes 16777240
  171.6 2.3 %grad_terms.3 = (f32[16,1024]{1,0:T(8,128)S(1)}, bf16[16,1024]{1,0:T(8,128)(2,1)S(1)}, f32[16,8192]{1,0:T(8,128)S(1)}) custom-call(f32[16,8,128]{2,1,0:T(8,128)S(1)} %bitcast.34, f32[16,1024]{1,0:T(8,128)S(1)} %get-tuple-element.26.tgt_ref, bf16[1024,8192]{1,0:T(8,128)(2,1)S(1)} %copy-done.1), custom_call_target="tpu_custom_call" | custom-call | flops 268435456 | bytes 16777216 | tf_op jit(solution)/shard_map/grad_terms/pallas_call | solution.py:142
  173.9 3.5 %copy-done.3 = bf16[1024,8192]{1,0:T(8,128)(2,1)S(1)} copy-done((bf16[1024,8192]{1,0:T(8,128)(2,1)S(1)}, bf16[1024,8192]{1,0:T(8,128)(2,1)}, u32[]{:S(2)}) %copy-start.3) | copy-done | bytes 16777240
  177.4 2.3 %grad_terms.2 = (f32[16,1024]{1,0:T(8,128)S(1)}, bf16[16,1024]{1,0:T(8,128)(2,1)S(1)}, f32[16,8192]{1,0:T(8,128)S(1)}) custom-call(f32[16,8,128]{2,1,0:T(8,128)S(1)} %bitcast.35, f32[16,1024]{1,0:T(8,128)S(1)} %get-tuple-element.27.tgt_ref, bf16[1024,8192]{1,0:T(8,128)(2,1)S(1)} %copy-done.3), custom_call_target="tpu_custom_call" | custom-call | flops 268435456 | bytes 16777216 | tf_op jit(solution)/shard_map/grad_terms/pallas_call | solution.py:142
  180.6 2.2 %update.1 = f32[16,8192]{1,0:T(8,128)} custom-call(s32[64]{0:T(128)S(1)} %copy-done.8, f32[1,128]{1,0:T(1,128)S(1)} %bitcast.44, f32[64,128]{1,0:T(8,128)S(1)} %copy-done.7, f32[16,8192]{1,0:T(8,128)S(1)} %copy-done.6, f32[16,8192]{1,0:T(8,128)S(1)} %get-tuple-element.14.refs_0_, f32[16,8192]{1,0:T(8,128)S(1)} %get-tuple-element.17.refs_1_, ...), custom_call_target="tpu_custom_call" | custom-call | tf_op jit(solution)/shard_map/update/pallas_call | solution.py:179
  (53 shorter events, 9.8 us)
Async XLA Ops:
  0.6 23.6 %copy-start.8 = (s32[64]{0:T(128)S(1)}, s32[64]{0:T(128)}, u32[]{:S(2)}) copy-start(s32[64]{0:T(128)} %idx_ref.1) | copy-start | bytes 772
  0.6 39.3 %copy-start.7 = (f32[64,128]{1,0:T(8,128)S(1)}, f32[64,128]{1,0:T(8,128)}, u32[]{:S(2)}) copy-start(f32[64,128]{1,0:T(8,128)} %eig_ref.1) | copy-start | bytes 98308
  0.7 39.4 %copy-start.6 = (f32[16,8192]{1,0:T(8,128)S(1)}, f32[16,8192]{1,0:T(8,128)}, u32[]{:S(2)}) copy-start(f32[16,8192]{1,0:T(8,128)} %w_ref.1) | copy-start | bytes 1572868
  5.2 2.3 %collective-permute-start = (bf16[2,16,256]{2,1,0:T(8,128)(2,1)S(1)}, bf16[2,16,256]{2,1,0:T(8,128)(2,1)S(1)}, u32[]{:S(2)}, u32[]{:S(2)}) collective-permute-start(bf16[2,16,256]{2,1,0:T(8,128)(2,1)S(1)} %dynamic-slice_bitcast_fusion), channel_id=1, source_target_pairs={{0,32},{32,0},{1,33},{33,1},{2,34},{34,2},{3,35},{35,3},{4,36},{36... | collective-permute-start | bytes 49160 | tf_op jit(solution)/shard_map/ppermute | solution.py:198
  7.5 4.8 %collective-permute-start.1 = (bf16[2,16,256]{2,1,0:T(8,128)(2,1)S(1)}, bf16[2,16,256]{2,1,0:T(8,128)(2,1)S(1)}, u32[]{:S(2)}, u32[]{:S(2)}) collective-permute-start(bf16[2,16,256]{2,1,0:T(8,128)(2,1)S(1)} %bitcast_add_fusion), channel_id=1, source_target_pairs={{0,64},{64,0},{1,65},{65,1},{2,66},{66,2},{3,67},{67,3},{4,68},{68... | collective-permute-start | bytes 49160 | tf_op jit(solution)/shard_map/ppermute | solution.py:198
  13.1 15.9 %all-to-all-start.3 = ((bf16[32,16,256]{2,1,0:T(8,128)(2,1)}), bf16[32,16,256]{2,1,0:T(8,128)(2,1)S(1)}, u32[]{:S(2)}, u32[]{:S(2)}) async-start(bf16[32,16,256]{2,1,0:T(8,128)(2,1)} %broadcast_in_dim.69), calls=%async_computation.3 | async-start | bytes 524288 | tf_op jit(solution)/shard_map/all_to_all | solution.py:202
  29.7 12.0 %all-to-all-start = ((bf16[32,16,256]{2,1,0:T(8,128)(2,1)}), bf16[32,16,256]{2,1,0:T(8,128)(2,1)S(1)}, u32[]{:S(2)}, u32[]{:S(2)}) async-start(bf16[32,16,256]{2,1,0:T(8,128)(2,1)} %broadcast_in_dim.65), calls=%async_computation | async-start | bytes 524288 | tf_op jit(solution)/shard_map/all_to_all | solution.py:202
  33.6 12.1 %collective-permute-start.3 = (bf16[512,256]{1,0:T(8,128)(2,1)S(1)}, bf16[512,256]{1,0:T(8,128)(2,1)S(1)}, u32[]{:S(2)}, u32[]{:S(2)}) collective-permute-start(bf16[512,256]{1,0:T(8,128)(2,1)S(1)} %bitcast.36), channel_id=1, source_target_pairs={{0,32},{32,0},{1,33},{33,1},{2,34},{34,2},{3,35},{35,3},{4,36},{36... | collective-permute-start | bytes 786440 | tf_op jit(solution)/shard_map/ppermute | solution.py:198
  41.7 30.6 %collective-permute-start.2 = (bf16[512,256]{1,0:T(8,128)(2,1)S(1)}, bf16[512,256]{1,0:T(8,128)(2,1)S(1)}, u32[]{:S(2)}, u32[]{:S(2)}) collective-permute-start(bf16[512,256]{1,0:T(8,128)(2,1)S(1)} %bitcast.39), channel_id=1, source_target_pairs={{0,32},{32,0},{1,33},{33,1},{2,34},{34,2},{3,35},{35,3},{4,36},{36... | collective-permute-start | bytes 786440 | tf_op jit(solution)/shard_map/ppermute | solution.py:198
  45.7 2.2 %copy-start.4 = (bf16[8192,256]{1,0:T(8,128)(2,1)S(1)}, bf16[8192,256]{1,0:T(8,128)(2,1)}, u32[]{:S(2)}) copy-start(bf16[8192,256]{1,0:T(8,128)(2,1)} %cen_ref.3) | copy-start | bytes 12582916
  60.9 5.7 %copy-start = (bf16[1024,8192]{1,0:T(8,128)(2,1)}, bf16[1024,8192]{1,0:T(8,128)(2,1)S(1)}, u32[]{:S(2)}) copy-start(bf16[1024,8192]{1,0:T(8,128)(2,1)S(1)} %get-tuple-element.16.kern_ref) | copy-start | bytes 50331652
  66.6 26.6 %all-to-all-start.4 = ((f32[128,1,128]{2,1,0:T(1,128)}), f32[128,1,128]{2,1,0:T(1,128)S(1)}, u32[]{:S(2)}, u32[]{:S(2)}) async-start(f32[128,1,128]{2,1,0:T(1,128)} %bitcast.15), calls=%async_computation.4 | async-start | bytes 131072 | tf_op jit(solution)/shard_map/all_to_all | solution.py:202
  72.3 2.2 %copy-start.5 = (bf16[8192,256]{1,0:T(8,128)(2,1)S(1)}, bf16[8192,256]{1,0:T(8,128)(2,1)}, u32[]{:S(2)}) copy-start(bf16[8192,256]{1,0:T(8,128)(2,1)} %cen_ref.3) | copy-start | bytes 12582916
  87.5 5.7 %copy-start.2 = (bf16[1024,8192]{1,0:T(8,128)(2,1)}, bf16[1024,8192]{1,0:T(8,128)(2,1)S(1)}, u32[]{:S(2)}) copy-start(bf16[1024,8192]{1,0:T(8,128)(2,1)S(1)} %get-tuple-element.13.kern_ref) | copy-start | bytes 50331652
  93.2 19.4 %all-to-all-start.1 = ((f32[128,1,128]{2,1,0:T(1,128)}), f32[128,1,128]{2,1,0:T(1,128)S(1)}, u32[]{:S(2)}, u32[]{:S(2)}) async-start(f32[128,1,128]{2,1,0:T(1,128)} %bitcast.10), calls=%async_computation.1 | async-start | bytes 131072 | tf_op jit(solution)/shard_map/all_to_all | solution.py:202
  113.4 14.1 %all-to-all-start.5 = ((f32[128,1,128]{2,1,0:T(1,128)}), f32[128,1,128]{2,1,0:T(1,128)S(1)}, u32[]{:S(2)}, u32[]{:S(2)}) async-start(f32[128,1,128]{2,1,0:T(1,128)} %broadcast_in_dim.70), calls=%async_computation.5 | async-start | bytes 131072 | tf_op jit(solution)/shard_map/all_to_all | solution.py:202
  117.8 48.1 %copy-start.10 = (f32[16,2048]{1,0:T(8,128)S(1)}, f32[16,2048]{1,0:T(8,128)}, u32[]{:S(2)}) copy-start(f32[16,2048]{1,0:T(8,128)} %param.10) | copy-start | bytes 393220
  127.4 18.1 %all-to-all-start.6 = ((bf16[128,16,128]{2,1,0:T(8,128)(2,1)}), bf16[128,16,128]{2,1,0:T(8,128)(2,1)S(1)}, u32[]{:S(2)}, u32[]{:S(2)}) async-start(bf16[128,16,128]{2,1,0:T(8,128)(2,1)} %nystrom_terms.1), calls=%async_computation.6 | async-start | bytes 1048576 | tf_op jit(solution)/shard_map/all_to_all | solution.py:202
  146.2 14.3 %all-to-all-start.2 = ((f32[128,1,128]{2,1,0:T(1,128)}), f32[128,1,128]{2,1,0:T(1,128)S(1)}, u32[]{:S(2)}, u32[]{:S(2)}) async-start(f32[128,1,128]{2,1,0:T(1,128)} %broadcast_in_dim.67), calls=%async_computation.2 | async-start | bytes 131072 | tf_op jit(solution)/shard_map/all_to_all | solution.py:202
  161.4 19.0 %all-to-all-start.7 = ((bf16[128,16,128]{2,1,0:T(8,128)(2,1)}), bf16[128,16,128]{2,1,0:T(8,128)(2,1)S(1)}, u32[]{:S(2)}, u32[]{:S(2)}) async-start(bf16[128,16,128]{2,1,0:T(8,128)(2,1)} %broadcast_in_dim.73), calls=%async_computation.7 | async-start | bytes 1048576 | tf_op jit(solution)/shard_map/all_to_all | solution.py:202
  165.9 5.8 %copy-start.1 = (bf16[1024,8192]{1,0:T(8,128)(2,1)S(1)}, bf16[1024,8192]{1,0:T(8,128)(2,1)}, u32[]{:S(2)}) copy-start(bf16[1024,8192]{1,0:T(8,128)(2,1)} %copy-done) | copy-start | bytes 50331652
  171.6 5.8 %copy-start.3 = (bf16[1024,8192]{1,0:T(8,128)(2,1)S(1)}, bf16[1024,8192]{1,0:T(8,128)(2,1)}, u32[]{:S(2)}) copy-start(bf16[1024,8192]{1,0:T(8,128)(2,1)} %copy-done.2) | copy-start | bytes 50331652
  177.4 3.2 %copy-start.9 = (f32[128]{0:T(128)S(1)}, f32[128]{0:T(128)}, u32[]{:S(2)}) copy-start(f32[128]{0:T(128)} %param.15) | copy-start | bytes 1540

commit v2 on v0

v2 whole, which is shorter than its diff:
```python
import functools
import math

import jax
import jax.numpy as jnp
from jax import lax
from jax.experimental import pallas as pl
from jax.experimental.pallas import tpu as pltpu
from jax.sharding import Mesh
from jax.sharding import PartitionSpec as P

f32, bf16 = jnp.float32, jnp.bfloat16
MIB = 2**20
LOADER = ("zh", "core")
CENTERS = ("y", "zl", "x")
ALL = LOADER + CENTERS
CHIPS = ("zh",) + CENTERS
PACK = 24
D = 256
LANES = 128
RATE = -4.0 / math.sqrt(D) * math.log2(math.e)
VMEM = pl.BlockSpec(memory_space=pltpu.VMEM)
SMEM = pl.BlockSpec(memory_space=pltpu.SMEM)
ANY = pl.BlockSpec(memory_space=pl.ANY)
HBM = pl.BlockSpec(memory_space=pltpu.HBM)
NT = (((1,), (1,)), ((), ()))


def laplacian(dist_sq):
    safe = jnp.maximum(dist_sq, 1e-30)
    return jnp.exp2(safe * lax.rsqrt(safe) * RATE).astype(bf16)


def pick_kernel(place_ref, index_ref, pool_ref, keep_ref, give_ref, held_ref, sems):
    share = keep_ref.shape[0]
    group = held_ref.shape[1]
    total = index_ref.shape[0]
    mine, core, first = place_ref[0], place_ref[1], place_ref[2]
    rows = pool_ref.shape[0]

    def local(n):
        half = core if n < share else 1 - core
        return index_ref[half * (total // 2) + first + n % share] - mine * rows

    def copy(n):
        at = jnp.clip(local(n), 0, rows - 1) // group * group
        return pltpu.make_async_copy(pool_ref.at[pl.ds(pl.multiple_of(at, group), group), :], held_ref.at[n], sems.at[n])

    for n in range(2 * share):
        copy(n).start()
    line = lax.broadcasted_iota(jnp.int32, (group, D), 0)
    for ref, base in ((keep_ref, 0), (give_ref, share)):
        picked = []
        for n in range(base, base + share):
            copy(n).wait()
            here = local(n)
            owned = jnp.logical_and(here >= 0, here < rows)
            spot = jnp.where(owned, lax.rem(jnp.clip(here, 0, rows - 1), group), -1)
            block = held_ref[n].astype(f32)
            picked.append(jnp.sum(jnp.where(line == spot, block, 0.0), axis=0, keepdims=True))
        ref[...] = jnp.concatenate(picked, axis=0).astype(bf16)


def pick_rows(place, batch_index, pool, share):
    group = 16
    return pl.pallas_call(
        pick_kernel,
        in_specs=[SMEM, SMEM, ANY],
        out_specs=[VMEM, VMEM],
        out_shape=[jax.ShapeDtypeStruct((share, D), bf16)] * 2,
        scratch_shapes=[pltpu.VMEM((2 * share, group, D), bf16), pltpu.SemaphoreType.DMA((2 * share,))],
        compiler_params=pltpu.CompilerParams(vmem_limit_bytes=4 * MIB),
        name="pick_rows",
    )(place, batch_index, pool)


def values_kernel(core_ref, w_ref, batch_ref, cen_sq_ref, cen_ref, *refs, first):
    n_out = 2 if first else 3
    outs_ref, (rows_ref, sq_ref, acc_ref, held_ref, sems) = refs[-5 - n_out : -5], refs[-5:]
    kern_ref = outs_ref[0]
    batch, count = kern_ref.shape
    col, row = held_ref.shape[1], 256
    steps = count // col

    def fetch(i):
        return pltpu.make_async_copy(cen_ref.at[pl.ds(pl.multiple_of(i * col, col), col), :], held_ref.at[i], sems.at[i])

    for i in range(steps):
        fetch(i).start()
    rows = batch_ref[...]
    wide = rows.astype(f32)
    rows_ref[...] = rows * (-2)
    sq_ref[...] = jnp.broadcast_to(jnp.sum(wide * wide, axis=1, keepdims=True), (batch, LANES))
    acc_ref[...] = jnp.zeros_like(acc_ref)

    def step(i, carry):
        fetch(i).wait()
        cols = pl.ds(pl.multiple_of(i * col, col), col)
        cen = held_ref[i]
        w = w_ref[:, cols]
        cen_sq = cen_sq_ref[:, cols]
        for j in range(batch // row):
            at = slice(j * row, (j + 1) * row)
            cross = lax.dot_general(rows_ref[at, :], cen, NT, preferred_element_type=f32)
            row_sq = jnp.concatenate([sq_ref[at, :]] * (col // LANES), axis=1)
            kern = laplacian((cross + row_sq) + cen_sq)
            kern_ref[at, cols] = kern
            acc_ref[:, at] += lax.dot_general(w, kern, NT, preferred_element_type=f32)
        return carry

    lax.fori_loop(0, steps, step, 0)
    blocks = batch // LANES
    if first:
        for r in range(blocks):
            outs_ref[1][:, r, :] = acc_ref[:, r * LANES : (r + 1) * LANES]
        return
    before_ref, keep_ref, give_ref = refs[0], outs_ref[1], outs_ref[2]
    core = core_ref[0]
    outs = keep_ref.shape[0]
    for ref, half in ((keep_ref, core), (give_ref, 1 - core)):
        at = pl.ds(pl.multiple_of(half * outs, outs), outs)
        ref[:, pl.ds(pl.multiple_of(core * blocks, blocks), blocks), :] = before_ref[at, :, :]
        for r in range(blocks):
            ref[:, pl.ds((1 - core) * blocks + r, 1), :] = acc_ref[at, r * LANES : (r + 1) * LANES][:, None, :]


def kernel_values(core, w_half, centers, batch, cen_sq, after, before=None):
    half, count, outs = batch.shape[0], centers.shape[0], w_half.shape[0]
    col, blocks = 2048, half // LANES
    first = before is None
    terms = [(outs, blocks, LANES)] if first else [(outs // 2, 2 * blocks, LANES)] * 2
    extra = [] if first else [before]
    return pl.pallas_call(
        functools.partial(values_kernel, first=first),
        in_specs=[SMEM] + [VMEM] * 3 + [HBM] + [VMEM] * len(extra) + [ANY] * len(after),
        out_specs=[VMEM] * (1 + len(terms)),
        out_shape=[pltpu.VMEM((half, count), bf16)] + [jax.ShapeDtypeStruct(t, f32) for t in terms],
        scratch_shapes=[
            pltpu.VMEM((half, D), bf16),
            pltpu.VMEM((half, LANES), f32),
            pltpu.VMEM((outs, half), f32),
            pltpu.VMEM((count // col, col, D), bf16),
            pltpu.SemaphoreType.DMA((count // col,)),
        ],
        compiler_params=pltpu.CompilerParams(vmem_limit_bytes=12 * MIB),
        cost_estimate=pl.CostEstimate(
            flops=8 * half * count * D, bytes_accessed=2 * half * count, transcendentals=2 * half * count
        ),
        name="kernel_values",
    )(core, w_half, batch, cen_sq, centers, *extra, *after)


def nystrom_kernel(core_ref, cen_ref, sq_ref, hi_ref, lo_ref, own_ref, other_ref, keep_ref, give_ref, acc_ref):
    cen = cen_ref[...]
    core = core_ref[0]
    half = own_ref.shape[0]
    for ref, place in ((own_ref, core), (other_ref, 1 - core)):
        rows = ref[...]
        wide = rows.astype(f32)
        cross = lax.dot_general(rows * (-2), cen, NT, preferred_element_type=f32)
        kern = laplacian((cross + jnp.sum(wide * wide, axis=1, keepdims=True)) + sq_ref[...])
        part = lax.dot_general(hi_ref[...], kern, NT, preferred_element_type=f32)
        part += lax.dot_general(lo_ref[...], kern, NT, preferred_element_type=f32)
        for r in range(half // LANES):
            at = pl.ds(place * (half // LANES) + r, 1)
            acc_ref[:, at, :] = part[:, None, r * LANES : (r + 1) * LANES]
    vectors = keep_ref.shape[0]
    keep_ref[...] = acc_ref[pl.ds(core * vectors, vectors), :, :].astype(bf16)
    give_ref[...] = acc_ref[pl.ds((1 - core) * vectors, vectors), :, :].astype(bf16)


def nystrom_terms(core, nys, own, other):
    vectors, blocks = nys[2].shape[0], 2 * own.shape[0] // LANES
    return pl.pallas_call(
        nystrom_kernel,
        in_specs=[SMEM] + [VMEM] * 6,
        out_specs=[VMEM, VMEM],
        out_shape=[jax.ShapeDtypeStruct((vectors // 2, blocks, LANES), bf16)] * 2,
        scratch_shapes=[pltpu.VMEM((vectors, blocks, LANES), f32)],
        compiler_params=pltpu.CompilerParams(vmem_limit_bytes=12 * MIB),
        cost_estimate=pl.CostEstimate(flops=2 * 10**9, bytes_accessed=2**20, transcendentals=2**18),
        name="nystrom_terms",
    )(core, *nys, own, other)


def split3(x):
    hi = x.astype(bf16).astype(f32)
    mid = (x - hi).astype(bf16).astype(f32)
    return hi, mid, (x - hi) - mid


def pack_kernel(moment_ref, moment_in_ref, pred_ref, pred_in_ref, out_ref, acc_ref):
    vectors, blocks, _ = moment_ref.shape
    acc_ref[:, :blocks, :] = moment_ref[...].astype(f32) + moment_in_ref[...].astype(f32)
    acc_ref[:, blocks:, :] = jnp.zeros((vectors, PACK - blocks, LANES), f32)
    pred = pred_ref[...] + pred_in_ref[...]
    parts = split3(pred)
    for j in range(vectors):
        o, r = j // (blocks // 2), j % (blocks // 2) * 2
        for n, part in enumerate(parts):
            acc_ref[j, blocks + 2 * n : blocks + 2 * n + 2, :] = part[o, r : r + 2, :]
    out_ref[...] = acc_ref[...].astype(bf16)


def pack(moment, moment_in, pred, pred_in):
    shape = (moment.shape[0], PACK, LANES)
    return pl.pallas_call(
        pack_kernel,
        in_specs=[VMEM] * 4,
        out_specs=VMEM,
        out_shape=jax.ShapeDtypeStruct(shape, bf16),
        scratch_shapes=[pltpu.VMEM(shape, f32)],
        compiler_params=pltpu.CompilerParams(vmem_limit_bytes=8 * MIB),
        name="pack",
    )(moment, moment_in, pred, pred_in)


def sum_kernel(part_ref, out_ref, acc_ref):
    blocks = 16
    acc_ref[...] = jnp.sum(part_ref[...].astype(f32), axis=0)
    pred = (acc_ref[blocks : blocks + 2, :] + acc_ref[blocks + 2 : blocks + 4, :]) + acc_ref[blocks + 4 : blocks + 6, :]
    for n, part in enumerate(split3(pred)):
        acc_ref[blocks + 2 * n : blocks + 2 * n + 2, :] = part
    out_ref[...] = jnp.broadcast_to(acc_ref[...].astype(bf16)[None], out_ref.shape)


def sum_chips(parts):
    return pl.pallas_call(
        sum_kernel,
        in_specs=[VMEM],
        out_specs=VMEM,
        out_shape=jax.ShapeDtypeStruct(parts.shape, bf16),
        scratch_shapes=[pltpu.VMEM(parts.shape[1:], f32)],
        compiler_params=pltpu.CompilerParams(vmem_limit_bytes=8 * MIB),
        name="sum_chips",
    )(parts)


def finish_kernel(
    core_ref, idx_ref, mine_ref, got_ref, tgt_ref, damp_ref, eig_ref, w_ref, own_ref, other_ref, out_ref, out_pred_ref, resid_ref, sum_ref
):
    half, count = own_ref.shape
    core = core_ref[0]
    chips = mine_ref.shape[0]
    blocks = tgt_ref.shape[1] // LANES
    outs = tgt_ref.shape[0] // 2
    sum_ref[pl.ds(core * chips, chips), :, :] = mine_ref[...].astype(f32)
    sum_ref[pl.ds((1 - core) * chips, chips), :, :] = got_ref[...].astype(f32)
    coeff = 0.0
    for r in range(blocks):
        at = slice(r * LANES, (r + 1) * LANES)
        halves = []
        for h in range(2):
            chip = pl.ds(h * chips + r // 2, outs, stride=chips // outs)
            line = blocks + r % 2
            halves.append((sum_ref[chip, line, :] + sum_ref[chip, line + 2, :]) + sum_ref[chip, line + 4, :])
        pred = jnp.concatenate(halves, axis=0)
        out_pred_ref[:, at] = pred
        resid = (pred - tgt_ref[:, at]).astype(bf16)
        resid_ref[:, at] = resid
        coeff += lax.dot_general(resid, sum_ref[:, r, :].astype(bf16), NT, preferred_element_type=f32)
    delta = 2.0 * lax.dot_general(
        coeff * damp_ref[...], eig_ref[...], NT, precision=lax.Precision.HIGHEST, preferred_element_type=f32
    )
    own = resid_ref[:, pl.ds(pl.multiple_of(core * half, half), half)]
    other = resid_ref[:, pl.ds(pl.multiple_of((1 - core) * half, half), half)]
    lane = lax.broadcasted_iota(jnp.int32, (w_ref.shape[0], LANES), 1)
    col = 1024
    for i in range(count // col):
        at = slice(i * col, (i + 1) * col)
        grad = jnp.dot(own, own_ref[:, at], preferred_element_type=f32)
        grad += jnp.dot(other, other_ref[:, at], preferred_element_type=f32)
        shifts = []
        for k in range(i * (col // LANES), (i + 1) * (col // LANES)):
            shifts.append(jnp.where(lane == idx_ref[k] - k * LANES, delta[:, k : k + 1], 0.0))
        out_ref[:, at] = (w_ref[:, at] - 2.0 * grad) + jnp.concatenate(shifts, axis=1)


def finish(core, nys_index, mine, got, targets, damping, eigvecs, weights, own, other):
    own = pltpu.with_memory_space_constraint(own, pltpu.VMEM)
    other = pltpu.with_memory_space_constraint(other, pltpu.VMEM)
    return pl.pallas_call(
        finish_kernel,
        in_specs=[SMEM] * 2 + [VMEM] * 8,
        out_specs=[VMEM, VMEM],
        out_shape=[jax.ShapeDtypeStruct(weights.shape, f32), jax.ShapeDtypeStruct(targets.shape, f32)],
        scratch_shapes=[
            pltpu.VMEM(targets.shape, bf16),
            pltpu.VMEM((2 * mine.shape[0],) + mine.shape[1:], f32),
        ],
        compiler_params=pltpu.CompilerParams(vmem_limit_bytes=12 * MIB),
        name="finish",
    )(core, nys_index, mine, got, targets, damping[None, :], eigvecs, weights, own, other)


def swap(x, axis):
    return lax.ppermute(x, axis, [(0, 1), (1, 0)])


def exchange(x, axes):
    return lax.all_to_all(x, axes, split_axis=0, concat_axis=0, tiled=True)


def spread(x, axes):
    return exchange(jnp.broadcast_to(x[None], (lax.axis_size(axes),) + x.shape), axes)


def body(pool, batch_index, targets, centers, weights, nys_index, eigvecs, damping):
    total = targets.shape[1]
    core = lax.axis_index("core").astype(jnp.int32)
    groups = lax.axis_size(CENTERS)
    share = total // (2 * groups)
    place = jnp.stack([lax.axis_index(LOADER), core, lax.axis_index(CENTERS) * share]).astype(jnp.int32)
    keep, give = pick_rows(place, batch_index, pool, share)
    rows = keep + swap(give, "core")
    rows = rows + swap(rows, "zh")
    own = spread(rows, CENTERS).reshape(groups * share, D)
    other = swap(own, "core")

    wide = centers.astype(f32)
    cen_sq = jnp.sum(wide * wide, axis=1)[None, :]
    w_half = weights.astype(bf16)
    core = core[None]

    nys_cen = centers[nys_index]
    nys_wide = nys_cen.astype(f32)
    eig_t = eigvecs.T
    eig_hi = eig_t.astype(bf16)
    eig_lo = (eig_t - eig_hi.astype(f32)).astype(bf16)
    nys = (nys_cen, jnp.sum(nys_wide * nys_wide, axis=1)[None, :], eig_hi, eig_lo)

    kern_own, pred = kernel_values(core, w_half, centers, own, cen_sq, nys)
    moment, give = nystrom_terms(core, nys, own, other)
    kern_other, pred, pred_give = kernel_values(core, w_half, centers, other, cen_sq, (give,), pred)
    packed = pack(moment, swap(give, "core"), pred, swap(pred_give, "core"))
    mine = exchange(sum_chips(exchange(packed, CHIPS)), CHIPS)
    return tuple(
        finish(core, nys_index, mine, swap(mine, "core"), targets, damping, eigvecs, weights, kern_own, kern_other)
    )


def solution(mesh):
    fine = Mesh(mesh.devices.reshape(2, 2, 4, 2, 4), ALL)
    return jax.shard_map(
        body,
        mesh=fine,
        in_specs=(
            P(LOADER, None),
            P(),
            P(),
            P(ALL, None),
            P(None, ALL),
            P(ALL),
            P(ALL, None),
            P(),
        ),
        out_specs=(P(None, ALL), P()),
        check_vma=False,
    )
```

time: 499 us -> 112 us (0.22)
  waiting for transfers between devices: 289 us -> 4.07 us
  matrix products: 84.8 us -> 0 us
  blocking collectives: 79.1 us -> 33.2 us
  Pallas kernels: 0 us -> 37.2 us
  starting transfers between devices: 0.08 us -> 20.1 us
  between operations: 14.1 us -> 0.83 us
  other arithmetic: 15 us -> 5.3 us
  local copies, waits for them, and re-layouts: 15.7 us -> 10.2 us
    psum x1 -> x0, waiting for transfers between devices: 162 us -> none  [body(): predictions = lax.psum(partial_value, ('loader', 'centers'))]
    all_gather x1 -> x0, waiting for transfers between devices: 128 us -> none  [body(): batch = lax.all_gather(summed, 'centers', axis=0, tiled=True)]
    dot_general x8 -> x0, matrix products: 84.8 us -> none  [the longest x4 54 us: tile(): cross = jnp.dot(rows, centers.T, preferred_element_type=jnp.float32)]
    psum x2 -> x0, blocking collectives: 79.1 us -> none  [the longest x1 63.4 us: body(): coeff = lax.psum(local_coeff, ('loader', 'centers'))]
    pallas_call x0 -> x7, Pallas kernels: none -> 37.2 us  [the longest x2 24.7 us: kernel_values(): pl.pallas_call(functools.partial(values_kernel, first=first), in_specs=[S...]
    all_to_all x0 -> x2, blocking collectives: none -> 33.2 us  [exchange(): return lax.all_to_all(x, axes, split_axis=0, concat_axis=0, tiled=True)]
    ppermute x0 -> x6, starting transfers between devices: none -> 12.4 us  [swap(): return lax.ppermute(x, axis, [(0, 1), (1, 0)])]
    all_to_all x0 -> x1, starting transfers between devices: none -> 7.76 us  [exchange(): return lax.all_to_all(x, axes, split_axis=0, concat_axis=0, tiled=True)]
  transfers between devices with their start and end apart: 2 -> 7, of which waited for: 2 -> 4; matrix products, arithmetic and copies ran while one was open for 1% -> 9% of each run, Pallas kernels for 0% -> 22%
where the time goes in v2:
time: 112 us; the launch traced here: 111 us
  Pallas kernels  37.2 us (33%)
  blocking collectives  33.2 us (30%)
  starting transfers between devices  20.1 us (18%)
  local copies, waits for them, and re-layouts  10.2 us (9%)
  other arithmetic  5.3 us (5%)
  waiting for transfers between devices  4.07 us (4%)
    all_to_all x2, blocking collectives, exchange(): return lax.all_to_all(x, axes, split_axis=0, concat_axis=0, tiled=True)  33.2 us
    pallas_call x2, Pallas kernels, kernel_values(): pl.pallas_call(functools.partial(values_kernel, first=first), in_specs=[S...  24.7 us
    ppermute x6, starting transfers between devices, swap(): return lax.ppermute(x, axis, [(0, 1), (1, 0)])  12.4 us
    all_to_all x1, starting transfers between devices, exchange(): return lax.all_to_all(x, axes, split_axis=0, concat_axis=0, tiled=True)  7.76 us
    pallas_call x1, Pallas kernels, finish(): pl.pallas_call(finish_kernel, in_specs=[SMEM] * 2 + [VMEM] * 8, out_specs...  7.29 us
    unnamed x19, local copies, waits for them, and re-layouts  5.96 us
    pallas_call x1, Pallas kernels, pick_rows(): pl.pallas_call(pick_kernel, in_specs=[SMEM, SMEM, ANY], out_specs=[VMEM,...  3.55 us
    gather x1, local copies, waits for them, and re-layouts, body(): nys_cen = centers[nys_index]  3.38 us
  transfers between devices with their start and end apart: 7, of which 4 were waited for; matrix products, arithmetic and copies ran while one was open for 9% of the time, Pallas kernels for 22%

profile of v2, /device:TPU:1, one launch (start us, length us, event | category | flops | bytes accessed | tf_op | source)
XLA Modules:
  0.0 111.0 jit_solution(6354196987115670962)
XLA Ops:
  0.6 0.1 pad_add_fusion.place_ref
  0.7 2.2 %copy-done.2 = bf16[8192,256]{1,0:T(8,128)(2,1)S(1)} copy-done((bf16[8192,256]{1,0:T(8,128)(2,1)S(1)}, bf16[8192,256]{1,0:T(8,128)(2,1)}, u32[]{:S(2)}) %copy-start.2) | copy-done | bytes 4194328
  2.9 0.7 copy-done.6
  3.6 3.6 %pick_rows.1 = (bf16[32,256]{1,0:T(8,128)(2,1)S(1)}, bf16[32,256]{1,0:T(8,128)(2,1)S(1)}) custom-call(s32[3]{0:T(128)S(1)} %pad_add_fusion.place_ref, s32[2048]{0:T(1024)S(1)} %copy-done.6, bf16[8192,256]{1,0:T(8,128)(2,1)S(1)} %copy-done.2), custom_call_target="tpu_custom_call" | custom-call | tf_op jit(solution)/shard_map/pick_rows/pallas_call | solution.py:66
  7.2 1.5 %collective-permute-start = (bf16[32,256]{1,0:T(8,128)(2,1)S(1)}, bf16[32,256]{1,0:T(8,128)(2,1)S(1)}, u32[]{:S(2)}, u32[]{:S(2)}) collective-permute-start(bf16[32,256]{1,0:T(8,128)(2,1)S(1)} %get-tuple-element.12), channel_id=1, source_target_pairs={{0,32},{32,0},{1,33},{33,1},{2,34},{34,2},{3,35},{35,3},{4,36},{36... | collective-permute-start | bytes 49160 | tf_op jit(solution)/shard_map/ppermute | solution.py:297
  8.7 0.8 copy.10
  9.6 3.8 %collective-permute-start.1 = (bf16[32,256]{1,0:T(8,128)(2,1)S(1)}, bf16[32,256]{1,0:T(8,128)(2,1)S(1)}, u32[]{:S(2)}, u32[]{:S(2)}) collective-permute-start(bf16[32,256]{1,0:T(8,128)(2,1)S(1)} %add.26), channel_id=1, source_target_pairs={{0,64},{64,0},{1,65},{65,1},{2,66},{66,2},{3,67},{67,3},{4,68},{68... | collective-permute-start | bytes 49160 | tf_op jit(solution)/shard_map/ppermute | solution.py:297
  13.3 0.7 compare_select_fusion
  14.0 0.5 collective-permute-done.1
  14.5 0.9 broadcast_in_dim.24
  15.3 7.8 %all-to-all-start = ((bf16[32,32,256]{2,1,0:T(8,128)(2,1)}), bf16[32,32,256]{2,1,0:T(8,128)(2,1)S(1)}, u32[]{:S(2)}, u32[]{:S(2)}) async-start(bf16[32,32,256]{2,1,0:T(8,128)(2,1)} %broadcast_in_dim.24), calls=%async_computation | async-start | bytes 1048576 | tf_op jit(solution)/shard_map/all_to_all | solution.py:301
  23.1 1.1 convert_element_type.22.w_ref
  24.2 3.4 %gather_fusion = bf16[64,256]{1,0:T(8,128)(2,1)S(1)} fusion(bf16[8192,256]{1,0:T(8,128)(2,1)} %cen_ref.3, s32[1024]{0:T(1024)S(1)} %pad_clamp_fusion), kind=kCustom, calls=%fused_computation | custom fusion | bytes 65792 | tf_op jit(solution)/shard_map/gather | solution.py:325
  27.6 0.1 multiply_reduce_fusion.1
  27.7 3.4 %multiply_reduce_fusion = f32[8192]{0:T(1024)S(1)} fusion(bf16[8192,256]{1,0:T(8,128)(2,1)} %cen_ref.3), kind=kLoop, calls=%fused_computation.1 | loop fusion | flops 6283264 | bytes 4227072 | tf_op jit(solution)/shard_map/reduce_sum | solution.py:321
  31.0 1.3 %all-to-all-done = bf16[32,32,256]{2,1,0:T(8,128)(2,1)S(1)} async-done(((bf16[32,32,256]{2,1,0:T(8,128)(2,1)}), bf16[32,32,256]{2,1,0:T(8,128)(2,1)S(1)}, u32[]{:S(2)}, u32[]{:S(2)}) %all-to-all-start) | async-done | bytes 524320 | tf_op jit(solution)/shard_map/all_to_all | solution.py:301
  32.4 3.3 %collective-permute-start.2 = (bf16[1024,256]{1,0:T(8,128)(2,1)S(1)}, bf16[1024,256]{1,0:T(8,128)(2,1)S(1)}, u32[]{:S(2)}, u32[]{:S(2)}) collective-permute-start(bf16[1024,256]{1,0:T(8,128)(2,1)S(1)} %bitcast.13), channel_id=1, source_target_pairs={{0,32},{32,0},{1,33},{33,1},{2,34},{34,2},{3,35},{35,3},{4,36},{36... | collective-permute-start | bytes 1572872 | tf_op jit(solution)/shard_map/ppermute | solution.py:297
  35.6 2.2 %copy-done = bf16[8192,256]{1,0:T(8,128)(2,1)S(1)} copy-done((bf16[8192,256]{1,0:T(8,128)(2,1)S(1)}, bf16[8192,256]{1,0:T(8,128)(2,1)}, u32[]{:S(2)}) %copy-start) | copy-done | bytes 4194328
  37.8 12.4 %kernel_values.2 = (bf16[1024,8192]{1,0:T(8,128)(2,1)S(1)}, f32[16,8,128]{2,1,0:T(8,128)S(1)}) custom-call(s32[1]{0:T(128)} %bitcast.core_ref, bf16[16,8192]{1,0:T(8,128)(2,1)S(1)} %convert_element_type.22.w_ref, bf16[1024,256]{1,0:T(8,128)(2,1)S(1)} %bitcast.14, f32[1,8192]{1,0:T(1,128)S(1)} %bitcast.16, bf16[8192,256]{1,0:T(8,128)(2,1)S(1)} %copy-done, ...), custom_call_target="tpu_custom_call" | custom-call | flops 17179869184 | bytes 16777216 | tf_op jit(solution)/shard_map/kernel_values/pallas_call | solution.py:133
  50.2 1.4 %nystrom_terms.1 = (bf16[64,16,128]{2,1,0:T(8,128)(2,1)S(1)}, bf16[64,16,128]{2,1,0:T(8,128)(2,1)S(1)}) custom-call(s32[1]{0:T(128)} %bitcast.core_ref, bf16[64,256]{1,0:T(8,128)(2,1)S(1)} %gather_fusion, f32[1,64]{1,0:T(1,128)S(1)} %bitcast.20, bf16[128,64]{1,0:T(8,128)(2,1)S(1)} %get-tuple-element.21.hi_ref.refs_2_, ...), custom_call_target="tpu_custom_call" | custom-call | flops 2000000000 | bytes 1048576 | tf_op jit(solution)/shard_map/nystrom_terms/pallas_call | solution.py:174
  51.6 0.3 collective-permute-start.3
  51.9 0.0 copy-start.3
  52.0 12.4 %kernel_values.3 = (bf16[1024,8192]{1,0:T(8,128)(2,1)S(1)}, f32[8,16,128]{2,1,0:T(8,128)S(1)}, f32[8,16,128]{2,1,0:T(8,128)S(1)}) custom-call(s32[1]{0:T(128)} %bitcast.core_ref, bf16[16,8192]{1,0:T(8,128)(2,1)S(1)} %convert_element_type.22.w_ref, bf16[1024,256]{1,0:T(8,128)(2,1)S(1)} %collective-permute-done.2.other_ref.batch_ref, f32[1,8192]{1,0:T(1,128)S(1)} %bitcast.17, ...), custom_call_target="tpu_custom_call" | custom-call | flops 17179869184 | bytes 16777216 | tf_op jit(solution)/shard_map/kernel_values/pallas_call | solution.py:133
  64.3 0.5 collective-permute-start.4
  64.9 0.9 collective-permute-done.4.pred_in_ref
  65.8 0.2 pack.1
  66.0 19.1 %all_to_all.15.part_ref = bf16[64,24,128]{2,1,0:T(8,128)(2,1)S(1)} all-to-all(bf16[64,24,128]{2,1,0:T(8,128)(2,1)S(1)} %pack.1), channel_id=1, replica_groups=mesh['zh'=2,'core'=2,'y'=4,'zl'=2,'x'=4] {'zh','y','zl','x'}, dimensions={0} | all-to-all | bytes 786432 | tf_op jit(solution)/shard_map/all_to_all | solution.py:301
  85.0 0.1 sum_chips.1
  85.1 14.2 %all_to_all.16.mine_ref = bf16[64,24,128]{2,1,0:T(8,128)(2,1)S(1)} all-to-all(bf16[64,24,128]{2,1,0:T(8,128)(2,1)S(1)} %sum_chips.1), channel_id=1, replica_groups=mesh['zh'=2,'core'=2,'y'=4,'zl'=2,'x'=4] {'zh','y','zl','x'}, dimensions={0} | all-to-all | bytes 786432 | tf_op jit(solution)/shard_map/all_to_all | solution.py:301
  99.3 3.1 %collective-permute-start.5 = (bf16[64,24,128]{2,1,0:T(8,128)(2,1)S(1)}, bf16[64,24,128]{2,1,0:T(8,128)(2,1)S(1)}, u32[]{:S(2)}, u32[]{:S(2)}) collective-permute-start(bf16[64,24,128]{2,1,0:T(8,128)(2,1)S(1)} %all_to_all.16.mine_ref), channel_id=1, source_target_pairs={{0,32},{32,0},{1,33},{33,1},{2,34},{34,2},{3,35},{35,3},{4,36},{36... | collective-permute-start | bytes 1179656 | tf_op jit(solution)/shard_map/ppermute | solution.py:297
  102.4 1.3 %collective-permute-done.5.got_ref = bf16[64,24,128]{2,1,0:T(8,128)(2,1)S(1)} collective-permute-done((bf16[64,24,128]{2,1,0:T(8,128)(2,1)S(1)}, bf16[64,24,128]{2,1,0:T(8,128)(2,1)S(1)}, u32[]{:S(2)}, u32[]{:S(2)}) %collective-permute-start.5) | collective-permute-done | bytes 393248 | tf_op jit(solution)/shard_map/ppermute | solution.py:297
  103.7 7.3 %finish.1 = (f32[16,8192]{1,0:T(8,128)}, f32[16,2048]{1,0:T(8,128)}) custom-call(s32[1]{0:T(128)} %bitcast.core_ref, s32[64]{0:T(128)S(1)} %copy-done.7, bf16[64,24,128]{2,1,0:T(8,128)(2,1)S(1)} %all_to_all.16.mine_ref, bf16[64,24,128]{2,1,0:T(8,128)(2,1)S(1)} %collective-permute-done.5.got_ref, f32[16,2048]{1,0:T(8,128)S(1)} %copy-done.4, ...), custom_call_target="tpu_custom_call" | custom-call | tf_op jit(solution)/shard_map/finish/pallas_call | solution.py:282
  (21 shorter events, 0.1 us)
Async XLA Ops:
  0.7 2.2 %copy-start.2 = (bf16[8192,256]{1,0:T(8,128)(2,1)S(1)}, bf16[8192,256]{1,0:T(8,128)(2,1)}, u32[]{:S(2)}) copy-start(bf16[8192,256]{1,0:T(8,128)(2,1)} %pool_ref.1) | copy-start | bytes 12582916
  2.9 0.7 copy-start.6
  7.2 2.4 %collective-permute-start = (bf16[32,256]{1,0:T(8,128)(2,1)S(1)}, bf16[32,256]{1,0:T(8,128)(2,1)S(1)}, u32[]{:S(2)}, u32[]{:S(2)}) collective-permute-start(bf16[32,256]{1,0:T(8,128)(2,1)S(1)} %get-tuple-element.12), channel_id=1, source_target_pairs={{0,32},{32,0},{1,33},{33,1},{2,34},{34,2},{3,35},{35,3},{4,36},{36... | collective-permute-start | bytes 49160 | tf_op jit(solution)/shard_map/ppermute | solution.py:297
  9.6 4.9 %collective-permute-start.1 = (bf16[32,256]{1,0:T(8,128)(2,1)S(1)}, bf16[32,256]{1,0:T(8,128)(2,1)S(1)}, u32[]{:S(2)}, u32[]{:S(2)}) collective-permute-start(bf16[32,256]{1,0:T(8,128)(2,1)S(1)} %add.26), channel_id=1, source_target_pairs={{0,64},{64,0},{1,65},{65,1},{2,66},{66,2},{3,67},{67,3},{4,68},{68... | collective-permute-start | bytes 49160 | tf_op jit(solution)/shard_map/ppermute | solution.py:297
  15.3 17.1 %all-to-all-start = ((bf16[32,32,256]{2,1,0:T(8,128)(2,1)}), bf16[32,32,256]{2,1,0:T(8,128)(2,1)S(1)}, u32[]{:S(2)}, u32[]{:S(2)}) async-start(bf16[32,32,256]{2,1,0:T(8,128)(2,1)} %broadcast_in_dim.24), calls=%async_computation | async-start | bytes 1048576 | tf_op jit(solution)/shard_map/all_to_all | solution.py:301
  32.4 17.8 %collective-permute-start.2 = (bf16[1024,256]{1,0:T(8,128)(2,1)S(1)}, bf16[1024,256]{1,0:T(8,128)(2,1)S(1)}, u32[]{:S(2)}, u32[]{:S(2)}) collective-permute-start(bf16[1024,256]{1,0:T(8,128)(2,1)S(1)} %bitcast.13), channel_id=1, source_target_pairs={{0,32},{32,0},{1,33},{33,1},{2,34},{34,2},{3,35},{35,3},{4,36},{36... | collective-permute-start | bytes 1572872 | tf_op jit(solution)/shard_map/ppermute | solution.py:297
  35.6 2.2 %copy-start = (bf16[8192,256]{1,0:T(8,128)(2,1)S(1)}, bf16[8192,256]{1,0:T(8,128)(2,1)}, u32[]{:S(2)}) copy-start(bf16[8192,256]{1,0:T(8,128)(2,1)} %cen_ref.3) | copy-start | bytes 12582916
  37.8 14.1 %copy-start.1 = (bf16[8192,256]{1,0:T(8,128)(2,1)S(1)}, bf16[8192,256]{1,0:T(8,128)(2,1)}, u32[]{:S(2)}) copy-start(bf16[8192,256]{1,0:T(8,128)(2,1)} %cen_ref.3) | copy-start | bytes 12582916
  51.6 14.2 %collective-permute-start.3 = (bf16[64,16,128]{2,1,0:T(8,128)(2,1)S(1)}, bf16[64,16,128]{2,1,0:T(8,128)(2,1)S(1)}, u32[]{:S(2)}, u32[]{:S(2)}) collective-permute-start(bf16[64,16,128]{2,1,0:T(8,128)(2,1)S(1)} %get-tuple-element.14.refs_1_), channel_id=1, source_target_pairs={{0,32},{32,0},{1,33},{33,1},{2,34},{34,2},{3,35},{35,3},{4,36},{36... | collective-permute-start | bytes 786440 | tf_op jit(solution)/shard_map/ppermute | solution.py:297
  51.9 51.8 %copy-start.3 = (f32[16,8192]{1,0:T(8,128)S(1)}, f32[16,8192]{1,0:T(8,128)}, u32[]{:S(2)}) copy-start(f32[16,8192]{1,0:T(8,128)} %w_ref.1) | copy-start | bytes 1572868
  51.9 51.8 %copy-start.4 = (f32[16,2048]{1,0:T(8,128)S(1)}, f32[16,2048]{1,0:T(8,128)}, u32[]{:S(2)}) copy-start(f32[16,2048]{1,0:T(8,128)} %tgt_ref.1) | copy-start | bytes 393220
  51.9 51.8 %copy-start.5 = (f32[64,128]{1,0:T(8,128)S(1)}, f32[64,128]{1,0:T(8,128)}, u32[]{:S(2)}) copy-start(f32[64,128]{1,0:T(8,128)} %eig_ref.1) | copy-start | bytes 98308
  52.0 51.8 %copy-start.7 = (s32[64]{0:T(128)S(1)}, s32[64]{0:T(128)}, u32[]{:S(2)}) copy-start(s32[64]{0:T(128)} %idx_ref.1) | copy-start | bytes 772
  52.0 51.8 %copy-start.8 = (f32[128]{0:T(128)S(1)}, f32[128]{0:T(128)}, u32[]{:S(2)}) copy-start(f32[128]{0:T(128)} %param.15) | copy-start | bytes 1540
  64.3 1.4 %collective-permute-start.4 = (f32[8,16,128]{2,1,0:T(8,128)S(1)}, f32[8,16,128]{2,1,0:T(8,128)S(1)}, u32[]{:S(2)}, u32[]{:S(2)}) collective-permute-start(f32[8,16,128]{2,1,0:T(8,128)S(1)} %get-tuple-element.17), channel_id=1, source_target_pairs={{0,32},{32,0},{1,33},{33,1},{2,34},{34,2},{3,35},{35,3},{4,36},{36... | collective-permute-start | bytes 196616 | tf_op jit(solution)/shard_map/ppermute | solution.py:297
  99.3 4.4 %collective-permute-start.5 = (bf16[64,24,128]{2,1,0:T(8,128)(2,1)S(1)}, bf16[64,24,128]{2,1,0:T(8,128)(2,1)S(1)}, u32[]{:S(2)}, u32[]{:S(2)}) collective-permute-start(bf16[64,24,128]{2,1,0:T(8,128)(2,1)S(1)} %all_to_all.16.mine_ref), channel_id=1, source_target_pairs={{0,32},{32,0},{1,33},{33,1},{2,34},{34,2},{3,35},{35,3},{4,36},{36... | collective-permute-start | bytes 1179656 | tf_op jit(solution)/shard_map/ppermute | solution.py:297

commit v3 on v2

v3 whole, which is shorter than its diff:
```python
import functools
import math

import jax
import jax.numpy as jnp
from jax import lax
from jax.experimental import pallas as pl
from jax.experimental.pallas import tpu as pltpu
from jax.sharding import Mesh
from jax.sharding import PartitionSpec as P

f32, bf16 = jnp.float32, jnp.bfloat16
MIB = 2**20
LOADER = ("zh", "core")
CENTERS = ("y", "zl", "x")
ALL = LOADER + CENTERS
CHIPS = ("zh",) + CENTERS
PACK = 24
D = 256
LANES = 128
RATE = -4.0 / math.sqrt(D) * math.log2(math.e)
VMEM = pl.BlockSpec(memory_space=pltpu.VMEM)
SMEM = pl.BlockSpec(memory_space=pltpu.SMEM)
ANY = pl.BlockSpec(memory_space=pl.ANY)
HBM = pl.BlockSpec(memory_space=pltpu.HBM)
NT = (((1,), (1,)), ((), ()))


def in_hbm(x):
    return pltpu.with_memory_space_constraint(x, pltpu.HBM)


def in_vmem(x):
    return pltpu.with_memory_space_constraint(x, pltpu.VMEM)


def laplacian(dist_sq):
    safe = jnp.maximum(dist_sq, 1e-30)
    return jnp.exp2(safe * lax.rsqrt(safe) * RATE).astype(bf16)


def pick_kernel(place_ref, wanted_ref, pool_ref, keep_ref, give_ref, held_ref, index_ref, sems, index_sem):
    share = keep_ref.shape[0]
    group = held_ref.shape[1]
    total = index_ref.shape[0]
    mine, core, first = place_ref[0], place_ref[1], place_ref[2]
    rows = pool_ref.shape[0]
    listed = pltpu.make_async_copy(wanted_ref, index_ref, index_sem)
    listed.start()
    listed.wait()

    def local(n):
        half = core if n < share else 1 - core
        return index_ref[half * (total // 2) + first + n % share] - mine * rows

    def copy(n):
        at = jnp.clip(local(n), 0, rows - 1) // group * group
        return pltpu.make_async_copy(pool_ref.at[pl.ds(pl.multiple_of(at, group), group), :], held_ref.at[n], sems.at[n])

    for n in range(2 * share):
        copy(n).start()
    line = lax.broadcasted_iota(jnp.int32, (group, D), 0)
    for ref, base in ((keep_ref, 0), (give_ref, share)):
        picked = []
        for n in range(base, base + share):
            copy(n).wait()
            here = local(n)
            owned = jnp.logical_and(here >= 0, here < rows)
            spot = jnp.where(owned, lax.rem(jnp.clip(here, 0, rows - 1), group), -1)
            block = held_ref[n].astype(f32)
            picked.append(jnp.sum(jnp.where(line == spot, block, 0.0), axis=0, keepdims=True))
        ref[...] = jnp.concatenate(picked, axis=0).astype(bf16)


def pick_rows(place, batch_index, pool, share):
    group = 16
    return pl.pallas_call(
        pick_kernel,
        in_specs=[SMEM, HBM, HBM],
        out_specs=[VMEM, VMEM],
        out_shape=[jax.ShapeDtypeStruct((share, D), bf16)] * 2,
        scratch_shapes=[
            pltpu.VMEM((2 * share, group, D), bf16),
            pltpu.SMEM(batch_index.shape, jnp.int32),
            pltpu.SemaphoreType.DMA((2 * share,)),
            pltpu.SemaphoreType.DMA,
        ],
        compiler_params=pltpu.CompilerParams(vmem_limit_bytes=4 * MIB),
        name="pick_rows",
    )(place, in_hbm(batch_index), in_hbm(pool))


def repeat_kernel(keep_ref, got_ref, out_ref):
    out_ref[...] = jnp.broadcast_to((keep_ref[...] + got_ref[...])[None], out_ref.shape)


def repeat_sum(keep, got, times):
    return pl.pallas_call(
        repeat_kernel,
        in_specs=[VMEM, VMEM],
        out_specs=VMEM,
        out_shape=jax.ShapeDtypeStruct((times,) + keep.shape, bf16),
        compiler_params=pltpu.CompilerParams(vmem_limit_bytes=4 * MIB),
        name="repeat_sum",
    )(keep, got)


def values_kernel(w_ref, batch_ref, cen_sq_ref, cen_ref, *refs):
    kern_ref, pred_ref, rows_ref, sq_ref, acc_ref, held_ref, sems = refs[-7:]
    batch, count = kern_ref.shape
    col, row, sub = held_ref.shape[1], 512, 256
    steps = count // col

    def fetch(i):
        return pltpu.make_async_copy(cen_ref.at[pl.ds(pl.multiple_of(i * col, col), col), :], held_ref.at[i], sems.at[i])

    for i in range(steps):
        fetch(i).start()
    rows = batch_ref[0] + batch_ref[1]
    wide = rows.astype(f32)
    rows_ref[...] = rows * (-2)
    sq_ref[...] = jnp.broadcast_to(jnp.sum(wide * wide, axis=1, keepdims=True), (batch, LANES))
    acc_ref[...] = jnp.zeros_like(acc_ref)

    def step(i, carry):
        fetch(i).wait()
        for j in range(batch // row):
            at = slice(j * row, (j + 1) * row)
            row_sq = jnp.concatenate([sq_ref[at, :]] * (sub // LANES), axis=1)
            acc = acc_ref[:, at]
            for n in range(col // sub):
                cols = pl.ds(pl.multiple_of(i * col + n * sub, sub), sub)
                cen = held_ref[i, n * sub : (n + 1) * sub, :]
                cross = lax.dot_general(rows_ref[at, :], cen, NT, preferred_element_type=f32)
                kern = laplacian((cross + row_sq) + cen_sq_ref[:, cols])
                kern_ref[at, cols] = kern
                acc += lax.dot_general(w_ref[:, cols], kern, NT, preferred_element_type=f32)
            acc_ref[:, at] = acc
        return carry

    lax.fori_loop(0, steps, step, 0)
    for r in range(batch // LANES):
        pred_ref[:, r, :] = acc_ref[:, r * LANES : (r + 1) * LANES]


def kernel_values(w_half, centers, batch, cen_sq, after):
    half, count, outs = batch.shape[1], centers.shape[0], w_half.shape[0]
    col = 2048
    return pl.pallas_call(
        values_kernel,
        in_specs=[VMEM] * 3 + [HBM] + [ANY] * len(after),
        out_specs=[VMEM, VMEM],
        out_shape=[pltpu.VMEM((half, count), bf16), jax.ShapeDtypeStruct((outs, half // LANES, LANES), f32)],
        scratch_shapes=[
            pltpu.VMEM((half, D), bf16),
            pltpu.VMEM((half, LANES), f32),
            pltpu.VMEM((outs, half), f32),
            pltpu.VMEM((count // col, col, D), bf16),
            pltpu.SemaphoreType.DMA((count // col,)),
        ],
        compiler_params=pltpu.CompilerParams(vmem_limit_bytes=12 * MIB),
        cost_estimate=pl.CostEstimate(
            flops=8 * half * count * D, bytes_accessed=2 * half * count, transcendentals=2 * half * count
        ),
        name="kernel_values",
    )(w_half, batch, cen_sq, in_hbm(centers), *after)


def nystrom_kernel(core_ref, cen_ref, sq_ref, hi_ref, lo_ref, own_ref, other_ref, keep_ref, give_ref, acc_ref):
    cen = cen_ref[...]
    core = core_ref[0]
    half = own_ref.shape[1]
    for ref, place in ((own_ref, core), (other_ref, 1 - core)):
        rows = ref[0] + ref[1]
        wide = rows.astype(f32)
        cross = lax.dot_general(rows * (-2), cen, NT, preferred_element_type=f32)
        kern = laplacian((cross + jnp.sum(wide * wide, axis=1, keepdims=True)) + sq_ref[...])
        part = lax.dot_general(hi_ref[...], kern, NT, preferred_element_type=f32)
        part += lax.dot_general(lo_ref[...], kern, NT, preferred_element_type=f32)
        for r in range(half // LANES):
            at = pl.ds(place * (half // LANES) + r, 1)
            acc_ref[:, at, :] = part[:, None, r * LANES : (r + 1) * LANES]
    vectors = keep_ref.shape[0]
    keep_ref[...] = acc_ref[pl.ds(core * vectors, vectors), :, :].astype(bf16)
    give_ref[...] = acc_ref[pl.ds((1 - core) * vectors, vectors), :, :].astype(bf16)


def nystrom_terms(core, nys, own, other):
    vectors, blocks = nys[2].shape[0], 2 * own.shape[1] // LANES
    return pl.pallas_call(
        nystrom_kernel,
        in_specs=[SMEM] + [VMEM] * 6,
        out_specs=[VMEM, VMEM],
        out_shape=[jax.ShapeDtypeStruct((vectors // 2, blocks, LANES), bf16)] * 2,
        scratch_shapes=[pltpu.VMEM((vectors, blocks, LANES), f32)],
        compiler_params=pltpu.CompilerParams(vmem_limit_bytes=12 * MIB),
        cost_estimate=pl.CostEstimate(flops=2 * 10**9, bytes_accessed=2**20, transcendentals=2**18),
        name="nystrom_terms",
    )(core, *nys, own, other)


def split3(x):
    hi = x.astype(bf16).astype(f32)
    mid = (x - hi).astype(bf16).astype(f32)
    return hi, mid, (x - hi) - mid


def pack_kernel(moment_ref, moment_in_ref, pred_ref, pred_in_ref, out_ref, acc_ref):
    vectors, blocks, _ = moment_ref.shape
    acc_ref[:, :blocks, :] = moment_ref[...].astype(f32) + moment_in_ref[...].astype(f32)
    acc_ref[:, blocks:, :] = jnp.zeros((vectors, PACK - blocks, LANES), f32)
    pred = pred_ref[...] + pred_in_ref[...]
    parts = split3(pred)
    per = pred.shape[1] // 2
    for j in range(vectors):
        o, r = j // per, j % per * 2
        for n, part in enumerate(parts):
            acc_ref[j, blocks + 2 * n : blocks + 2 * n + 2, :] = part[o, r : r + 2, :]
    out_ref[...] = acc_ref[...].astype(bf16)


def pack(moment, moment_in, pred, pred_in):
    shape = (moment.shape[0], PACK, LANES)
    return pl.pallas_call(
        pack_kernel,
        in_specs=[VMEM] * 4,
        out_specs=VMEM,
        out_shape=jax.ShapeDtypeStruct(shape, bf16),
        scratch_shapes=[pltpu.VMEM(shape, f32)],
        compiler_params=pltpu.CompilerParams(vmem_limit_bytes=8 * MIB),
        name="pack",
    )(moment, moment_in, pred, pred_in)


def sum_kernel(part_ref, out_ref, acc_ref):
    blocks = 16
    acc_ref[...] = jnp.sum(part_ref[...].astype(f32), axis=0)
    pred = (acc_ref[blocks : blocks + 2, :] + acc_ref[blocks + 2 : blocks + 4, :]) + acc_ref[blocks + 4 : blocks + 6, :]
    for n, part in enumerate(split3(pred)):
        acc_ref[blocks + 2 * n : blocks + 2 * n + 2, :] = part
    out_ref[...] = jnp.broadcast_to(acc_ref[...].astype(bf16)[None], out_ref.shape)


def sum_chips(parts):
    return pl.pallas_call(
        sum_kernel,
        in_specs=[VMEM],
        out_specs=VMEM,
        out_shape=jax.ShapeDtypeStruct(parts.shape, bf16),
        scratch_shapes=[pltpu.VMEM(parts.shape[1:], f32)],
        compiler_params=pltpu.CompilerParams(vmem_limit_bytes=8 * MIB),
        name="sum_chips",
    )(parts)


def read_pred(sum_ref, r, outs, blocks):
    chip = pl.ds(r // 2, outs, stride=sum_ref.shape[0] // outs)
    line = blocks + r % 2
    return (sum_ref[chip, line, :] + sum_ref[chip, line + 2, :]) + sum_ref[chip, line + 4, :]


def grad_kernel(core_ref, mine_ref, tgt_ref, kern_ref, pred_ref, resid_ref, grad_ref, sum_ref):
    half, count = kern_ref.shape
    blocks = half // LANES
    sum_ref[...] = mine_ref[...].astype(f32)
    for r in range(blocks):
        at = slice(r * LANES, (r + 1) * LANES)
        pred = read_pred(sum_ref, r, tgt_ref.shape[0], 2 * blocks)
        pred_ref[:, at] = pred
        tgt = tgt_ref[:, pl.ds(pl.multiple_of(core_ref[0] * half + r * LANES, LANES), LANES)]
        resid_ref[:, at] = (pred - tgt).astype(bf16)
    resid = resid_ref[...]
    col = 1024
    for i in range(count // col):
        at = slice(i * col, (i + 1) * col)
        grad_ref[:, at] = jnp.dot(resid, kern_ref[:, at], preferred_element_type=f32)


def own_grad(core, mine, targets, kern):
    half, count = kern.shape
    outs = targets.shape[0]
    return pl.pallas_call(
        grad_kernel,
        in_specs=[SMEM] + [VMEM] * 3,
        out_specs=[VMEM] * 3,
        out_shape=[
            jax.ShapeDtypeStruct((outs, half), f32),
            jax.ShapeDtypeStruct((outs, half), bf16),
            jax.ShapeDtypeStruct((outs, count), f32),
        ],
        scratch_shapes=[pltpu.VMEM(mine.shape, f32)],
        compiler_params=pltpu.CompilerParams(vmem_limit_bytes=8 * MIB),
        cost_estimate=pl.CostEstimate(flops=512 * half * count, bytes_accessed=2 * half * count, transcendentals=0),
        name="own_grad",
    )(core, mine, targets, in_vmem(kern))


def finish_kernel(
    core_ref, idx_ref, mine_ref, got_ref, pred_ref, resid_ref, grad_ref, tgt_ref, damp_ref, eig_ref, w_ref, kern_ref,
    out_ref, out_pred_ref, sum_ref, moment_ref,
):
    half, count = kern_ref.shape
    core = core_ref[0]
    chips = mine_ref.shape[0]
    blocks = half // LANES
    outs = tgt_ref.shape[0]
    sum_ref[...] = got_ref[...].astype(f32)
    out_pred_ref[:, pl.ds(pl.multiple_of(core * half, half), half)] = pred_ref[...]
    resids = []
    for r in range(blocks):
        at = pl.ds(pl.multiple_of((1 - core) * half + r * LANES, LANES), LANES)
        pred = read_pred(sum_ref, r, outs, 2 * blocks)
        out_pred_ref[:, at] = pred
        resids.append((pred - tgt_ref[:, at]).astype(bf16))
    other = jnp.concatenate(resids, axis=1)
    own = resid_ref[...]
    moment_ref[pl.ds(core * chips, chips), :, :] = mine_ref[:, : 2 * blocks, :].astype(f32)
    moment_ref[pl.ds((1 - core) * chips, chips), :, :] = sum_ref[:, : 2 * blocks, :]
    coeff = 0.0
    for r in range(blocks):
        at = slice(r * LANES, (r + 1) * LANES)
        for resid, place in ((own, core), (other, 1 - core)):
            line = pl.ds(place * blocks + r, 1)
            moment = moment_ref[:, line, :].reshape(2 * chips, LANES).astype(bf16)
            coeff += lax.dot_general(resid[:, at], moment, NT, preferred_element_type=f32)
    delta = 2.0 * lax.dot_general(
        coeff * damp_ref[...], eig_ref[...], NT, precision=lax.Precision.HIGHEST, preferred_element_type=f32
    )
    lane = lax.broadcasted_iota(jnp.int32, (outs, LANES), 1)
    col = 1024
    for i in range(count // col):
        at = slice(i * col, (i + 1) * col)
        grad = grad_ref[:, at] + jnp.dot(other, kern_ref[:, at], preferred_element_type=f32)
        shifts = []
        for k in range(i * (col // LANES), (i + 1) * (col // LANES)):
            shifts.append(jnp.where(lane == idx_ref[k] - k * LANES, delta[:, k : k + 1], 0.0))
        out_ref[:, at] = (w_ref[:, at] - 2.0 * grad) + jnp.concatenate(shifts, axis=1)


def finish(core, nys_index, mine, got, pred, resid, grad, targets, damping, eigvecs, weights, kern):
    chips, _, lanes = mine.shape
    return pl.pallas_call(
        finish_kernel,
        in_specs=[SMEM] * 2 + [VMEM] * 10,
        out_specs=[VMEM, VMEM],
        out_shape=[jax.ShapeDtypeStruct(weights.shape, f32), jax.ShapeDtypeStruct(targets.shape, f32)],
        scratch_shapes=[
            pltpu.VMEM(mine.shape, f32),
            pltpu.VMEM((2 * chips, 2 * kern.shape[0] // LANES, lanes), f32),
        ],
        compiler_params=pltpu.CompilerParams(vmem_limit_bytes=12 * MIB),
        name="finish",
    )(core, nys_index, mine, got, pred, resid, grad, targets, damping[None, :], eigvecs, weights, in_vmem(kern))


def swap(x, axis):
    return lax.ppermute(x, axis, [(0, 1), (1, 0)])


def exchange(x, axes):
    return lax.all_to_all(x, axes, split_axis=0, concat_axis=0, tiled=True)


def body(pool, batch_index, targets, centers, weights, nys_index, eigvecs, damping):
    total = targets.shape[1]
    core = lax.axis_index("core").astype(jnp.int32)
    groups = lax.axis_size(CENTERS)
    share = total // (2 * groups)
    place = jnp.stack([lax.axis_index(LOADER), core, lax.axis_index(CENTERS) * share]).astype(jnp.int32)
    keep, give = pick_rows(place, batch_index, pool, share)
    rows = exchange(repeat_sum(keep, swap(give, "core"), lax.axis_size(CHIPS)), CHIPS)
    wide = centers.astype(f32)
    cen_sq = jnp.sum(wide * wide, axis=1)[None, :]
    w_half = weights.astype(bf16)
    core = core[None]

    nys_cen = centers[nys_index]
    nys_wide = nys_cen.astype(f32)
    eig_t = eigvecs.T
    eig_hi = eig_t.astype(bf16)
    eig_lo = (eig_t - eig_hi.astype(f32)).astype(bf16)
    nys = (nys_cen, jnp.sum(nys_wide * nys_wide, axis=1)[None, :], eig_hi, eig_lo)

    rows, cen_sq, w_half, nys = lax.optimization_barrier((rows, cen_sq, w_half, nys))
    own = rows.reshape(2, groups * share, D)
    other = swap(own, "core")

    kern_own, pred = kernel_values(w_half, centers, own, cen_sq, nys)
    moment, give = nystrom_terms(core, nys, own, other)
    kern_other, pred_give = kernel_values(w_half, centers, other, cen_sq, (give, pred))
    packed = pack(moment, swap(give, "core"), pred, swap(pred_give, "core"))
    mine = exchange(sum_chips(exchange(packed, CHIPS)), CHIPS)
    got = swap(mine, "core")
    pred, resid, grad = own_grad(core, mine, targets, kern_own)
    return tuple(
        finish(core, nys_index, mine, got, pred, resid, grad, targets, damping, eigvecs, weights, kern_other)
    )


def solution(mesh):
    fine = Mesh(mesh.devices.reshape(2, 2, 4, 2, 4), ALL)
    return jax.shard_map(
        body,
        mesh=fine,
        in_specs=(
            P(LOADER, None),
            P(),
            P(),
            P(ALL, None),
            P(None, ALL),
            P(ALL),
            P(ALL, None),
            P(),
        ),
        out_specs=(P(None, ALL), P()),
        check_vma=False,
    )
```

time: 112 us -> 108 us (0.964)
  waiting for transfers between devices: 4.07 us -> 11.9 us
  local copies, waits for them, and re-layouts: 10.2 us -> 4.25 us
  blocking collectives: 33.2 us -> 29.3 us
  starting transfers between devices: 20.1 us -> 17.9 us
    all_to_all x1, waiting for transfers between devices: 1.34 us -> 11 us  [exchange(): return lax.all_to_all(x, axes, split_axis=0, concat_axis=0, tiled=True)]
    ppermute x6 -> x5, starting transfers between devices: 12.4 us -> 6.83 us  [swap(): return lax.ppermute(x, axis, [(0, 1), (1, 0)])]
    unnamed x19 -> x11, local copies, waits for them, and re-layouts: 5.96 us -> 0.87 us
    all_to_all x2, blocking collectives: 33.2 us -> 29.3 us  [exchange(): return lax.all_to_all(x, axes, split_axis=0, concat_axis=0, tiled=True)]
    all_to_all x1, starting transfers between devices: 7.76 us -> 11.1 us  [exchange(): return lax.all_to_all(x, axes, split_axis=0, concat_axis=0, tiled=True)]
    ppermute x6 -> x5, waiting for transfers between devices: 2.73 us -> 0.91 us  [swap(): return lax.ppermute(x, axis, [(0, 1), (1, 0)])]
    pallas_call x4 -> x6, Pallas kernels: 35.6 us -> 36.1 us  [the longest x2 23 us: kernel_values(): pl.pallas_call(values_kernel, in_specs=[VMEM] * 3 + [HBM] + [ANY] * len(a...]
  transfers between devices with their start and end apart: 7 -> 6, of which waited for: 4 -> 2; matrix products, arithmetic and copies ran while one was open for 9% -> 9% of each run, Pallas kernels for 22% -> 24%
where the time goes in v3:
time: 108 us; the launch traced here: 107 us
  Pallas kernels  37.8 us (35%)
  blocking collectives  29.3 us (27%)
  starting transfers between devices  17.9 us (17%)
  waiting for transfers between devices  11.9 us (11%)
  other arithmetic  5.29 us (5%)
  local copies, waits for them, and re-layouts  4.25 us (4%)
    all_to_all x2, blocking collectives, exchange(): return lax.all_to_all(x, axes, split_axis=0, concat_axis=0, tiled=True)  29.3 us
    pallas_call x2, Pallas kernels, kernel_values(): pl.pallas_call(values_kernel, in_specs=[VMEM] * 3 + [HBM] + [ANY] * len(a...  23 us
    all_to_all x1, starting transfers between devices, exchange(): return lax.all_to_all(x, axes, split_axis=0, concat_axis=0, tiled=True)  11.1 us
    all_to_all x1, waiting for transfers between devices, exchange(): return lax.all_to_all(x, axes, split_axis=0, concat_axis=0, tiled=True)  11 us
    ppermute x5, starting transfers between devices, swap(): return lax.ppermute(x, axis, [(0, 1), (1, 0)])  6.83 us
    pallas_call x1, Pallas kernels, finish(): pl.pallas_call(finish_kernel, in_specs=[SMEM] * 2 + [VMEM] * 10, out_spec...  5.3 us
    pallas_call x1, Pallas kernels, pick_rows(): pl.pallas_call(pick_kernel, in_specs=[SMEM, HBM, HBM], out_specs=[VMEM, V...  4.37 us
    gather x1, local copies, waits for them, and re-layouts, body(): nys_cen = centers[nys_index]  3.38 us
  transfers between devices with their start and end apart: 6, of which 2 were waited for; matrix products, arithmetic and copies ran while one was open for 9% of the time, Pallas kernels for 24%

profile of v3, /device:TPU:1, one launch (start us, length us, event | category | flops | bytes accessed | tf_op | source)
XLA Modules:
  0.0 107.3 jit_solution(6115111754925668762)
XLA Ops:
  0.6 0.1 pad_add_fusion.place_ref
  0.7 4.4 %pick_rows.1 = (bf16[32,256]{1,0:T(8,128)(2,1)S(1)}, bf16[32,256]{1,0:T(8,128)(2,1)S(1)}) custom-call(s32[3]{0:T(128)S(1)} %pad_add_fusion.place_ref, s32[2048]{0:T(1024)} %wanted_ref.1, bf16[8192,256]{1,0:T(8,128)(2,1)} %pool_ref.1), custom_call_target="tpu_custom_call" | custom-call | tf_op jit(solution)/shard_map/pick_rows/pallas_call | solution.py:77
  5.1 1.5 %collective-permute-start = (bf16[32,256]{1,0:T(8,128)(2,1)S(1)}, bf16[32,256]{1,0:T(8,128)(2,1)S(1)}, u32[]{:S(2)}, u32[]{:S(2)}) collective-permute-start(bf16[32,256]{1,0:T(8,128)(2,1)S(1)} %get-tuple-element.21), channel_id=1, source_target_pairs={{0,32},{32,0},{1,33},{33,1},{2,34},{34,2},{3,35},{35,3},{4,36},{36... | collective-permute-start | bytes 49160 | tf_op jit(solution)/shard_map/ppermute | solution.py:357
  6.6 0.8 copy.10
  7.5 1.1 %convert_element_type.19.w_ref = bf16[16,8192]{1,0:T(8,128)(2,1)S(1)} convert(f32[16,8192]{1,0:T(8,128)} %w_ref.1) | non-fusion elementwise | flops 131072 | bytes 786432 | tf_op jit(solution)/shard_map/convert_element_type | solution.py:374
  8.6 0.0 collective-permute-done.got_ref
  8.6 1.1 %repeat_sum.1 = bf16[64,32,256]{2,1,0:T(8,128)(2,1)} custom-call(bf16[32,256]{1,0:T(8,128)(2,1)S(1)} %get-tuple-element.20.keep_ref, bf16[32,256]{1,0:T(8,128)(2,1)S(1)} %collective-permute-done.got_ref), custom_call_target="tpu_custom_call" | custom-call | tf_op jit(solution)/shard_map/repeat_sum/pallas_call | solution.py:98
  9.7 11.1 %all-to-all-start = ((bf16[64,32,256]{2,1,0:T(8,128)(2,1)}), bf16[64,32,256]{2,1,0:T(8,128)(2,1)S(1)}, u32[]{:S(2)}, u32[]{:S(2)}) async-start(bf16[64,32,256]{2,1,0:T(8,128)(2,1)} %repeat_sum.1), calls=%async_computation | async-start | bytes 2097152 | tf_op jit(solution)/shard_map/all_to_all | solution.py:361
  20.7 0.7 compare_select_fusion
  21.4 3.4 %gather_fusion = bf16[64,256]{1,0:T(8,128)(2,1)S(1)} fusion(bf16[8192,256]{1,0:T(8,128)(2,1)} %cen_ref.3, s32[1024]{0:T(1024)S(1)} %pad_clamp_fusion), kind=kCustom, calls=%fused_computation | custom fusion | bytes 65792 | tf_op jit(solution)/shard_map/gather | solution.py:377
  24.8 0.1 multiply_reduce_fusion.1
  24.9 3.3 %multiply_reduce_fusion = f32[8192]{0:T(1024)S(1)} fusion(bf16[8192,256]{1,0:T(8,128)(2,1)} %cen_ref.3), kind=kLoop, calls=%fused_computation.1 | loop fusion | flops 6283264 | bytes 4227072 | tf_op jit(solution)/shard_map/reduce_sum | solution.py:373
  28.3 11.0 %all-to-all-done = bf16[64,32,256]{2,1,0:T(8,128)(2,1)S(1)} async-done(((bf16[64,32,256]{2,1,0:T(8,128)(2,1)}), bf16[64,32,256]{2,1,0:T(8,128)(2,1)S(1)}, u32[]{:S(2)}, u32[]{:S(2)}) %all-to-all-start) | async-done | bytes 1048608 | tf_op jit(solution)/shard_map/all_to_all | solution.py:361
  39.3 1.4 %collective-permute-start.1 = (bf16[2,1024,256]{2,1,0:T(8,128)(2,1)S(1)}, bf16[2,1024,256]{2,1,0:T(8,128)(2,1)S(1)}, u32[]{:S(2)}, u32[]{:S(2)}) collective-permute-start(bf16[2,1024,256]{2,1,0:T(8,128)(2,1)S(1)} %bitcast.13), channel_id=1, source_target_pairs={{0,32},{32,0},{1,33},{33,1},{2,34},{34,2},{3,35},{35,3},{4,36},{36... | collective-permute-start | bytes 3145736 | tf_op jit(solution)/shard_map/ppermute | solution.py:357
  40.7 11.5 %kernel_values.2 = (bf16[1024,8192]{1,0:T(8,128)(2,1)S(1)}, f32[16,8,128]{2,1,0:T(8,128)S(1)}) custom-call(bf16[16,8192]{1,0:T(8,128)(2,1)S(1)} %convert_element_type.19.w_ref, bf16[2,1024,256]{2,1,0:T(8,128)(2,1)S(1)} %bitcast.14, f32[1,8192]{1,0:T(1,128)S(1)} %bitcast.16, bf16[8192,256]{1,0:T(8,128)(2,1)} %cen_ref.3, bf16[64,256]{1,0:T(8,128)(2,1)S(1)} %gather_fusion, ...), custom_call_target="tpu_custom_call" | custom-call | flops 17179869184 | bytes 16777216 | tf_op jit(solution)/shard_map/kernel_values/pallas_call | solution.py:149
  52.2 0.0 collective-permute-done.1.other_ref.batch_ref
  52.2 1.4 %nystrom_terms.1 = (bf16[64,16,128]{2,1,0:T(8,128)(2,1)S(1)}, bf16[64,16,128]{2,1,0:T(8,128)(2,1)S(1)}) custom-call(s32[1]{0:T(128)} %bitcast.core_ref, bf16[64,256]{1,0:T(8,128)(2,1)S(1)} %gather_fusion, f32[1,64]{1,0:T(1,128)S(1)} %bitcast.20, bf16[128,64]{1,0:T(8,128)(2,1)S(1)} %get-tuple-element.24.hi_ref.refs_2_, ...), custom_call_target="tpu_custom_call" | custom-call | flops 2000000000 | bytes 1048576 | tf_op jit(solution)/shard_map/nystrom_terms/pallas_call | solution.py:190
  53.7 0.3 collective-permute-start.2
  53.9 0.0 copy-start.1
  54.0 11.5 %kernel_values.3 = (bf16[1024,8192]{1,0:T(8,128)(2,1)S(1)}, f32[16,8,128]{2,1,0:T(8,128)S(1)}) custom-call(bf16[16,8192]{1,0:T(8,128)(2,1)S(1)} %convert_element_type.19.w_ref, bf16[2,1024,256]{2,1,0:T(8,128)(2,1)S(1)} %collective-permute-done.1.other_ref.batch_ref, f32[1,8192]{1,0:T(1,128)S(1)} %bitcast.17, bf16[8192,256]{1,0:T(8,128)(2,1)} %cen_ref.3, ...), custom_call_target="tpu_custom_call" | custom-call | flops 17179869184 | bytes 16777216 | tf_op jit(solution)/shard_map/kernel_values/pallas_call | solution.py:149
  65.5 0.6 collective-permute-start.3
  66.0 0.9 collective-permute-done.3.pred_in_ref
  66.9 0.0 collective-permute-done.2.moment_in_ref
  66.9 0.2 pack.1
  67.1 15.1 %all_to_all.15.part_ref = bf16[64,24,128]{2,1,0:T(8,128)(2,1)S(1)} all-to-all(bf16[64,24,128]{2,1,0:T(8,128)(2,1)S(1)} %pack.1), channel_id=1, replica_groups=mesh['zh'=2,'core'=2,'y'=4,'zl'=2,'x'=4] {'zh','y','zl','x'}, dimensions={0} | all-to-all | bytes 786432 | tf_op jit(solution)/shard_map/all_to_all | solution.py:361
  82.2 0.1 sum_chips.1
  82.3 14.2 %all_to_all.16.mine_ref = bf16[64,24,128]{2,1,0:T(8,128)(2,1)S(1)} all-to-all(bf16[64,24,128]{2,1,0:T(8,128)(2,1)S(1)} %sum_chips.1), channel_id=1, replica_groups=mesh['zh'=2,'core'=2,'y'=4,'zl'=2,'x'=4] {'zh','y','zl','x'}, dimensions={0} | all-to-all | bytes 786432 | tf_op jit(solution)/shard_map/all_to_all | solution.py:361
  96.5 3.1 %collective-permute-start.4 = (bf16[64,24,128]{2,1,0:T(8,128)(2,1)S(1)}, bf16[64,24,128]{2,1,0:T(8,128)(2,1)S(1)}, u32[]{:S(2)}, u32[]{:S(2)}) collective-permute-start(bf16[64,24,128]{2,1,0:T(8,128)(2,1)S(1)} %all_to_all.16.mine_ref), channel_id=1, source_target_pairs={{0,32},{32,0},{1,33},{33,1},{2,34},{34,2},{3,35},{35,3},{4,36},{36... | collective-permute-start | bytes 1179656 | tf_op jit(solution)/shard_map/ppermute | solution.py:357
  99.6 0.0 copy-start.4
  99.6 2.4 %own_grad.1 = (f32[16,1024]{1,0:T(8,128)S(1)}, bf16[16,1024]{1,0:T(8,128)(2,1)S(1)}, f32[16,8192]{1,0:T(8,128)S(1)}) custom-call(s32[1]{0:T(128)} %bitcast.core_ref, bf16[64,24,128]{2,1,0:T(8,128)(2,1)S(1)} %all_to_all.16.mine_ref, f32[16,2048]{1,0:T(8,128)S(1)} %copy-done.1, bf16[1024,8192]{1,0:T(8,128)(2,1)S(1)} %get-tuple-element.33.kern_ref), custom_call_target="tpu_custom_call" | custom-call | flops 4294967296 | bytes 16777216 | tf_op jit(solution)/shard_map/own_grad/pallas_call | solution.py:282
  102.0 0.0 copy-done
  102.0 5.3 %finish.1 = (f32[16,8192]{1,0:T(8,128)}, f32[16,2048]{1,0:T(8,128)}) custom-call(s32[1]{0:T(128)} %bitcast.core_ref, s32[64]{0:T(128)S(1)} %copy-done.3, bf16[64,24,128]{2,1,0:T(8,128)(2,1)S(1)} %all_to_all.16.mine_ref, bf16[64,24,128]{2,1,0:T(8,128)(2,1)S(1)} %collective-permute-done.4.got_ref, f32[16,1024]{1,0:T(8,128)S(1)} %get-tuple-element.34.pred_ref, ...), custom_call_target="tpu_custom_call" | custom-call | tf_op jit(solution)/shard_map/finish/pallas_call | solution.py:342
  (10 shorter events, 0.0 us)
Async XLA Ops:
  5.1 3.5 %collective-permute-start = (bf16[32,256]{1,0:T(8,128)(2,1)S(1)}, bf16[32,256]{1,0:T(8,128)(2,1)S(1)}, u32[]{:S(2)}, u32[]{:S(2)}) collective-permute-start(bf16[32,256]{1,0:T(8,128)(2,1)S(1)} %get-tuple-element.21), channel_id=1, source_target_pairs={{0,32},{32,0},{1,33},{33,1},{2,34},{34,2},{3,35},{35,3},{4,36},{36... | collective-permute-start | bytes 49160 | tf_op jit(solution)/shard_map/ppermute | solution.py:357
  9.7 29.6 %all-to-all-start = ((bf16[64,32,256]{2,1,0:T(8,128)(2,1)}), bf16[64,32,256]{2,1,0:T(8,128)(2,1)S(1)}, u32[]{:S(2)}, u32[]{:S(2)}) async-start(bf16[64,32,256]{2,1,0:T(8,128)(2,1)} %repeat_sum.1), calls=%async_computation | async-start | bytes 2097152 | tf_op jit(solution)/shard_map/all_to_all | solution.py:361
  39.3 12.9 %collective-permute-start.1 = (bf16[2,1024,256]{2,1,0:T(8,128)(2,1)S(1)}, bf16[2,1024,256]{2,1,0:T(8,128)(2,1)S(1)}, u32[]{:S(2)}, u32[]{:S(2)}) collective-permute-start(bf16[2,1024,256]{2,1,0:T(8,128)(2,1)S(1)} %bitcast.13), channel_id=1, source_target_pairs={{0,32},{32,0},{1,33},{33,1},{2,34},{34,2},{3,35},{35,3},{4,36},{36... | collective-permute-start | bytes 3145736 | tf_op jit(solution)/shard_map/ppermute | solution.py:357
  53.7 13.3 %collective-permute-start.2 = (bf16[64,16,128]{2,1,0:T(8,128)(2,1)S(1)}, bf16[64,16,128]{2,1,0:T(8,128)(2,1)S(1)}, u32[]{:S(2)}, u32[]{:S(2)}) collective-permute-start(bf16[64,16,128]{2,1,0:T(8,128)(2,1)S(1)} %get-tuple-element.28.refs_0_), channel_id=1, source_target_pairs={{0,32},{32,0},{1,33},{33,1},{2,34},{34,2},{3,35},{35,3},{4,36},{36... | collective-permute-start | bytes 786440 | tf_op jit(solution)/shard_map/ppermute | solution.py:357
  53.9 45.6 %copy-start.1 = (f32[16,2048]{1,0:T(8,128)S(1)}, f32[16,2048]{1,0:T(8,128)}, u32[]{:S(2)}) copy-start(f32[16,2048]{1,0:T(8,128)} %tgt_ref.3) | copy-start | bytes 393220
  65.5 1.5 %collective-permute-start.3 = (f32[16,8,128]{2,1,0:T(8,128)S(1)}, f32[16,8,128]{2,1,0:T(8,128)S(1)}, u32[]{:S(2)}, u32[]{:S(2)}) collective-permute-start(f32[16,8,128]{2,1,0:T(8,128)S(1)} %get-tuple-element.32), channel_id=1, source_target_pairs={{0,32},{32,0},{1,33},{33,1},{2,34},{34,2},{3,35},{35,3},{4,36},{36... | collective-permute-start | bytes 196616 | tf_op jit(solution)/shard_map/ppermute | solution.py:357
  96.5 5.4 %collective-permute-start.4 = (bf16[64,24,128]{2,1,0:T(8,128)(2,1)S(1)}, bf16[64,24,128]{2,1,0:T(8,128)(2,1)S(1)}, u32[]{:S(2)}, u32[]{:S(2)}) collective-permute-start(bf16[64,24,128]{2,1,0:T(8,128)(2,1)S(1)} %all_to_all.16.mine_ref), channel_id=1, source_target_pairs={{0,32},{32,0},{1,33},{33,1},{2,34},{34,2},{3,35},{35,3},{4,36},{36... | collective-permute-start | bytes 1179656 | tf_op jit(solution)/shard_map/ppermute | solution.py:357
  99.6 2.4 %copy-start = (f32[16,8192]{1,0:T(8,128)S(1)}, f32[16,8192]{1,0:T(8,128)}, u32[]{:S(2)}) copy-start(f32[16,8192]{1,0:T(8,128)} %w_ref.1) | copy-start | bytes 1572868
  99.6 2.4 %copy-start.2 = (f32[64,128]{1,0:T(8,128)S(1)}, f32[64,128]{1,0:T(8,128)}, u32[]{:S(2)}) copy-start(f32[64,128]{1,0:T(8,128)} %eig_ref.1) | copy-start | bytes 98308
  99.6 2.4 %copy-start.3 = (s32[64]{0:T(128)S(1)}, s32[64]{0:T(128)}, u32[]{:S(2)}) copy-start(s32[64]{0:T(128)} %idx_ref.1) | copy-start | bytes 772
  99.6 2.4 %copy-start.4 = (f32[128]{0:T(128)S(1)}, f32[128]{0:T(128)}, u32[]{:S(2)}) copy-start(f32[128]{0:T(128)} %param.15) | copy-start | bytes 1540

commit v4 on v3

--- a/solution.py
+++ b/solution.py
@@ -39,10 +39,10 @@
     return jnp.exp2(safe * lax.rsqrt(safe) * RATE).astype(bf16)
 
 
-def pick_kernel(place_ref, wanted_ref, pool_ref, keep_ref, give_ref, held_ref, index_ref, sems, index_sem):
+def pick_kernel(place_ref, wanted_ref, pool_ref, keep_ref, give_ref, held_ref, row_ref, index_ref, sems, index_sem):
     share = keep_ref.shape[0]
     group = held_ref.shape[1]
-    total = index_ref.shape[0]
+    half = index_ref.shape[0] // 2
     mine, core, first = place_ref[0], place_ref[1], place_ref[2]
     rows = pool_ref.shape[0]
     listed = pltpu.make_async_copy(wanted_ref, index_ref, index_sem)
@@ -50,26 +50,32 @@
     listed.wait()
 
     def local(n):
-        half = core if n < share else 1 - core
-        return index_ref[half * (total // 2) + first + n % share] - mine * rows
-
-    def copy(n):
-        at = jnp.clip(local(n), 0, rows - 1) // group * group
+        of = jnp.where(n < share, core, 1 - core)
+        return index_ref[of * half + first + jnp.where(n < share, n, n - share)] - mine * rows
+
+    def copy(n, at):
         return pltpu.make_async_copy(pool_ref.at[pl.ds(pl.multiple_of(at, group), group), :], held_ref.at[n], sems.at[n])
 
-    for n in range(2 * share):
-        copy(n).start()
+    def start(n, carry):
+        at = jnp.clip(local(n), 0, rows - 1)
+        copy(n, at - lax.rem(at, group)).start()
+        return carry
+
+    lax.fori_loop(0, 2 * share, start, 0, unroll=4)
     line = lax.broadcasted_iota(jnp.int32, (group, D), 0)
-    for ref, base in ((keep_ref, 0), (give_ref, share)):
-        picked = []
-        for n in range(base, base + share):
-            copy(n).wait()
-            here = local(n)
-            owned = jnp.logical_and(here >= 0, here < rows)
-            spot = jnp.where(owned, lax.rem(jnp.clip(here, 0, rows - 1), group), -1)
-            block = held_ref[n].astype(f32)
-            picked.append(jnp.sum(jnp.where(line == spot, block, 0.0), axis=0, keepdims=True))
-        ref[...] = jnp.concatenate(picked, axis=0).astype(bf16)
+
+    def select(n, carry):
+        copy(n, 0).wait()
+        here = local(n)
+        owned = jnp.logical_and(here >= 0, here < rows)
+        spot = jnp.where(owned, lax.rem(here, group), -1)
+        block = held_ref[n].astype(f32)
+        row_ref[pl.ds(n, 1), :] = jnp.sum(jnp.where(line == spot, block, 0.0), axis=0, keepdims=True)
+        return carry
+
+    lax.fori_loop(0, 2 * share, select, 0, unroll=4)
+    keep_ref[...] = row_ref[:share, :].astype(bf16)
+    give_ref[...] = row_ref[share:, :].astype(bf16)
 
 
 def pick_rows(place, batch_index, pool, share):
@@ -81,6 +87,7 @@
         out_shape=[jax.ShapeDtypeStruct((share, D), bf16)] * 2,
         scratch_shapes=[
             pltpu.VMEM((2 * share, group, D), bf16),
+            pltpu.VMEM((2 * share, D), f32),
             pltpu.SMEM(batch_index.shape, jnp.int32),
             pltpu.SemaphoreType.DMA((2 * share,)),
             pltpu.SemaphoreType.DMA,
@@ -114,15 +121,20 @@
     def fetch(i):
         return pltpu.make_async_copy(cen_ref.at[pl.ds(pl.multiple_of(i * col, col), col), :], held_ref.at[i], sems.at[i])
 
-    for i in range(steps):
+    ahead = 2
+    for i in range(ahead):
         fetch(i).start()
-    rows = batch_ref[0] + batch_ref[1]
+    rows = batch_ref[...]
     wide = rows.astype(f32)
     rows_ref[...] = rows * (-2)
     sq_ref[...] = jnp.broadcast_to(jnp.sum(wide * wide, axis=1, keepdims=True), (batch, LANES))
     acc_ref[...] = jnp.zeros_like(acc_ref)
 
     def step(i, carry):
+        @pl.when(i + ahead < steps)
+        def _():
+            fetch(i + ahead).start()
+
         fetch(i).wait()
         for j in range(batch // row):
             at = slice(j * row, (j + 1) * row)
@@ -144,8 +156,8 @@
 
 
 def kernel_values(w_half, centers, batch, cen_sq, after):
-    half, count, outs = batch.shape[1], centers.shape[0], w_half.shape[0]
-    col = 2048
+    half, count, outs = batch.shape[0], centers.shape[0], w_half.shape[0]
+    col = 1024
     return pl.pallas_call(
         values_kernel,
         in_specs=[VMEM] * 3 + [HBM] + [ANY] * len(after),
@@ -169,30 +181,31 @@
 def nystrom_kernel(core_ref, cen_ref, sq_ref, hi_ref, lo_ref, own_ref, other_ref, keep_ref, give_ref, acc_ref):
     cen = cen_ref[...]
     core = core_ref[0]
-    half = own_ref.shape[1]
-    for ref, place in ((own_ref, core), (other_ref, 1 - core)):
-        rows = ref[0] + ref[1]
+    half = own_ref.shape[0]
+    count, blocks = hi_ref.shape[0], keep_ref.shape[1]
+    for ref, first in ((own_ref, 0), (other_ref, half // LANES)):
+        rows = ref[...]
         wide = rows.astype(f32)
         cross = lax.dot_general(rows * (-2), cen, NT, preferred_element_type=f32)
         kern = laplacian((cross + jnp.sum(wide * wide, axis=1, keepdims=True)) + sq_ref[...])
         part = lax.dot_general(hi_ref[...], kern, NT, preferred_element_type=f32)
         part += lax.dot_general(lo_ref[...], kern, NT, preferred_element_type=f32)
         for r in range(half // LANES):
-            at = pl.ds(place * (half // LANES) + r, 1)
-            acc_ref[:, at, :] = part[:, None, r * LANES : (r + 1) * LANES]
-    vectors = keep_ref.shape[0]
-    keep_ref[...] = acc_ref[pl.ds(core * vectors, vectors), :, :].astype(bf16)
-    give_ref[...] = acc_ref[pl.ds((1 - core) * vectors, vectors), :, :].astype(bf16)
+            acc_ref[pl.ds(first + r, count, stride=blocks), :] = part[:, r * LANES : (r + 1) * LANES]
+    lines = count // 2 * blocks
+    for ref, place in ((keep_ref, core), (give_ref, 1 - core)):
+        part = acc_ref[pl.ds(pl.multiple_of(place * lines, lines), lines), :]
+        ref[...] = part.reshape(ref.shape).astype(bf16)
 
 
 def nystrom_terms(core, nys, own, other):
-    vectors, blocks = nys[2].shape[0], 2 * own.shape[1] // LANES
+    vectors, blocks = nys[2].shape[0], 2 * own.shape[0] // LANES
     return pl.pallas_call(
         nystrom_kernel,
         in_specs=[SMEM] + [VMEM] * 6,
         out_specs=[VMEM, VMEM],
         out_shape=[jax.ShapeDtypeStruct((vectors // 2, blocks, LANES), bf16)] * 2,
-        scratch_shapes=[pltpu.VMEM((vectors, blocks, LANES), f32)],
+        scratch_shapes=[pltpu.VMEM((vectors * blocks, LANES), f32)],
         compiler_params=pltpu.CompilerParams(vmem_limit_bytes=12 * MIB),
         cost_estimate=pl.CostEstimate(flops=2 * 10**9, bytes_accessed=2**20, transcendentals=2**18),
         name="nystrom_terms",
@@ -205,9 +218,14 @@
     return hi, mid, (x - hi) - mid
 
 
+def swap_halves(x, axis):
+    first, last = jnp.split(x, 2, axis)
+    return jnp.concatenate([last, first], axis)
+
+
 def pack_kernel(moment_ref, moment_in_ref, pred_ref, pred_in_ref, out_ref, acc_ref):
     vectors, blocks, _ = moment_ref.shape
-    acc_ref[:, :blocks, :] = moment_ref[...].astype(f32) + moment_in_ref[...].astype(f32)
+    acc_ref[:, :blocks, :] = swap_halves(moment_in_ref[...].astype(f32), 1) + moment_ref[...].astype(f32)
     acc_ref[:, blocks:, :] = jnp.zeros((vectors, PACK - blocks, LANES), f32)
     pred = pred_ref[...] + pred_in_ref[...]
     parts = split3(pred)
@@ -254,15 +272,19 @@
 
 
 def read_pred(sum_ref, r, outs, blocks):
-    chip = pl.ds(r // 2, outs, stride=sum_ref.shape[0] // outs)
-    line = blocks + r % 2
-    return (sum_ref[chip, line, :] + sum_ref[chip, line + 2, :]) + sum_ref[chip, line + 4, :]
+    chips = sum_ref.shape[0] // PACK
+
+    def part(n):
+        line = r // 2 * PACK + blocks + r % 2 + 2 * n
+        return sum_ref[pl.ds(line, outs, stride=chips // outs * PACK), :]
+
+    return (part(0) + part(1)) + part(2)
 
 
 def grad_kernel(core_ref, mine_ref, tgt_ref, kern_ref, pred_ref, resid_ref, grad_ref, sum_ref):
     half, count = kern_ref.shape
     blocks = half // LANES
-    sum_ref[...] = mine_ref[...].astype(f32)
+    sum_ref[...] = mine_ref[...].astype(f32).reshape(sum_ref.shape)
     for r in range(blocks):
         at = slice(r * LANES, (r + 1) * LANES)
         pred = read_pred(sum_ref, r, tgt_ref.shape[0], 2 * blocks)
@@ -288,7 +310,7 @@
             jax.ShapeDtypeStruct((outs, half), bf16),
             jax.ShapeDtypeStruct((outs, count), f32),
         ],
-        scratch_shapes=[pltpu.VMEM(mine.shape, f32)],
+        scratch_shapes=[pltpu.VMEM((mine.shape[0] * PACK, LANES), f32)],
         compiler_params=pltpu.CompilerParams(vmem_limit_bytes=8 * MIB),
         cost_estimate=pl.CostEstimate(flops=512 * half * count, bytes_accessed=2 * half * count, transcendentals=0),
         name="own_grad",
@@ -304,7 +326,8 @@
     chips = mine_ref.shape[0]
     blocks = half // LANES
     outs = tgt_ref.shape[0]
-    sum_ref[...] = got_ref[...].astype(f32)
+    got = got_ref[...].astype(f32)
+    sum_ref[...] = got.reshape(sum_ref.shape)
     out_pred_ref[:, pl.ds(pl.multiple_of(core * half, half), half)] = pred_ref[...]
     resids = []
     for r in range(blocks):
@@ -314,14 +337,14 @@
         resids.append((pred - tgt_ref[:, at]).astype(bf16))
     other = jnp.concatenate(resids, axis=1)
     own = resid_ref[...]
-    moment_ref[pl.ds(core * chips, chips), :, :] = mine_ref[:, : 2 * blocks, :].astype(f32)
-    moment_ref[pl.ds((1 - core) * chips, chips), :, :] = sum_ref[:, : 2 * blocks, :]
+    lines = chips * 2 * blocks
+    for place, part in ((core, mine_ref[...].astype(f32)[:, : 2 * blocks]), (1 - core, swap_halves(got[:, : 2 * blocks], 1))):
+        moment_ref[pl.ds(pl.multiple_of(place * lines, lines), lines), :] = part.reshape(lines, LANES)
     coeff = 0.0
-    for r in range(blocks):
-        at = slice(r * LANES, (r + 1) * LANES)
-        for resid, place in ((own, core), (other, 1 - core)):
-            line = pl.ds(place * blocks + r, 1)
-            moment = moment_ref[:, line, :].reshape(2 * chips, LANES).astype(bf16)
+    for n, resid in enumerate((own, other)):
+        for r in range(blocks):
+            moment = moment_ref[pl.ds(n * blocks + r, 2 * chips, stride=2 * blocks), :].astype(bf16)
+            at = slice(r * LANES, (r + 1) * LANES)
             coeff += lax.dot_general(resid[:, at], moment, NT, preferred_element_type=f32)
     delta = 2.0 * lax.dot_general(
         coeff * damp_ref[...], eig_ref[...], NT, precision=lax.Precision.HIGHEST, preferred_element_type=f32
@@ -345,8 +368,8 @@
         out_specs=[VMEM, VMEM],
         out_shape=[jax.ShapeDtypeStruct(weights.shape, f32), jax.ShapeDtypeStruct(targets.shape, f32)],
         scratch_shapes=[
-            pltpu.VMEM(mine.shape, f32),
-            pltpu.VMEM((2 * chips, 2 * kern.shape[0] // LANES, lanes), f32),
+            pltpu.VMEM((chips * PACK, lanes), f32),
+            pltpu.VMEM((2 * chips * 2 * kern.shape[0] // LANES, lanes), f32),
         ],
         compiler_params=pltpu.CompilerParams(vmem_limit_bytes=12 * MIB),
         name="finish",
@@ -368,7 +391,8 @@
     share = total // (2 * groups)
     place = jnp.stack([lax.axis_index(LOADER), core, lax.axis_index(CENTERS) * share]).astype(jnp.int32)
     keep, give = pick_rows(place, batch_index, pool, share)
-    rows = exchange(repeat_sum(keep, swap(give, "core"), lax.axis_size(CHIPS)), CHIPS)
+    rows = keep + swap(give, "core")
+    rows = exchange(repeat_sum(rows, swap(rows, "zh"), groups), CENTERS)
     wide = centers.astype(f32)
     cen_sq = jnp.sum(wide * wide, axis=1)[None, :]
     w_half = weights.astype(bf16)
@@ -382,7 +406,7 @@
     nys = (nys_cen, jnp.sum(nys_wide * nys_wide, axis=1)[None, :], eig_hi, eig_lo)
 
     rows, cen_sq, w_half, nys = lax.optimization_barrier((rows, cen_sq, w_half, nys))
-    own = rows.reshape(2, groups * share, D)
+    own = rows.reshape(groups * share, D)
     other = swap(own, "core")
 
     kern_own, pred = kernel_values(w_half, centers, own, cen_sq, nys)

time: 108 us -> 106 us (0.981)
  waiting for transfers between devices: 11.9 us -> 2.73 us
  blocking collectives: 29.3 us -> 33.1 us
  starting transfers between devices: 17.9 us -> 20.3 us
  Pallas kernels: 37.8 us -> 38.9 us
    all_to_all x1, waiting for transfers between devices: 11 us -> 1.34 us  [exchange(): return lax.all_to_all(x, axes, split_axis=0, concat_axis=0, tiled=True)]
    ppermute x5 -> x6, starting transfers between devices: 6.83 us -> 12.3 us  [swap(): return lax.ppermute(x, axis, [(0, 1), (1, 0)])]
    all_to_all x2, blocking collectives: 29.3 us -> 33.1 us  [exchange(): return lax.all_to_all(x, axes, split_axis=0, concat_axis=0, tiled=True)]
    all_to_all x1, starting transfers between devices: 11.1 us -> 8.02 us  [exchange(): return lax.all_to_all(x, axes, split_axis=0, concat_axis=0, tiled=True)]
    pallas_call x2, Pallas kernels: 23 us -> 25.2 us  [kernel_values(): pl.pallas_call(values_kernel, in_specs=[VMEM] * 3 + [HBM] + [ANY] * len(a...]
  transfers between devices with their start and end apart: 6 -> 7, of which waited for: 2 -> 3; matrix products, arithmetic and copies ran while one was open for 9% -> 9% of each run, Pallas kernels for 24% -> 26%
where the time goes in v4:
time: 106 us; the launch traced here: 105 us
  Pallas kernels  38.9 us (37%)
  blocking collectives  33.1 us (31%)
  starting transfers between devices  20.3 us (19%)
  other arithmetic  5.29 us (5%)
  local copies, waits for them, and re-layouts  4.26 us (4%)
  waiting for transfers between devices  2.73 us (3%)
    all_to_all x2, blocking collectives, exchange(): return lax.all_to_all(x, axes, split_axis=0, concat_axis=0, tiled=True)  33.1 us
    pallas_call x2, Pallas kernels, kernel_values(): pl.pallas_call(values_kernel, in_specs=[VMEM] * 3 + [HBM] + [ANY] * len(a...  25.2 us
    ppermute x6, starting transfers between devices, swap(): return lax.ppermute(x, axis, [(0, 1), (1, 0)])  12.3 us
    all_to_all x1, starting transfers between devices, exchange(): return lax.all_to_all(x, axes, split_axis=0, concat_axis=0, tiled=True)  8.02 us
    pallas_call x1, Pallas kernels, finish(): pl.pallas_call(finish_kernel, in_specs=[SMEM] * 2 + [VMEM] * 10, out_spec...  4.71 us
    pallas_call x1, Pallas kernels, pick_rows(): pl.pallas_call(pick_kernel, in_specs=[SMEM, HBM, HBM], out_specs=[VMEM, V...  4.24 us
    gather x1, local copies, waits for them, and re-layouts, body(): nys_cen = centers[nys_index]  3.38 us
    reduce_sum x1, other arithmetic, body(): cen_sq = jnp.sum(wide * wide, axis=1)[None, :]  3.35 us
  transfers between devices with their start and end apart: 7, of which 3 were waited for; matrix products, arithmetic and copies ran while one was open for 9% of the time, Pallas kernels for 26%

profile of v4, /device:TPU:1, one launch (start us, length us, event | category | flops | bytes accessed | tf_op | source)
XLA Modules:
  0.0 105.4 jit_solution(2919750461232282034)
XLA Ops:
  0.6 0.1 pad_add_fusion.place_ref
  0.7 4.2 %pick_rows.1 = (bf16[32,256]{1,0:T(8,128)(2,1)S(1)}, bf16[32,256]{1,0:T(8,128)(2,1)S(1)}) custom-call(s32[3]{0:T(128)S(1)} %pad_add_fusion.place_ref, s32[2048]{0:T(1024)} %wanted_ref.1, bf16[8192,256]{1,0:T(8,128)(2,1)} %pool_ref.1), custom_call_target="tpu_custom_call" | custom-call | tf_op jit(solution)/shard_map/pick_rows/pallas_call | solution.py:83
  5.0 1.6 %collective-permute-start = (bf16[32,256]{1,0:T(8,128)(2,1)S(1)}, bf16[32,256]{1,0:T(8,128)(2,1)S(1)}, u32[]{:S(2)}, u32[]{:S(2)}) collective-permute-start(bf16[32,256]{1,0:T(8,128)(2,1)S(1)} %get-tuple-element.21), channel_id=1, source_target_pairs={{0,32},{32,0},{1,33},{33,1},{2,34},{34,2},{3,35},{35,3},{4,36},{36... | collective-permute-start | bytes 49160 | tf_op jit(solution)/shard_map/ppermute | solution.py:380
  6.6 0.8 copy.10
  7.5 0.0 collective-permute-done
  7.5 3.7 %collective-permute-start.1 = (bf16[32,256]{1,0:T(8,128)(2,1)S(1)}, bf16[32,256]{1,0:T(8,128)(2,1)S(1)}, u32[]{:S(2)}, u32[]{:S(2)}) collective-permute-start(bf16[32,256]{1,0:T(8,128)(2,1)S(1)} %add.21.keep_ref), channel_id=1, source_target_pairs={{0,64},{64,0},{1,65},{65,1},{2,66},{66,2},{3,67},{67,3},{4,68},{68... | collective-permute-start | bytes 49160 | tf_op jit(solution)/shard_map/ppermute | solution.py:380
  11.2 0.7 compare_select_fusion
  11.9 0.5 collective-permute-done.1.got_ref
  12.3 0.9 repeat_sum.1
  13.2 8.0 %all-to-all-start = ((bf16[32,32,256]{2,1,0:T(8,128)(2,1)}), bf16[32,32,256]{2,1,0:T(8,128)(2,1)S(1)}, u32[]{:S(2)}, u32[]{:S(2)}) async-start(bf16[32,32,256]{2,1,0:T(8,128)(2,1)} %repeat_sum.1), calls=%async_computation | async-start | bytes 1048576 | tf_op jit(solution)/shard_map/all_to_all | solution.py:384
  21.2 1.1 %convert_element_type.19.w_ref = bf16[16,8192]{1,0:T(8,128)(2,1)S(1)} convert(f32[16,8192]{1,0:T(8,128)} %w_ref.1) | non-fusion elementwise | flops 131072 | bytes 786432 | tf_op jit(solution)/shard_map/convert_element_type | solution.py:398
  22.3 3.4 %gather_fusion = bf16[64,256]{1,0:T(8,128)(2,1)S(1)} fusion(bf16[8192,256]{1,0:T(8,128)(2,1)} %cen_ref.3, s32[1024]{0:T(1024)S(1)} %pad_clamp_fusion), kind=kCustom, calls=%fused_computation | custom fusion | bytes 65792 | tf_op jit(solution)/shard_map/gather | solution.py:401
  25.7 0.1 multiply_reduce_fusion.1
  25.8 3.4 %multiply_reduce_fusion = f32[8192]{0:T(1024)S(1)} fusion(bf16[8192,256]{1,0:T(8,128)(2,1)} %cen_ref.3), kind=kLoop, calls=%fused_computation.1 | loop fusion | flops 6283264 | bytes 4227072 | tf_op jit(solution)/shard_map/reduce_sum | solution.py:397
  29.1 1.3 %all-to-all-done = bf16[32,32,256]{2,1,0:T(8,128)(2,1)S(1)} async-done(((bf16[32,32,256]{2,1,0:T(8,128)(2,1)}), bf16[32,32,256]{2,1,0:T(8,128)(2,1)S(1)}, u32[]{:S(2)}, u32[]{:S(2)}) %all-to-all-start) | async-done | bytes 524320 | tf_op jit(solution)/shard_map/all_to_all | solution.py:384
  30.5 3.3 %collective-permute-start.2 = (bf16[1024,256]{1,0:T(8,128)(2,1)S(1)}, bf16[1024,256]{1,0:T(8,128)(2,1)S(1)}, u32[]{:S(2)}, u32[]{:S(2)}) collective-permute-start(bf16[1024,256]{1,0:T(8,128)(2,1)S(1)} %bitcast.13), channel_id=1, source_target_pairs={{0,32},{32,0},{1,33},{33,1},{2,34},{34,2},{3,35},{35,3},{4,36},{36... | collective-permute-start | bytes 1572872 | tf_op jit(solution)/shard_map/ppermute | solution.py:380
  33.8 12.6 %kernel_values.2 = (bf16[1024,8192]{1,0:T(8,128)(2,1)S(1)}, f32[16,8,128]{2,1,0:T(8,128)S(1)}) custom-call(bf16[16,8192]{1,0:T(8,128)(2,1)S(1)} %convert_element_type.19.w_ref, bf16[1024,256]{1,0:T(8,128)(2,1)S(1)} %bitcast.14, f32[1,8192]{1,0:T(1,128)S(1)} %bitcast.16, bf16[8192,256]{1,0:T(8,128)(2,1)} %cen_ref.3, bf16[64,256]{1,0:T(8,128)(2,1)S(1)} %gather_fusion, ...), custom_call_target="tpu_custom_call" | custom-call | flops 17179869184 | bytes 16777216 | tf_op jit(solution)/shard_map/kernel_values/pallas_call | solution.py:161
  46.4 1.2 %nystrom_terms.1 = (bf16[64,16,128]{2,1,0:T(8,128)(2,1)S(1)}, bf16[64,16,128]{2,1,0:T(8,128)(2,1)S(1)}) custom-call(s32[1]{0:T(128)} %bitcast.core_ref, bf16[64,256]{1,0:T(8,128)(2,1)S(1)} %gather_fusion, f32[1,64]{1,0:T(1,128)S(1)} %bitcast.20, bf16[128,64]{1,0:T(8,128)(2,1)S(1)} %get-tuple-element.24.hi_ref.refs_2_, ...), custom_call_target="tpu_custom_call" | custom-call | flops 2000000000 | bytes 1048576 | tf_op jit(solution)/shard_map/nystrom_terms/pallas_call | solution.py:203
  47.6 0.1 collective-permute-start.3
  47.7 0.0 copy-start.1
  47.7 12.6 %kernel_values.3 = (bf16[1024,8192]{1,0:T(8,128)(2,1)S(1)}, f32[16,8,128]{2,1,0:T(8,128)S(1)}) custom-call(bf16[16,8192]{1,0:T(8,128)(2,1)S(1)} %convert_element_type.19.w_ref, bf16[1024,256]{1,0:T(8,128)(2,1)S(1)} %collective-permute-done.2.other_ref.batch_ref, f32[1,8192]{1,0:T(1,128)S(1)} %bitcast.17, bf16[8192,256]{1,0:T(8,128)(2,1)} %cen_ref.3, ...), custom_call_target="tpu_custom_call" | custom-call | flops 17179869184 | bytes 16777216 | tf_op jit(solution)/shard_map/kernel_values/pallas_call | solution.py:161
  60.3 0.6 collective-permute-start.4
  60.9 0.9 collective-permute-done.4.pred_in_ref
  61.8 0.2 pack.1
  61.9 18.9 %all_to_all.15.part_ref = bf16[64,24,128]{2,1,0:T(8,128)(2,1)S(1)} all-to-all(bf16[64,24,128]{2,1,0:T(8,128)(2,1)S(1)} %pack.1), channel_id=1, replica_groups=mesh['zh'=2,'core'=2,'y'=4,'zl'=2,'x'=4] {'zh','y','zl','x'}, dimensions={0} | all-to-all | bytes 786432 | tf_op jit(solution)/shard_map/all_to_all | solution.py:384
  80.8 0.1 sum_chips.1
  81.0 14.2 %all_to_all.16.mine_ref = bf16[64,24,128]{2,1,0:T(8,128)(2,1)S(1)} all-to-all(bf16[64,24,128]{2,1,0:T(8,128)(2,1)S(1)} %sum_chips.1), channel_id=1, replica_groups=mesh['zh'=2,'core'=2,'y'=4,'zl'=2,'x'=4] {'zh','y','zl','x'}, dimensions={0} | all-to-all | bytes 786432 | tf_op jit(solution)/shard_map/all_to_all | solution.py:384
  95.1 3.1 %collective-permute-start.5 = (bf16[64,24,128]{2,1,0:T(8,128)(2,1)S(1)}, bf16[64,24,128]{2,1,0:T(8,128)(2,1)S(1)}, u32[]{:S(2)}, u32[]{:S(2)}) collective-permute-start(bf16[64,24,128]{2,1,0:T(8,128)(2,1)S(1)} %all_to_all.16.mine_ref), channel_id=1, source_target_pairs={{0,32},{32,0},{1,33},{33,1},{2,34},{34,2},{3,35},{35,3},{4,36},{36... | collective-permute-start | bytes 1179656 | tf_op jit(solution)/shard_map/ppermute | solution.py:380
  98.2 0.0 copy-start.4
  98.2 2.4 %own_grad.1 = (f32[16,1024]{1,0:T(8,128)S(1)}, bf16[16,1024]{1,0:T(8,128)(2,1)S(1)}, f32[16,8192]{1,0:T(8,128)S(1)}) custom-call(s32[1]{0:T(128)} %bitcast.core_ref, bf16[64,24,128]{2,1,0:T(8,128)(2,1)S(1)} %all_to_all.16.mine_ref, f32[16,2048]{1,0:T(8,128)S(1)} %copy-done.1, bf16[1024,8192]{1,0:T(8,128)(2,1)S(1)} %get-tuple-element.33.kern_ref), custom_call_target="tpu_custom_call" | custom-call | flops 4294967296 | bytes 16777216 | tf_op jit(solution)/shard_map/own_grad/pallas_call | solution.py:304
  100.6 0.0 copy-done.2
  100.6 4.7 %finish.1 = (f32[16,8192]{1,0:T(8,128)}, f32[16,2048]{1,0:T(8,128)}) custom-call(s32[1]{0:T(128)} %bitcast.core_ref, s32[64]{0:T(128)S(1)} %copy-done.3, bf16[64,24,128]{2,1,0:T(8,128)(2,1)S(1)} %all_to_all.16.mine_ref, bf16[64,24,128]{2,1,0:T(8,128)(2,1)S(1)} %collective-permute-done.5.got_ref, f32[16,1024]{1,0:T(8,128)S(1)} %get-tuple-element.34.pred_ref, ...), custom_call_target="tpu_custom_call" | custom-call | tf_op jit(solution)/shard_map/finish/pallas_call | solution.py:365
  (13 shorter events, 0.0 us)
Async XLA Ops:
  5.0 2.5 %collective-permute-start = (bf16[32,256]{1,0:T(8,128)(2,1)S(1)}, bf16[32,256]{1,0:T(8,128)(2,1)S(1)}, u32[]{:S(2)}, u32[]{:S(2)}) collective-permute-start(bf16[32,256]{1,0:T(8,128)(2,1)S(1)} %get-tuple-element.21), channel_id=1, source_target_pairs={{0,32},{32,0},{1,33},{33,1},{2,34},{34,2},{3,35},{35,3},{4,36},{36... | collective-permute-start | bytes 49160 | tf_op jit(solution)/shard_map/ppermute | solution.py:380
  7.5 4.8 %collective-permute-start.1 = (bf16[32,256]{1,0:T(8,128)(2,1)S(1)}, bf16[32,256]{1,0:T(8,128)(2,1)S(1)}, u32[]{:S(2)}, u32[]{:S(2)}) collective-permute-start(bf16[32,256]{1,0:T(8,128)(2,1)S(1)} %add.21.keep_ref), channel_id=1, source_target_pairs={{0,64},{64,0},{1,65},{65,1},{2,66},{66,2},{3,67},{67,3},{4,68},{68... | collective-permute-start | bytes 49160 | tf_op jit(solution)/shard_map/ppermute | solution.py:380
  13.2 17.3 %all-to-all-start = ((bf16[32,32,256]{2,1,0:T(8,128)(2,1)}), bf16[32,32,256]{2,1,0:T(8,128)(2,1)S(1)}, u32[]{:S(2)}, u32[]{:S(2)}) async-start(bf16[32,32,256]{2,1,0:T(8,128)(2,1)} %repeat_sum.1), calls=%async_computation | async-start | bytes 1048576 | tf_op jit(solution)/shard_map/all_to_all | solution.py:384
  30.5 15.9 %collective-permute-start.2 = (bf16[1024,256]{1,0:T(8,128)(2,1)S(1)}, bf16[1024,256]{1,0:T(8,128)(2,1)S(1)}, u32[]{:S(2)}, u32[]{:S(2)}) collective-permute-start(bf16[1024,256]{1,0:T(8,128)(2,1)S(1)} %bitcast.13), channel_id=1, source_target_pairs={{0,32},{32,0},{1,33},{33,1},{2,34},{34,2},{3,35},{35,3},{4,36},{36... | collective-permute-start | bytes 1572872 | tf_op jit(solution)/shard_map/ppermute | solution.py:380
  47.6 14.2 %collective-permute-start.3 = (bf16[64,16,128]{2,1,0:T(8,128)(2,1)S(1)}, bf16[64,16,128]{2,1,0:T(8,128)(2,1)S(1)}, u32[]{:S(2)}, u32[]{:S(2)}) collective-permute-start(bf16[64,16,128]{2,1,0:T(8,128)(2,1)S(1)} %get-tuple-element.28.refs_0_), channel_id=1, source_target_pairs={{0,32},{32,0},{1,33},{33,1},{2,34},{34,2},{3,35},{35,3},{4,36},{36... | collective-permute-start | bytes 786440 | tf_op jit(solution)/shard_map/ppermute | solution.py:380
  47.7 50.5 %copy-start.1 = (f32[16,2048]{1,0:T(8,128)S(1)}, f32[16,2048]{1,0:T(8,128)}, u32[]{:S(2)}) copy-start(f32[16,2048]{1,0:T(8,128)} %tgt_ref.3) | copy-start | bytes 393220
  60.3 1.5 %collective-permute-start.4 = (f32[16,8,128]{2,1,0:T(8,128)S(1)}, f32[16,8,128]{2,1,0:T(8,128)S(1)}, u32[]{:S(2)}, u32[]{:S(2)}) collective-permute-start(f32[16,8,128]{2,1,0:T(8,128)S(1)} %get-tuple-element.32), channel_id=1, source_target_pairs={{0,32},{32,0},{1,33},{33,1},{2,34},{34,2},{3,35},{35,3},{4,36},{36... | collective-permute-start | bytes 196616 | tf_op jit(solution)/shard_map/ppermute | solution.py:380
  95.1 5.5 %collective-permute-start.5 = (bf16[64,24,128]{2,1,0:T(8,128)(2,1)S(1)}, bf16[64,24,128]{2,1,0:T(8,128)(2,1)S(1)}, u32[]{:S(2)}, u32[]{:S(2)}) collective-permute-start(bf16[64,24,128]{2,1,0:T(8,128)(2,1)S(1)} %all_to_all.16.mine_ref), channel_id=1, source_target_pairs={{0,32},{32,0},{1,33},{33,1},{2,34},{34,2},{3,35},{35,3},{4,36},{36... | collective-permute-start | bytes 1179656 | tf_op jit(solution)/shard_map/ppermute | solution.py:380
  98.2 2.4 %copy-start = (f32[16,8192]{1,0:T(8,128)S(1)}, f32[16,8192]{1,0:T(8,128)}, u32[]{:S(2)}) copy-start(f32[16,8192]{1,0:T(8,128)} %w_ref.1) | copy-start | bytes 1572868
  98.2 2.4 %copy-start.2 = (f32[64,128]{1,0:T(8,128)S(1)}, f32[64,128]{1,0:T(8,128)}, u32[]{:S(2)}) copy-start(f32[64,128]{1,0:T(8,128)} %eig_ref.1) | copy-start | bytes 98308
  98.2 2.4 %copy-start.3 = (s32[64]{0:T(128)S(1)}, s32[64]{0:T(128)}, u32[]{:S(2)}) copy-start(s32[64]{0:T(128)} %idx_ref.1) | copy-start | bytes 772
  98.2 2.4 %copy-start.4 = (f32[128]{0:T(128)S(1)}, f32[128]{0:T(128)}, u32[]{:S(2)}) copy-start(f32[128]{0:T(128)} %param.15) | copy-start | bytes 1540

commit v5 on v4

--- a/solution.py
+++ b/solution.py
@@ -56,21 +56,28 @@
     def copy(n, at):
         return pltpu.make_async_copy(pool_ref.at[pl.ds(pl.multiple_of(at, group), group), :], held_ref.at[n], sems.at[n])
 
+    def owned(n, act):
+        here = local(n)
+
+        @pl.when(jnp.logical_and(here >= 0, here < rows))
+        def _():
+            act(jnp.clip(here, 0, rows - 1))
+
     def start(n, carry):
-        at = jnp.clip(local(n), 0, rows - 1)
-        copy(n, at - lax.rem(at, group)).start()
+        owned(n, lambda here: copy(n, here - lax.rem(here, group)).start())
         return carry
 
     lax.fori_loop(0, 2 * share, start, 0, unroll=4)
+    row_ref[...] = jnp.zeros_like(row_ref)
     line = lax.broadcasted_iota(jnp.int32, (group, D), 0)
 
     def select(n, carry):
-        copy(n, 0).wait()
-        here = local(n)
-        owned = jnp.logical_and(here >= 0, here < rows)
-        spot = jnp.where(owned, lax.rem(here, group), -1)
-        block = held_ref[n].astype(f32)
-        row_ref[pl.ds(n, 1), :] = jnp.sum(jnp.where(line == spot, block, 0.0), axis=0, keepdims=True)
+        def take(here):
+            copy(n, here - lax.rem(here, group)).wait()
+            block = held_ref[n].astype(f32)
+            row_ref[pl.ds(n, 1), :] = jnp.sum(jnp.where(line == lax.rem(here, group), block, 0.0), axis=0, keepdims=True)
+
+        owned(n, take)
         return carry
 
     lax.fori_loop(0, 2 * share, select, 0, unroll=4)
@@ -112,6 +119,86 @@
     )(keep, got)
 
 
+def row_norms(rows):
+    wide = rows.astype(f32)
+    square = wide * wide
+    hi = square.astype(bf16)
+    lo = (square - hi.astype(f32)).astype(bf16)
+    ones = jnp.ones((8, rows.shape[1]), bf16)
+    norms = lax.dot_general(ones, hi, NT, preferred_element_type=f32)
+    norms += lax.dot_general(ones, lo, NT, preferred_element_type=f32)
+    return norms[:1]
+
+
+def prepare_kernel(
+    idx_ref, w_ref, eig_ref, cen_ref, w_half_ref, cen_sq_ref, nys_ref, nys_sq_ref, hi_ref, lo_ref, held_ref, picked_ref, sems
+):
+    steps, col, _ = held_ref.shape
+    per = 8
+
+    def fetch(i):
+        return pltpu.make_async_copy(cen_ref.at[pl.ds(pl.multiple_of(i * col, col), col), :], held_ref.at[i], sems.at[i])
+
+    fetch(0).start()
+    fetch(1).start()
+    eig_t = eig_ref[...].T
+    hi = eig_t.astype(bf16)
+    hi_ref[...] = hi
+    lo_ref[...] = (eig_t - hi.astype(f32)).astype(bf16)
+    w_half_ref[...] = w_ref[...].astype(bf16)
+    row = lax.broadcasted_iota(jnp.int32, (per, col), 0)
+    lane = lax.broadcasted_iota(jnp.int32, (per, col), 1)
+
+    def step(i, carry):
+        fetch(i).wait()
+
+        @pl.when(i + 2 < steps)
+        def _():
+            fetch(i + 2).start()
+
+        rows = held_ref[i]
+        cen_sq_ref[:, pl.ds(pl.multiple_of(i * col, col), col)] = row_norms(rows)
+        spot = jnp.full((per, col), -1, jnp.int32)
+        for g in range(per):
+            spot = jnp.where(row == g, idx_ref[i * per + g] - i * col, spot)
+        chosen = jnp.where(lane == spot, 1.0, 0.0).astype(bf16)
+        at = pl.ds(pl.multiple_of(i * per, per), per)
+        picked_ref[at, :] = jnp.dot(chosen, rows, preferred_element_type=f32)
+        return carry
+
+    lax.fori_loop(0, steps, step, 0)
+    nys = picked_ref[...].astype(bf16)
+    nys_ref[...] = nys
+    nys_sq_ref[...] = row_norms(nys)
+
+
+def prepare(nys_index, weights, eigvecs, centers):
+    count, points, vectors = centers.shape[0], nys_index.shape[0], eigvecs.shape[1]
+    col = count // points * 8
+    shapes = [
+        (weights.shape, bf16),
+        ((1, count), f32),
+        ((points, D), bf16),
+        ((1, points), f32),
+        ((vectors, points), bf16),
+        ((vectors, points), bf16),
+    ]
+    return pl.pallas_call(
+        prepare_kernel,
+        in_specs=[SMEM, VMEM, VMEM, HBM],
+        out_specs=[VMEM] * len(shapes),
+        out_shape=[jax.ShapeDtypeStruct(*shape) for shape in shapes],
+        scratch_shapes=[
+            pltpu.VMEM((count // col, col, D), bf16),
+            pltpu.VMEM((points, D), f32),
+            pltpu.SemaphoreType.DMA((count // col,)),
+        ],
+        compiler_params=pltpu.CompilerParams(vmem_limit_bytes=12 * MIB),
+        cost_estimate=pl.CostEstimate(flops=4 * 10**9, bytes_accessed=2 * centers.size, transcendentals=0),
+        name="prepare",
+    )(nys_index, weights, eigvecs, in_hbm(centers))
+
+
 def values_kernel(w_ref, batch_ref, cen_sq_ref, cen_ref, *refs):
     kern_ref, pred_ref, rows_ref, sq_ref, acc_ref, held_ref, sems = refs[-7:]
     batch, count = kern_ref.shape
@@ -121,9 +208,7 @@
     def fetch(i):
         return pltpu.make_async_copy(cen_ref.at[pl.ds(pl.multiple_of(i * col, col), col), :], held_ref.at[i], sems.at[i])
 
-    ahead = 2
-    for i in range(ahead):
-        fetch(i).start()
+    fetch(0).start()
     rows = batch_ref[...]
     wide = rows.astype(f32)
     rows_ref[...] = rows * (-2)
@@ -131,11 +216,12 @@
     acc_ref[...] = jnp.zeros_like(acc_ref)
 
     def step(i, carry):
-        @pl.when(i + ahead < steps)
+        fetch(i).wait()
+
+        @pl.when(i + 1 < steps)
         def _():
-            fetch(i + ahead).start()
-
-        fetch(i).wait()
+            fetch(i + 1).start()
+
         for j in range(batch // row):
             at = slice(j * row, (j + 1) * row)
             row_sq = jnp.concatenate([sq_ref[at, :]] * (sub // LANES), axis=1)
@@ -157,7 +243,7 @@
 
 def kernel_values(w_half, centers, batch, cen_sq, after):
     half, count, outs = batch.shape[0], centers.shape[0], w_half.shape[0]
-    col = 1024
+    col = 2048
     return pl.pallas_call(
         values_kernel,
         in_specs=[VMEM] * 3 + [HBM] + [ANY] * len(after),
@@ -393,17 +479,8 @@
     keep, give = pick_rows(place, batch_index, pool, share)
     rows = keep + swap(give, "core")
     rows = exchange(repeat_sum(rows, swap(rows, "zh"), groups), CENTERS)
-    wide = centers.astype(f32)
-    cen_sq = jnp.sum(wide * wide, axis=1)[None, :]
-    w_half = weights.astype(bf16)
+    w_half, cen_sq, *nys = prepare(nys_index, weights, eigvecs, centers)
     core = core[None]
-
-    nys_cen = centers[nys_index]
-    nys_wide = nys_cen.astype(f32)
-    eig_t = eigvecs.T
-    eig_hi = eig_t.astype(bf16)
-    eig_lo = (eig_t - eig_hi.astype(f32)).astype(bf16)
-    nys = (nys_cen, jnp.sum(nys_wide * nys_wide, axis=1)[None, :], eig_hi, eig_lo)
 
     rows, cen_sq, w_half, nys = lax.optimization_barrier((rows, cen_sq, w_half, nys))
     own = rows.reshape(groups * share, D)

time: 106 us -> 104 us (0.981)
  other arithmetic: 5.29 us -> 0.08 us
  Pallas kernels: 38.9 us -> 42 us
  local copies, waits for them, and re-layouts: 4.26 us -> 2.49 us
    pallas_call x0 -> x1, Pallas kernels: none -> 6 us  [prepare(): pl.pallas_call(prepare_kernel, in_specs=[SMEM, VMEM, VMEM, HBM], out_spec...]
    reduce_sum x2 -> x0, other arithmetic: 3.46 us -> none  [the longest x1 3.35 us: body(): cen_sq = jnp.sum(wide * wide, axis=1)[None, :]]
    gather x1 -> x0, local copies, waits for them, and re-layouts: 3.38 us -> none  [body(): nys_cen = centers[nys_index]]
    pallas_call x2, Pallas kernels: 25.2 us -> 23 us  [kernel_values(): pl.pallas_call(values_kernel, in_specs=[VMEM] * 3 + [HBM] + [ANY] * len(a...]
    unnamed x11 -> x16, local copies, waits for them, and re-layouts: 0.88 us -> 2.49 us
    ppermute x6, waiting for transfers between devices: 1.38 us -> 2.88 us  [swap(): return lax.ppermute(x, axis, [(0, 1), (1, 0)])]
    convert_element_type x2 -> x0, other arithmetic: 1.08 us -> none  [the longest x1 1.07 us: body(): w_half = weights.astype(bf16)]
  transfers between devices with their start and end apart: 7 -> 7, of which waited for: 3 -> 4; matrix products, arithmetic and copies ran while one was open for 9% -> 0% of each run, Pallas kernels for 26% -> 30%
where the time goes in v5:
time: 104 us; the launch traced here: 103 us
  Pallas kernels  42 us (40%)
  blocking collectives  33.9 us (33%)
  starting transfers between devices  20.1 us (19%)
  waiting for transfers between devices  3.7 us (4%)
  local copies, waits for them, and re-layouts  2.49 us (2%)
    all_to_all x2, blocking collectives, exchange(): return lax.all_to_all(x, axes, split_axis=0, concat_axis=0, tiled=True)  33.9 us
    pallas_call x2, Pallas kernels, kernel_values(): pl.pallas_call(values_kernel, in_specs=[VMEM] * 3 + [HBM] + [ANY] * len(a...  23 us
    ppermute x6, starting transfers between devices, swap(): return lax.ppermute(x, axis, [(0, 1), (1, 0)])  12.2 us
    all_to_all x1, starting transfers between devices, exchange(): return lax.all_to_all(x, axes, split_axis=0, concat_axis=0, tiled=True)  7.88 us
    pallas_call x1, Pallas kernels, prepare(): pl.pallas_call(prepare_kernel, in_specs=[SMEM, VMEM, VMEM, HBM], out_spec...  6 us
    pallas_call x1, Pallas kernels, finish(): pl.pallas_call(finish_kernel, in_specs=[SMEM] * 2 + [VMEM] * 10, out_spec...  4.75 us
    pallas_call x1, Pallas kernels, pick_rows(): pl.pallas_call(pick_kernel, in_specs=[SMEM, HBM, HBM], out_specs=[VMEM, V...  3.6 us
    ppermute x6, waiting for transfers between devices, swap(): return lax.ppermute(x, axis, [(0, 1), (1, 0)])  2.88 us
  transfers between devices with their start and end apart: 7, of which 4 were waited for; matrix products, arithmetic and copies ran while one was open for 0% of the time, Pallas kernels for 30%

profile of v5, /device:TPU:1, one launch (start us, length us, event | category | flops | bytes accessed | tf_op | source)
XLA Modules:
  0.0 103.0 jit_solution(14084626686700378855)
XLA Ops:
  0.6 0.1 pad_add_fusion.place_ref
  0.7 3.6 %pick_rows.1 = (bf16[32,256]{1,0:T(8,128)(2,1)S(1)}, bf16[32,256]{1,0:T(8,128)(2,1)S(1)}) custom-call(s32[3]{0:T(128)S(1)} %pad_add_fusion.place_ref, s32[2048]{0:T(1024)} %wanted_ref.1, bf16[8192,256]{1,0:T(8,128)(2,1)} %pool_ref.1), custom_call_target="tpu_custom_call" | custom-call | tf_op jit(solution)/shard_map/pick_rows/pallas_call | solution.py:90
  4.3 1.6 %collective-permute-start = (bf16[32,256]{1,0:T(8,128)(2,1)S(1)}, bf16[32,256]{1,0:T(8,128)(2,1)S(1)}, u32[]{:S(2)}, u32[]{:S(2)}) collective-permute-start(bf16[32,256]{1,0:T(8,128)(2,1)S(1)} %get-tuple-element.27), channel_id=1, source_target_pairs={{0,32},{32,0},{1,33},{33,1},{2,34},{34,2},{3,35},{35,3},{4,36},{36... | collective-permute-start | bytes 49160 | tf_op jit(solution)/shard_map/ppermute | solution.py:466
  5.9 0.8 collective-permute-done
  6.8 3.6 %collective-permute-start.1 = (bf16[32,256]{1,0:T(8,128)(2,1)S(1)}, bf16[32,256]{1,0:T(8,128)(2,1)S(1)}, u32[]{:S(2)}, u32[]{:S(2)}) collective-permute-start(bf16[32,256]{1,0:T(8,128)(2,1)S(1)} %add.15.keep_ref), channel_id=1, source_target_pairs={{0,64},{64,0},{1,65},{65,1},{2,66},{66,2},{3,67},{67,3},{4,68},{68... | collective-permute-start | bytes 49160 | tf_op jit(solution)/shard_map/ppermute | solution.py:466
  10.4 1.1 %collective-permute-done.1.got_ref = bf16[32,256]{1,0:T(8,128)(2,1)S(1)} collective-permute-done((bf16[32,256]{1,0:T(8,128)(2,1)S(1)}, bf16[32,256]{1,0:T(8,128)(2,1)S(1)}, u32[]{:S(2)}, u32[]{:S(2)}) %collective-permute-start.1) | collective-permute-done | bytes 16416 | tf_op jit(solution)/shard_map/ppermute | solution.py:466
  11.5 0.9 repeat_sum.1
  12.4 7.9 %all-to-all-start = ((bf16[32,32,256]{2,1,0:T(8,128)(2,1)}), bf16[32,32,256]{2,1,0:T(8,128)(2,1)S(1)}, u32[]{:S(2)}, u32[]{:S(2)}) async-start(bf16[32,32,256]{2,1,0:T(8,128)(2,1)} %repeat_sum.1), calls=%async_computation | async-start | bytes 1048576 | tf_op jit(solution)/shard_map/all_to_all | solution.py:470
  20.3 0.0 copy-start.1
  20.3 1.0 %copy-done.1 = f32[16,8192]{1,0:T(8,128)S(1)} copy-done((f32[16,8192]{1,0:T(8,128)S(1)}, f32[16,8192]{1,0:T(8,128)}, u32[]{:S(2)}) %copy-start.1) | copy-done | bytes 524312
  21.3 0.8 copy-done.3
  22.1 0.7 copy-done.5
  22.7 6.0 %prepare.1 = (bf16[16,8192]{1,0:T(8,128)(2,1)S(1)}, f32[1,8192]{1,0:T(1,128)S(1)}, bf16[64,256]{1,0:T(8,128)(2,1)S(1)}, f32[1,64]{1,0:T(1,128)S(1)}, bf16[128,64...) custom-call(s32[64]{0:T(128)S(1)} %copy-done.5, f32[16,8192]{1,0:T(8,128)S(1)} %copy-done.1, f32[64,128]{1,0:T(8,128)S(1)} %copy-done.3, ...), custom_call_target="tpu_custom_call" | custom-call | flops 4000000000 | bytes 4194304 | tf_op jit(solution)/shard_map/prepare/pallas_call | solution.py:186
  28.7 0.8 all-to-all-done
  29.5 3.3 %collective-permute-start.2 = (bf16[1024,256]{1,0:T(8,128)(2,1)S(1)}, bf16[1024,256]{1,0:T(8,128)(2,1)S(1)}, u32[]{:S(2)}, u32[]{:S(2)}) collective-permute-start(bf16[1024,256]{1,0:T(8,128)(2,1)S(1)} %bitcast.5), channel_id=1, source_target_pairs={{0,32},{32,0},{1,33},{33,1},{2,34},{34,2},{3,35},{35,3},{4,36},{36... | collective-permute-start | bytes 1572872 | tf_op jit(solution)/shard_map/ppermute | solution.py:466
  32.8 11.5 %kernel_values.2 = (bf16[1024,8192]{1,0:T(8,128)(2,1)S(1)}, f32[16,8,128]{2,1,0:T(8,128)S(1)}) custom-call(bf16[16,8192]{1,0:T(8,128)(2,1)S(1)} %get-tuple-element.41.w_ref, bf16[1024,256]{1,0:T(8,128)(2,1)S(1)} %bitcast.6, f32[1,8192]{1,0:T(1,128)S(1)} %get-tuple-element.42.cen_sq_ref, bf16[8192,256]{1,0:T(8,128)(2,1)} %cen_ref.5, ...), custom_call_target="tpu_custom_call" | custom-call | flops 17179869184 | bytes 16777216 | tf_op jit(solution)/shard_map/kernel_values/pallas_call | solution.py:247
  44.3 1.2 %nystrom_terms.1 = (bf16[64,16,128]{2,1,0:T(8,128)(2,1)S(1)}, bf16[64,16,128]{2,1,0:T(8,128)(2,1)S(1)}) custom-call(s32[1]{0:T(128)} %bitcast.core_ref, bf16[64,256]{1,0:T(8,128)(2,1)S(1)} %get-tuple-element.34.cen_ref.refs_0_, f32[1,64]{1,0:T(1,128)S(1)} %get-tuple-element.35.sq_ref.refs_1_, bf16[128,64]{1,0:T(8,128)(2,1)S(1)} %get-tuple-element.36.hi_ref.refs_2_, ...), custom_call_target="tpu_custom_call" | custom-call | flops 2000000000 | bytes 1048576 | tf_op jit(solution)/shard_map/nystrom_terms/pallas_call | solution.py:289
  45.5 0.1 collective-permute-start.3
  45.6 0.0 copy-start
  45.6 11.5 %kernel_values.3 = (bf16[1024,8192]{1,0:T(8,128)(2,1)S(1)}, f32[16,8,128]{2,1,0:T(8,128)S(1)}) custom-call(bf16[16,8192]{1,0:T(8,128)(2,1)S(1)} %get-tuple-element.41.w_ref, bf16[1024,256]{1,0:T(8,128)(2,1)S(1)} %collective-permute-done.2.other_ref.batch_ref, f32[1,8192]{1,0:T(1,128)S(1)} %get-tuple-element.42.cen_sq_ref, bf16[8192,256]{1,0:T(8,128)(2,1)} %cen_ref.5, ...), custom_call_target="tpu_custom_call" | custom-call | flops 17179869184 | bytes 16777216 | tf_op jit(solution)/shard_map/kernel_values/pallas_call | solution.py:247
  57.1 0.0 copy-start.4
  57.1 0.0 copy-start.6
  57.2 0.6 collective-permute-start.4
  57.7 0.9 collective-permute-done.4.pred_in_ref
  58.6 0.2 pack.1
  58.8 19.7 %all_to_all.15.part_ref = bf16[64,24,128]{2,1,0:T(8,128)(2,1)S(1)} all-to-all(bf16[64,24,128]{2,1,0:T(8,128)(2,1)S(1)} %pack.1), channel_id=1, replica_groups=mesh['zh'=2,'core'=2,'y'=4,'zl'=2,'x'=4] {'zh','y','zl','x'}, dimensions={0} | all-to-all | bytes 786432 | tf_op jit(solution)/shard_map/all_to_all | solution.py:470
  78.5 0.1 sum_chips.1
  78.6 14.2 %all_to_all.16.mine_ref = bf16[64,24,128]{2,1,0:T(8,128)(2,1)S(1)} all-to-all(bf16[64,24,128]{2,1,0:T(8,128)(2,1)S(1)} %sum_chips.1), channel_id=1, replica_groups=mesh['zh'=2,'core'=2,'y'=4,'zl'=2,'x'=4] {'zh','y','zl','x'}, dimensions={0} | all-to-all | bytes 786432 | tf_op jit(solution)/shard_map/all_to_all | solution.py:470
  92.8 3.1 %collective-permute-start.5 = (bf16[64,24,128]{2,1,0:T(8,128)(2,1)S(1)}, bf16[64,24,128]{2,1,0:T(8,128)(2,1)S(1)}, u32[]{:S(2)}, u32[]{:S(2)}) collective-permute-start(bf16[64,24,128]{2,1,0:T(8,128)(2,1)S(1)} %all_to_all.16.mine_ref), channel_id=1, source_target_pairs={{0,32},{32,0},{1,33},{33,1},{2,34},{34,2},{3,35},{35,3},{4,36},{36... | collective-permute-start | bytes 1179656 | tf_op jit(solution)/shard_map/ppermute | solution.py:466
  95.8 2.4 %own_grad.1 = (f32[16,1024]{1,0:T(8,128)S(1)}, bf16[16,1024]{1,0:T(8,128)(2,1)S(1)}, f32[16,8192]{1,0:T(8,128)S(1)}) custom-call(s32[1]{0:T(128)} %bitcast.core_ref, bf16[64,24,128]{2,1,0:T(8,128)(2,1)S(1)} %all_to_all.16.mine_ref, f32[16,2048]{1,0:T(8,128)S(1)} %copy-done, bf16[1024,8192]{1,0:T(8,128)(2,1)S(1)} %get-tuple-element.45.kern_ref), custom_call_target="tpu_custom_call" | custom-call | flops 4294967296 | bytes 16777216 | tf_op jit(solution)/shard_map/own_grad/pallas_call | solution.py:390
  98.2 0.0 copy-done.4
  98.2 4.7 %finish.1 = (f32[16,8192]{1,0:T(8,128)}, f32[16,2048]{1,0:T(8,128)}) custom-call(s32[1]{0:T(128)} %bitcast.core_ref, s32[64]{0:T(128)S(1)} %copy-done.6, bf16[64,24,128]{2,1,0:T(8,128)(2,1)S(1)} %all_to_all.16.mine_ref, bf16[64,24,128]{2,1,0:T(8,128)(2,1)S(1)} %collective-permute-done.5.got_ref, f32[16,1024]{1,0:T(8,128)S(1)} %get-tuple-element.46.pred_ref, ...), custom_call_target="tpu_custom_call" | custom-call | tf_op jit(solution)/shard_map/finish/pallas_call | solution.py:451
  (12 shorter events, 0.0 us)
Async XLA Ops:
  4.3 2.5 %collective-permute-start = (bf16[32,256]{1,0:T(8,128)(2,1)S(1)}, bf16[32,256]{1,0:T(8,128)(2,1)S(1)}, u32[]{:S(2)}, u32[]{:S(2)}) collective-permute-start(bf16[32,256]{1,0:T(8,128)(2,1)S(1)} %get-tuple-element.27), channel_id=1, source_target_pairs={{0,32},{32,0},{1,33},{33,1},{2,34},{34,2},{3,35},{35,3},{4,36},{36... | collective-permute-start | bytes 49160 | tf_op jit(solution)/shard_map/ppermute | solution.py:466
  6.8 4.7 %collective-permute-start.1 = (bf16[32,256]{1,0:T(8,128)(2,1)S(1)}, bf16[32,256]{1,0:T(8,128)(2,1)S(1)}, u32[]{:S(2)}, u32[]{:S(2)}) collective-permute-start(bf16[32,256]{1,0:T(8,128)(2,1)S(1)} %add.15.keep_ref), channel_id=1, source_target_pairs={{0,64},{64,0},{1,65},{65,1},{2,66},{66,2},{3,67},{67,3},{4,68},{68... | collective-permute-start | bytes 49160 | tf_op jit(solution)/shard_map/ppermute | solution.py:466
  12.4 17.2 %all-to-all-start = ((bf16[32,32,256]{2,1,0:T(8,128)(2,1)}), bf16[32,32,256]{2,1,0:T(8,128)(2,1)S(1)}, u32[]{:S(2)}, u32[]{:S(2)}) async-start(bf16[32,32,256]{2,1,0:T(8,128)(2,1)} %repeat_sum.1), calls=%async_computation | async-start | bytes 1048576 | tf_op jit(solution)/shard_map/all_to_all | solution.py:470
  20.3 1.0 %copy-start.1 = (f32[16,8192]{1,0:T(8,128)S(1)}, f32[16,8192]{1,0:T(8,128)}, u32[]{:S(2)}) copy-start(f32[16,8192]{1,0:T(8,128)} %w_ref.3) | copy-start | bytes 1572868
  21.3 0.8 copy-start.3
  22.1 0.7 copy-start.5
  29.5 14.8 %collective-permute-start.2 = (bf16[1024,256]{1,0:T(8,128)(2,1)S(1)}, bf16[1024,256]{1,0:T(8,128)(2,1)S(1)}, u32[]{:S(2)}, u32[]{:S(2)}) collective-permute-start(bf16[1024,256]{1,0:T(8,128)(2,1)S(1)} %bitcast.5), channel_id=1, source_target_pairs={{0,32},{32,0},{1,33},{33,1},{2,34},{34,2},{3,35},{35,3},{4,36},{36... | collective-permute-start | bytes 1572872 | tf_op jit(solution)/shard_map/ppermute | solution.py:466
  45.5 13.1 %collective-permute-start.3 = (bf16[64,16,128]{2,1,0:T(8,128)(2,1)S(1)}, bf16[64,16,128]{2,1,0:T(8,128)(2,1)S(1)}, u32[]{:S(2)}, u32[]{:S(2)}) collective-permute-start(bf16[64,16,128]{2,1,0:T(8,128)(2,1)S(1)} %get-tuple-element.40.refs_0_), channel_id=1, source_target_pairs={{0,32},{32,0},{1,33},{33,1},{2,34},{34,2},{3,35},{35,3},{4,36},{36... | collective-permute-start | bytes 786440 | tf_op jit(solution)/shard_map/ppermute | solution.py:466
  45.6 50.2 %copy-start = (f32[16,2048]{1,0:T(8,128)S(1)}, f32[16,2048]{1,0:T(8,128)}, u32[]{:S(2)}) copy-start(f32[16,2048]{1,0:T(8,128)} %tgt_ref.3) | copy-start | bytes 393220
  57.1 41.1 %copy-start.2 = (f32[16,8192]{1,0:T(8,128)S(1)}, f32[16,8192]{1,0:T(8,128)}, u32[]{:S(2)}) copy-start(f32[16,8192]{1,0:T(8,128)} %w_ref.3) | copy-start | bytes 1572868
  57.1 41.1 %copy-start.4 = (f32[64,128]{1,0:T(8,128)S(1)}, f32[64,128]{1,0:T(8,128)}, u32[]{:S(2)}) copy-start(f32[64,128]{1,0:T(8,128)} %eig_ref.3) | copy-start | bytes 98308
  57.1 41.1 %copy-start.6 = (s32[64]{0:T(128)S(1)}, s32[64]{0:T(128)}, u32[]{:S(2)}) copy-start(s32[64]{0:T(128)} %idx_ref.3) | copy-start | bytes 772
  57.1 41.1 %copy-start.7 = (f32[128]{0:T(128)S(1)}, f32[128]{0:T(128)}, u32[]{:S(2)}) copy-start(f32[128]{0:T(128)} %param.15) | copy-start | bytes 1540
  57.2 1.5 %collective-permute-start.4 = (f32[16,8,128]{2,1,0:T(8,128)S(1)}, f32[16,8,128]{2,1,0:T(8,128)S(1)}, u32[]{:S(2)}, u32[]{:S(2)}) collective-permute-start(f32[16,8,128]{2,1,0:T(8,128)S(1)} %get-tuple-element.44), channel_id=1, source_target_pairs={{0,32},{32,0},{1,33},{33,1},{2,34},{34,2},{3,35},{35,3},{4,36},{36... | collective-permute-start | bytes 196616 | tf_op jit(solution)/shard_map/ppermute | solution.py:466
  92.8 5.4 %collective-permute-start.5 = (bf16[64,24,128]{2,1,0:T(8,128)(2,1)S(1)}, bf16[64,24,128]{2,1,0:T(8,128)(2,1)S(1)}, u32[]{:S(2)}, u32[]{:S(2)}) collective-permute-start(bf16[64,24,128]{2,1,0:T(8,128)(2,1)S(1)} %all_to_all.16.mine_ref), channel_id=1, source_target_pairs={{0,32},{32,0},{1,33},{33,1},{2,34},{34,2},{3,35},{35,3},{4,36},{36... | collective-permute-start | bytes 1179656 | tf_op jit(solution)/shard_map/ppermute | solution.py:466

commit v6 on v5

--- a/solution.py
+++ b/solution.py
@@ -131,7 +131,8 @@
 
 
 def prepare_kernel(
-    idx_ref, w_ref, eig_ref, cen_ref, w_half_ref, cen_sq_ref, nys_ref, nys_sq_ref, hi_ref, lo_ref, held_ref, picked_ref, sems
+    idx_hbm, w_hbm, eig_hbm, cen_ref, w_half_ref, cen_sq_ref, nys_ref, nys_sq_ref, hi_ref, lo_ref,
+    held_ref, picked_ref, idx_ref, w_ref, eig_ref, sems, side_sems,
 ):
     steps, col, _ = held_ref.shape
     per = 8
@@ -139,13 +140,16 @@
     def fetch(i):
         return pltpu.make_async_copy(cen_ref.at[pl.ds(pl.multiple_of(i * col, col), col), :], held_ref.at[i], sems.at[i])
 
+    side = [
+        pltpu.make_async_copy(*refs, side_sems.at[n])
+        for n, refs in enumerate(((idx_hbm, idx_ref), (eig_hbm, eig_ref), (w_hbm, w_ref)))
+    ]
+    side[0].start()
     fetch(0).start()
     fetch(1).start()
-    eig_t = eig_ref[...].T
-    hi = eig_t.astype(bf16)
-    hi_ref[...] = hi
-    lo_ref[...] = (eig_t - hi.astype(f32)).astype(bf16)
-    w_half_ref[...] = w_ref[...].astype(bf16)
+    side[1].start()
+    side[2].start()
+    side[0].wait()
     row = lax.broadcasted_iota(jnp.int32, (per, col), 0)
     lane = lax.broadcasted_iota(jnp.int32, (per, col), 1)
 
@@ -166,7 +170,14 @@
         picked_ref[at, :] = jnp.dot(chosen, rows, preferred_element_type=f32)
         return carry
 
-    lax.fori_loop(0, steps, step, 0)
+    lax.fori_loop(0, steps, step, 0, unroll=2)
+    side[1].wait()
+    eig_t = eig_ref[...].T
+    hi = eig_t.astype(bf16)
+    hi_ref[...] = hi
+    lo_ref[...] = (eig_t - hi.astype(f32)).astype(bf16)
+    side[2].wait()
+    w_half_ref[...] = w_ref[...].astype(bf16)
     nys = picked_ref[...].astype(bf16)
     nys_ref[...] = nys
     nys_sq_ref[...] = row_norms(nys)
@@ -185,30 +196,40 @@
     ]
     return pl.pallas_call(
         prepare_kernel,
-        in_specs=[SMEM, VMEM, VMEM, HBM],
+        in_specs=[HBM] * 4,
         out_specs=[VMEM] * len(shapes),
         out_shape=[jax.ShapeDtypeStruct(*shape) for shape in shapes],
         scratch_shapes=[
             pltpu.VMEM((count // col, col, D), bf16),
             pltpu.VMEM((points, D), f32),
+            pltpu.SMEM(nys_index.shape, jnp.int32),
+            pltpu.VMEM(weights.shape, f32),
+            pltpu.VMEM(eigvecs.shape, f32),
             pltpu.SemaphoreType.DMA((count // col,)),
+            pltpu.SemaphoreType.DMA((3,)),
         ],
         compiler_params=pltpu.CompilerParams(vmem_limit_bytes=12 * MIB),
         cost_estimate=pl.CostEstimate(flops=4 * 10**9, bytes_accessed=2 * centers.size, transcendentals=0),
         name="prepare",
-    )(nys_index, weights, eigvecs, in_hbm(centers))
-
-
-def values_kernel(w_ref, batch_ref, cen_sq_ref, cen_ref, *refs):
-    kern_ref, pred_ref, rows_ref, sq_ref, acc_ref, held_ref, sems = refs[-7:]
+    )(in_hbm(nys_index), in_hbm(weights), in_hbm(eigvecs), in_hbm(centers))
+
+
+def values_kernel(w_ref, batch_ref, cen_sq_ref, cen_ref, *refs, first):
+    if first:
+        kern_ref, pred_ref, held_ref, rows_ref, sq_ref, acc_ref, sems = refs[-7:]
+    else:
+        kern_ref, pred_ref, rows_ref, sq_ref, acc_ref = refs[-5:]
+        held_ref = cen_ref
     batch, count = kern_ref.shape
-    col, row, sub = held_ref.shape[1], 512, 256
+    col, row, sub = 2048, 512, 256
     steps = count // col
 
     def fetch(i):
-        return pltpu.make_async_copy(cen_ref.at[pl.ds(pl.multiple_of(i * col, col), col), :], held_ref.at[i], sems.at[i])
-
-    fetch(0).start()
+        at = pl.ds(pl.multiple_of(i * col, col), col)
+        return pltpu.make_async_copy(cen_ref.at[at, :], held_ref.at[at, :], sems.at[i])
+
+    if first:
+        fetch(0).start()
     rows = batch_ref[...]
     wide = rows.astype(f32)
     rows_ref[...] = rows * (-2)
@@ -216,11 +237,12 @@
     acc_ref[...] = jnp.zeros_like(acc_ref)
 
     def step(i, carry):
-        fetch(i).wait()
-
-        @pl.when(i + 1 < steps)
-        def _():
-            fetch(i + 1).start()
+        if first:
+            fetch(i).wait()
+
+            @pl.when(i + 1 < steps)
+            def _():
+                fetch(i + 1).start()
 
         for j in range(batch // row):
             at = slice(j * row, (j + 1) * row)
@@ -228,8 +250,7 @@
             acc = acc_ref[:, at]
             for n in range(col // sub):
                 cols = pl.ds(pl.multiple_of(i * col + n * sub, sub), sub)
-                cen = held_ref[i, n * sub : (n + 1) * sub, :]
-                cross = lax.dot_general(rows_ref[at, :], cen, NT, preferred_element_type=f32)
+                cross = lax.dot_general(rows_ref[at, :], held_ref[cols, :], NT, preferred_element_type=f32)
                 kern = laplacian((cross + row_sq) + cen_sq_ref[:, cols])
                 kern_ref[at, cols] = kern
                 acc += lax.dot_general(w_ref[:, cols], kern, NT, preferred_element_type=f32)
@@ -241,27 +262,27 @@
         pred_ref[:, r, :] = acc_ref[:, r * LANES : (r + 1) * LANES]
 
 
-def kernel_values(w_half, centers, batch, cen_sq, after):
+def kernel_values(w_half, centers, batch, cen_sq, after, first):
     half, count, outs = batch.shape[0], centers.shape[0], w_half.shape[0]
     col = 2048
-    return pl.pallas_call(
-        values_kernel,
-        in_specs=[VMEM] * 3 + [HBM] + [ANY] * len(after),
-        out_specs=[VMEM, VMEM],
-        out_shape=[pltpu.VMEM((half, count), bf16), jax.ShapeDtypeStruct((outs, half // LANES, LANES), f32)],
+    held = [pltpu.VMEM(centers.shape, bf16)] if first else []
+    return pl.pallas_call(
+        functools.partial(values_kernel, first=first),
+        in_specs=[VMEM] * 3 + [HBM if first else VMEM] + [ANY] * len(after),
+        out_specs=[VMEM] * (2 + len(held)),
+        out_shape=[pltpu.VMEM((half, count), bf16), jax.ShapeDtypeStruct((outs, half // LANES, LANES), f32)] + held,
         scratch_shapes=[
             pltpu.VMEM((half, D), bf16),
             pltpu.VMEM((half, LANES), f32),
             pltpu.VMEM((outs, half), f32),
-            pltpu.VMEM((count // col, col, D), bf16),
-            pltpu.SemaphoreType.DMA((count // col,)),
-        ],
-        compiler_params=pltpu.CompilerParams(vmem_limit_bytes=12 * MIB),
+        ]
+        + [pltpu.SemaphoreType.DMA((count // col,))] * len(held),
+        compiler_params=pltpu.CompilerParams(vmem_limit_bytes=8 * MIB),
         cost_estimate=pl.CostEstimate(
             flops=8 * half * count * D, bytes_accessed=2 * half * count, transcendentals=2 * half * count
         ),
         name="kernel_values",
-    )(w_half, batch, cen_sq, in_hbm(centers), *after)
+    )(w_half, batch, cen_sq, in_hbm(centers) if first else in_vmem(centers), *after)
 
 
 def nystrom_kernel(core_ref, cen_ref, sq_ref, hi_ref, lo_ref, own_ref, other_ref, keep_ref, give_ref, acc_ref):
@@ -405,7 +426,7 @@
 
 def finish_kernel(
     core_ref, idx_ref, mine_ref, got_ref, pred_ref, resid_ref, grad_ref, tgt_ref, damp_ref, eig_ref, w_ref, kern_ref,
-    out_ref, out_pred_ref, sum_ref, moment_ref,
+    out_hbm, out_pred_ref, sum_ref, moment_ref, out_ref, sems,
 ):
     half, count = kern_ref.shape
     core = core_ref[0]
@@ -437,6 +458,11 @@
     )
     lane = lax.broadcasted_iota(jnp.int32, (outs, LANES), 1)
     col = 1024
+
+    def leave(i):
+        at = slice(i * col, (i + 1) * col)
+        return pltpu.make_async_copy(out_ref.at[:, at], out_hbm.at[:, at], sems.at[i])
+
     for i in range(count // col):
         at = slice(i * col, (i + 1) * col)
         grad = grad_ref[:, at] + jnp.dot(other, kern_ref[:, at], preferred_element_type=f32)
@@ -444,6 +470,9 @@
         for k in range(i * (col // LANES), (i + 1) * (col // LANES)):
             shifts.append(jnp.where(lane == idx_ref[k] - k * LANES, delta[:, k : k + 1], 0.0))
         out_ref[:, at] = (w_ref[:, at] - 2.0 * grad) + jnp.concatenate(shifts, axis=1)
+        leave(i).start()
+    for i in range(count // col):
+        leave(i).wait()
 
 
 def finish(core, nys_index, mine, got, pred, resid, grad, targets, damping, eigvecs, weights, kern):
@@ -451,11 +480,13 @@
     return pl.pallas_call(
         finish_kernel,
         in_specs=[SMEM] * 2 + [VMEM] * 10,
-        out_specs=[VMEM, VMEM],
+        out_specs=[HBM, VMEM],
         out_shape=[jax.ShapeDtypeStruct(weights.shape, f32), jax.ShapeDtypeStruct(targets.shape, f32)],
         scratch_shapes=[
             pltpu.VMEM((chips * PACK, lanes), f32),
             pltpu.VMEM((2 * chips * 2 * kern.shape[0] // LANES, lanes), f32),
+            pltpu.VMEM(weights.shape, f32),
+            pltpu.SemaphoreType.DMA((8,)),
         ],
         compiler_params=pltpu.CompilerParams(vmem_limit_bytes=12 * MIB),
         name="finish",
@@ -486,9 +517,9 @@
     own = rows.reshape(groups * share, D)
     other = swap(own, "core")
 
-    kern_own, pred = kernel_values(w_half, centers, own, cen_sq, nys)
+    kern_own, pred, held = kernel_values(w_half, centers, own, cen_sq, nys, True)
     moment, give = nystrom_terms(core, nys, own, other)
-    kern_other, pred_give = kernel_values(w_half, centers, other, cen_sq, (give, pred))
+    kern_other, pred_give = kernel_values(w_half, held, other, cen_sq, (give, pred), False)
     packed = pack(moment, swap(give, "core"), pred, swap(pred_give, "core"))
     mine = exchange(sum_chips(exchange(packed, CHIPS)), CHIPS)
     got = swap(mine, "core")

time: 104 us -> 102 us (0.981)
  waiting for transfers between devices: 3.7 us -> 6.32 us
  local copies, waits for them, and re-layouts: 2.49 us -> 0.03 us
  blocking collectives: 33.9 us -> 32.7 us
    all_to_all x1, waiting for transfers between devices: 0.82 us -> 3.44 us  [exchange(): return lax.all_to_all(x, axes, split_axis=0, concat_axis=0, tiled=True)]
    unnamed x16 -> x10, local copies, waits for them, and re-layouts: 2.49 us -> 0.03 us
    pallas_call x3, Pallas kernels: 29 us -> 27.8 us  [the longest x2 21.9 us: kernel_values(): pl.pallas_call(functools.partial(values_kernel, first=first), in_specs=[V...]
    all_to_all x2, blocking collectives: 33.9 us -> 32.7 us  [exchange(): return lax.all_to_all(x, axes, split_axis=0, concat_axis=0, tiled=True)]
where the time goes in v6:
time: 102 us; the launch traced here: 101 us
  Pallas kernels  41.3 us (40%)
  blocking collectives  32.7 us (32%)
  starting transfers between devices  20 us (20%)
  waiting for transfers between devices  6.32 us (6%)
    all_to_all x2, blocking collectives, exchange(): return lax.all_to_all(x, axes, split_axis=0, concat_axis=0, tiled=True)  32.7 us
    pallas_call x2, Pallas kernels, kernel_values(): pl.pallas_call(functools.partial(values_kernel, first=first), in_specs=[V...  21.9 us
    ppermute x6, starting transfers between devices, swap(): return lax.ppermute(x, axis, [(0, 1), (1, 0)])  12.2 us
    all_to_all x1, starting transfers between devices, exchange(): return lax.all_to_all(x, axes, split_axis=0, concat_axis=0, tiled=True)  7.8 us
    pallas_call x1, Pallas kernels, prepare(): pl.pallas_call(prepare_kernel, in_specs=[HBM] * 4, out_specs=[VMEM] * len...  5.83 us
    pallas_call x1, Pallas kernels, finish(): pl.pallas_call(finish_kernel, in_specs=[SMEM] * 2 + [VMEM] * 10, out_spec...  5.31 us
    pallas_call x1, Pallas kernels, pick_rows(): pl.pallas_call(pick_kernel, in_specs=[SMEM, HBM, HBM], out_specs=[VMEM, V...  3.58 us
    all_to_all x1, waiting for transfers between devices, exchange(): return lax.all_to_all(x, axes, split_axis=0, concat_axis=0, tiled=True)  3.44 us
  transfers between devices with their start and end apart: 7, of which 4 were waited for; matrix products, arithmetic and copies ran while one was open for 0% of the time, Pallas kernels for 30%

profile of v6, /device:TPU:1, one launch (start us, length us, event | category | flops | bytes accessed | tf_op | source)
XLA Modules:
  0.0 101.5 jit_solution(4212346446132349375)
XLA Ops:
  0.6 0.1 pad_add_fusion.place_ref
  0.7 3.6 %pick_rows.1 = (bf16[32,256]{1,0:T(8,128)(2,1)S(1)}, bf16[32,256]{1,0:T(8,128)(2,1)S(1)}) custom-call(s32[3]{0:T(128)S(1)} %pad_add_fusion.place_ref, s32[2048]{0:T(1024)} %wanted_ref.1, bf16[8192,256]{1,0:T(8,128)(2,1)} %pool_ref.1), custom_call_target="tpu_custom_call" | custom-call | tf_op jit(solution)/shard_map/pick_rows/pallas_call | solution.py:90
  4.3 1.6 %collective-permute-start = (bf16[32,256]{1,0:T(8,128)(2,1)S(1)}, bf16[32,256]{1,0:T(8,128)(2,1)S(1)}, u32[]{:S(2)}, u32[]{:S(2)}) collective-permute-start(bf16[32,256]{1,0:T(8,128)(2,1)S(1)} %get-tuple-element.28), channel_id=1, source_target_pairs={{0,32},{32,0},{1,33},{33,1},{2,34},{34,2},{3,35},{35,3},{4,36},{36... | collective-permute-start | bytes 49160 | tf_op jit(solution)/shard_map/ppermute | solution.py:497
  5.9 0.8 collective-permute-done
  6.8 3.6 %collective-permute-start.1 = (bf16[32,256]{1,0:T(8,128)(2,1)S(1)}, bf16[32,256]{1,0:T(8,128)(2,1)S(1)}, u32[]{:S(2)}, u32[]{:S(2)}) collective-permute-start(bf16[32,256]{1,0:T(8,128)(2,1)S(1)} %add.15.keep_ref), channel_id=1, source_target_pairs={{0,64},{64,0},{1,65},{65,1},{2,66},{66,2},{3,67},{67,3},{4,68},{68... | collective-permute-start | bytes 49160 | tf_op jit(solution)/shard_map/ppermute | solution.py:497
  10.4 1.1 %collective-permute-done.1.got_ref = bf16[32,256]{1,0:T(8,128)(2,1)S(1)} collective-permute-done((bf16[32,256]{1,0:T(8,128)(2,1)S(1)}, bf16[32,256]{1,0:T(8,128)(2,1)S(1)}, u32[]{:S(2)}, u32[]{:S(2)}) %collective-permute-start.1) | collective-permute-done | bytes 16416 | tf_op jit(solution)/shard_map/ppermute | solution.py:497
  11.6 0.9 repeat_sum.1
  12.4 7.8 %all-to-all-start = ((bf16[32,32,256]{2,1,0:T(8,128)(2,1)}), bf16[32,32,256]{2,1,0:T(8,128)(2,1)S(1)}, u32[]{:S(2)}, u32[]{:S(2)}) async-start(bf16[32,32,256]{2,1,0:T(8,128)(2,1)} %repeat_sum.1), calls=%async_computation | async-start | bytes 1048576 | tf_op jit(solution)/shard_map/all_to_all | solution.py:501
  20.2 5.8 %prepare.1 = (bf16[16,8192]{1,0:T(8,128)(2,1)S(1)}, f32[1,8192]{1,0:T(1,128)S(1)}, bf16[64,256]{1,0:T(8,128)(2,1)S(1)}, f32[1,64]{1,0:T(1,128)S(1)}, bf16[128,64...) custom-call(s32[64]{0:T(128)} %idx_ref.1, f32[16,8192]{1,0:T(8,128)} %w_ref.1, f32[64,128]{1,0:T(8,128)} %eig_ref.1, ...), custom_call_target="tpu_custom_call" | custom-call | flops 4000000000 | bytes 4194304 | tf_op jit(solution)/shard_map/prepare/pallas_call | solution.py:197
  26.1 3.4 %all-to-all-done = bf16[32,32,256]{2,1,0:T(8,128)(2,1)S(1)} async-done(((bf16[32,32,256]{2,1,0:T(8,128)(2,1)}), bf16[32,32,256]{2,1,0:T(8,128)(2,1)S(1)}, u32[]{:S(2)}, u32[]{:S(2)}) %all-to-all-start) | async-done | bytes 524320 | tf_op jit(solution)/shard_map/all_to_all | solution.py:501
  29.5 3.3 %collective-permute-start.2 = (bf16[1024,256]{1,0:T(8,128)(2,1)S(1)}, bf16[1024,256]{1,0:T(8,128)(2,1)S(1)}, u32[]{:S(2)}, u32[]{:S(2)}) collective-permute-start(bf16[1024,256]{1,0:T(8,128)(2,1)S(1)} %bitcast.5), channel_id=1, source_target_pairs={{0,32},{32,0},{1,33},{33,1},{2,34},{34,2},{3,35},{35,3},{4,36},{36... | collective-permute-start | bytes 1572872 | tf_op jit(solution)/shard_map/ppermute | solution.py:497
  32.8 11.5 %kernel_values.2 = (bf16[1024,8192]{1,0:T(8,128)(2,1)S(1)}, f32[16,8,128]{2,1,0:T(8,128)S(1)}, bf16[8192,256]{1,0:T(8,128)(2,1)S(1)}) custom-call(bf16[16,8192]{1,0:T(8,128)(2,1)S(1)} %get-tuple-element.42.w_ref, bf16[1024,256]{1,0:T(8,128)(2,1)S(1)} %bitcast.6, f32[1,8192]{1,0:T(1,128)S(1)} %get-tuple-element.43.cen_sq_ref, bf16[8192,256]{1,0:T(8,128)(2,1)} %cen_ref.3, ...), custom_call_target="tpu_custom_call" | custom-call | flops 17179869184 | bytes 16777216 | tf_op jit(solution)/shard_map/kernel_values/pallas_call | solution.py:269
  44.3 0.0 collective-permute-done.2.other_ref.batch_ref
  44.3 1.2 %nystrom_terms.1 = (bf16[64,16,128]{2,1,0:T(8,128)(2,1)S(1)}, bf16[64,16,128]{2,1,0:T(8,128)(2,1)S(1)}) custom-call(s32[1]{0:T(128)} %bitcast.core_ref, bf16[64,256]{1,0:T(8,128)(2,1)S(1)} %get-tuple-element.35.cen_ref.refs_0_, f32[1,64]{1,0:T(1,128)S(1)} %get-tuple-element.36.sq_ref.refs_1_, bf16[128,64]{1,0:T(8,128)(2,1)S(1)} %get-tuple-element.37.hi_ref.refs_2_, ...), custom_call_target="tpu_custom_call" | custom-call | flops 2000000000 | bytes 1048576 | tf_op jit(solution)/shard_map/nystrom_terms/pallas_call | solution.py:310
  45.5 0.1 collective-permute-start.3
  45.6 0.0 copy-start
  45.6 10.4 %kernel_values.3 = (bf16[1024,8192]{1,0:T(8,128)(2,1)S(1)}, f32[16,8,128]{2,1,0:T(8,128)S(1)}) custom-call(bf16[16,8192]{1,0:T(8,128)(2,1)S(1)} %get-tuple-element.42.w_ref, bf16[1024,256]{1,0:T(8,128)(2,1)S(1)} %collective-permute-done.2.other_ref.batch_ref, f32[1,8192]{1,0:T(1,128)S(1)} %get-tuple-element.43.cen_sq_ref, ...), custom_call_target="tpu_custom_call" | custom-call | flops 17179869184 | bytes 16777216 | tf_op jit(solution)/shard_map/kernel_values/pallas_call | solution.py:269
  56.0 0.6 collective-permute-start.4
  56.6 0.9 collective-permute-done.4.pred_in_ref
  57.5 0.0 collective-permute-done.3.moment_in_ref
  57.5 0.2 pack.1
  57.6 18.5 %all_to_all.15.part_ref = bf16[64,24,128]{2,1,0:T(8,128)(2,1)S(1)} all-to-all(bf16[64,24,128]{2,1,0:T(8,128)(2,1)S(1)} %pack.1), channel_id=1, replica_groups=mesh['zh'=2,'core'=2,'y'=4,'zl'=2,'x'=4] {'zh','y','zl','x'}, dimensions={0} | all-to-all | bytes 786432 | tf_op jit(solution)/shard_map/all_to_all | solution.py:501
  76.2 0.1 sum_chips.1
  76.3 14.2 %all_to_all.16.mine_ref = bf16[64,24,128]{2,1,0:T(8,128)(2,1)S(1)} all-to-all(bf16[64,24,128]{2,1,0:T(8,128)(2,1)S(1)} %sum_chips.1), channel_id=1, replica_groups=mesh['zh'=2,'core'=2,'y'=4,'zl'=2,'x'=4] {'zh','y','zl','x'}, dimensions={0} | all-to-all | bytes 786432 | tf_op jit(solution)/shard_map/all_to_all | solution.py:501
  90.5 3.1 %collective-permute-start.5 = (bf16[64,24,128]{2,1,0:T(8,128)(2,1)S(1)}, bf16[64,24,128]{2,1,0:T(8,128)(2,1)S(1)}, u32[]{:S(2)}, u32[]{:S(2)}) collective-permute-start(bf16[64,24,128]{2,1,0:T(8,128)(2,1)S(1)} %all_to_all.16.mine_ref), channel_id=1, source_target_pairs={{0,32},{32,0},{1,33},{33,1},{2,34},{34,2},{3,35},{35,3},{4,36},{36... | collective-permute-start | bytes 1179656 | tf_op jit(solution)/shard_map/ppermute | solution.py:497
  93.6 0.0 copy-done
  93.6 0.0 copy-start.4
  93.6 2.4 %own_grad.1 = (f32[16,1024]{1,0:T(8,128)S(1)}, bf16[16,1024]{1,0:T(8,128)(2,1)S(1)}, f32[16,8192]{1,0:T(8,128)S(1)}) custom-call(s32[1]{0:T(128)} %bitcast.core_ref, bf16[64,24,128]{2,1,0:T(8,128)(2,1)S(1)} %all_to_all.16.mine_ref, f32[16,2048]{1,0:T(8,128)S(1)} %copy-done, bf16[1024,8192]{1,0:T(8,128)(2,1)S(1)} %get-tuple-element.47.kern_ref), custom_call_target="tpu_custom_call" | custom-call | flops 4294967296 | bytes 16777216 | tf_op jit(solution)/shard_map/own_grad/pallas_call | solution.py:411
  96.0 0.0 collective-permute-done.5.got_ref
  96.0 0.0 copy-done.1
  96.0 0.0 copy-done.2
  96.0 5.3 %finish.1 = (f32[16,8192]{1,0:T(8,128)}, f32[16,2048]{1,0:T(8,128)}) custom-call(s32[1]{0:T(128)} %bitcast.core_ref, s32[64]{0:T(128)S(1)} %copy-done.3, bf16[64,24,128]{2,1,0:T(8,128)(2,1)S(1)} %all_to_all.16.mine_ref, bf16[64,24,128]{2,1,0:T(8,128)(2,1)S(1)} %collective-permute-done.5.got_ref, f32[16,1024]{1,0:T(8,128)S(1)} %get-tuple-element.48.pred_ref, ...), custom_call_target="tpu_custom_call" | custom-call | tf_op jit(solution)/shard_map/finish/pallas_call | solution.py:480
  (6 shorter events, 0.0 us)
Async XLA Ops:
  4.3 2.5 %collective-permute-start = (bf16[32,256]{1,0:T(8,128)(2,1)S(1)}, bf16[32,256]{1,0:T(8,128)(2,1)S(1)}, u32[]{:S(2)}, u32[]{:S(2)}) collective-permute-start(bf16[32,256]{1,0:T(8,128)(2,1)S(1)} %get-tuple-element.28), channel_id=1, source_target_pairs={{0,32},{32,0},{1,33},{33,1},{2,34},{34,2},{3,35},{35,3},{4,36},{36... | collective-permute-start | bytes 49160 | tf_op jit(solution)/shard_map/ppermute | solution.py:497
  6.8 4.8 %collective-permute-start.1 = (bf16[32,256]{1,0:T(8,128)(2,1)S(1)}, bf16[32,256]{1,0:T(8,128)(2,1)S(1)}, u32[]{:S(2)}, u32[]{:S(2)}) collective-permute-start(bf16[32,256]{1,0:T(8,128)(2,1)S(1)} %add.15.keep_ref), channel_id=1, source_target_pairs={{0,64},{64,0},{1,65},{65,1},{2,66},{66,2},{3,67},{67,3},{4,68},{68... | collective-permute-start | bytes 49160 | tf_op jit(solution)/shard_map/ppermute | solution.py:497
  12.4 17.1 %all-to-all-start = ((bf16[32,32,256]{2,1,0:T(8,128)(2,1)}), bf16[32,32,256]{2,1,0:T(8,128)(2,1)S(1)}, u32[]{:S(2)}, u32[]{:S(2)}) async-start(bf16[32,32,256]{2,1,0:T(8,128)(2,1)} %repeat_sum.1), calls=%async_computation | async-start | bytes 1048576 | tf_op jit(solution)/shard_map/all_to_all | solution.py:501
  29.5 14.8 %collective-permute-start.2 = (bf16[1024,256]{1,0:T(8,128)(2,1)S(1)}, bf16[1024,256]{1,0:T(8,128)(2,1)S(1)}, u32[]{:S(2)}, u32[]{:S(2)}) collective-permute-start(bf16[1024,256]{1,0:T(8,128)(2,1)S(1)} %bitcast.5), channel_id=1, source_target_pairs={{0,32},{32,0},{1,33},{33,1},{2,34},{34,2},{3,35},{35,3},{4,36},{36... | collective-permute-start | bytes 1572872 | tf_op jit(solution)/shard_map/ppermute | solution.py:497
  45.5 12.0 %collective-permute-start.3 = (bf16[64,16,128]{2,1,0:T(8,128)(2,1)S(1)}, bf16[64,16,128]{2,1,0:T(8,128)(2,1)S(1)}, u32[]{:S(2)}, u32[]{:S(2)}) collective-permute-start(bf16[64,16,128]{2,1,0:T(8,128)(2,1)S(1)} %get-tuple-element.41.refs_0_), channel_id=1, source_target_pairs={{0,32},{32,0},{1,33},{33,1},{2,34},{34,2},{3,35},{35,3},{4,36},{36... | collective-permute-start | bytes 786440 | tf_op jit(solution)/shard_map/ppermute | solution.py:497
  45.6 48.0 %copy-start = (f32[16,2048]{1,0:T(8,128)S(1)}, f32[16,2048]{1,0:T(8,128)}, u32[]{:S(2)}) copy-start(f32[16,2048]{1,0:T(8,128)} %tgt_ref.3) | copy-start | bytes 393220
  56.0 1.5 %collective-permute-start.4 = (f32[16,8,128]{2,1,0:T(8,128)S(1)}, f32[16,8,128]{2,1,0:T(8,128)S(1)}, u32[]{:S(2)}, u32[]{:S(2)}) collective-permute-start(f32[16,8,128]{2,1,0:T(8,128)S(1)} %get-tuple-element.46), channel_id=1, source_target_pairs={{0,32},{32,0},{1,33},{33,1},{2,34},{34,2},{3,35},{35,3},{4,36},{36... | collective-permute-start | bytes 196616 | tf_op jit(solution)/shard_map/ppermute | solution.py:497
  90.5 5.5 %collective-permute-start.5 = (bf16[64,24,128]{2,1,0:T(8,128)(2,1)S(1)}, bf16[64,24,128]{2,1,0:T(8,128)(2,1)S(1)}, u32[]{:S(2)}, u32[]{:S(2)}) collective-permute-start(bf16[64,24,128]{2,1,0:T(8,128)(2,1)S(1)} %all_to_all.16.mine_ref), channel_id=1, source_target_pairs={{0,32},{32,0},{1,33},{33,1},{2,34},{34,2},{3,35},{35,3},{4,36},{36... | collective-permute-start | bytes 1179656 | tf_op jit(solution)/shard_map/ppermute | solution.py:497
  93.6 2.4 %copy-start.1 = (f32[16,8192]{1,0:T(8,128)S(1)}, f32[16,8192]{1,0:T(8,128)}, u32[]{:S(2)}) copy-start(f32[16,8192]{1,0:T(8,128)} %w_ref.1) | copy-start | bytes 1572868
  93.6 2.4 %copy-start.2 = (f32[64,128]{1,0:T(8,128)S(1)}, f32[64,128]{1,0:T(8,128)}, u32[]{:S(2)}) copy-start(f32[64,128]{1,0:T(8,128)} %eig_ref.1) | copy-start | bytes 98308
  93.6 2.4 %copy-start.3 = (s32[64]{0:T(128)S(1)}, s32[64]{0:T(128)}, u32[]{:S(2)}) copy-start(s32[64]{0:T(128)} %idx_ref.1) | copy-start | bytes 772
  93.6 2.4 %copy-start.4 = (f32[128]{0:T(128)S(1)}, f32[128]{0:T(128)}, u32[]{:S(2)}) copy-start(f32[128]{0:T(128)} %param.15) | copy-start | bytes 1540

commit v7 on v6

--- a/solution.py
+++ b/solution.py
@@ -16,6 +16,7 @@
 ALL = LOADER + CENTERS
 CHIPS = ("zh",) + CENTERS
 PACK = 24
+STEP = 2048
 D = 256
 LANES = 128
 RATE = -4.0 / math.sqrt(D) * math.log2(math.e)
@@ -131,7 +132,7 @@
 
 
 def prepare_kernel(
-    idx_hbm, w_hbm, eig_hbm, cen_ref, w_half_ref, cen_sq_ref, nys_ref, nys_sq_ref, hi_ref, lo_ref,
+    idx_hbm, w_hbm, eig_hbm, cen_ref, w_half_ref, cen_sq_ref, head_ref, nys_ref, nys_sq_ref, hi_ref, lo_ref,
     held_ref, picked_ref, idx_ref, w_ref, eig_ref, sems, side_sems,
 ):
     steps, col, _ = held_ref.shape
@@ -172,6 +173,8 @@
 
     lax.fori_loop(0, steps, step, 0, unroll=2)
     side[1].wait()
+    for n in range(head_ref.shape[0] // col):
+        head_ref[n * col : (n + 1) * col, :] = held_ref[n]
     eig_t = eig_ref[...].T
     hi = eig_t.astype(bf16)
     hi_ref[...] = hi
@@ -189,6 +192,7 @@
     shapes = [
         (weights.shape, bf16),
         ((1, count), f32),
+        ((STEP, D), bf16),
         ((points, D), bf16),
         ((1, points), f32),
         ((vectors, points), bf16),
@@ -198,7 +202,7 @@
         prepare_kernel,
         in_specs=[HBM] * 4,
         out_specs=[VMEM] * len(shapes),
-        out_shape=[jax.ShapeDtypeStruct(*shape) for shape in shapes],
+        out_shape=[pltpu.VMEM(*shape) if n == 2 else jax.ShapeDtypeStruct(*shape) for n, shape in enumerate(shapes)],
         scratch_shapes=[
             pltpu.VMEM((count // col, col, D), bf16),
             pltpu.VMEM((points, D), f32),
@@ -221,7 +225,7 @@
         kern_ref, pred_ref, rows_ref, sq_ref, acc_ref = refs[-5:]
         held_ref = cen_ref
     batch, count = kern_ref.shape
-    col, row, sub = 2048, 512, 256
+    col, row, sub = STEP, 512, 256
     steps = count // col
 
     def fetch(i):
@@ -229,7 +233,8 @@
         return pltpu.make_async_copy(cen_ref.at[at, :], held_ref.at[at, :], sems.at[i])
 
     if first:
-        fetch(0).start()
+        fetch(1).start()
+        held_ref[:col, :] = refs[0][...]
     rows = batch_ref[...]
     wide = rows.astype(f32)
     rows_ref[...] = rows * (-2)
@@ -238,9 +243,12 @@
 
     def step(i, carry):
         if first:
-            fetch(i).wait()
-
-            @pl.when(i + 1 < steps)
+
+            @pl.when(i > 0)
+            def _():
+                fetch(i).wait()
+
+            @pl.when(jnp.logical_and(i > 0, i + 1 < steps))
             def _():
                 fetch(i + 1).start()
 
@@ -262,13 +270,14 @@
         pred_ref[:, r, :] = acc_ref[:, r * LANES : (r + 1) * LANES]
 
 
-def kernel_values(w_half, centers, batch, cen_sq, after, first):
+def kernel_values(w_half, centers, batch, cen_sq, after, head=None):
     half, count, outs = batch.shape[0], centers.shape[0], w_half.shape[0]
-    col = 2048
+    first = head is not None
+    heads = [in_vmem(head)] if first else []
     held = [pltpu.VMEM(centers.shape, bf16)] if first else []
     return pl.pallas_call(
         functools.partial(values_kernel, first=first),
-        in_specs=[VMEM] * 3 + [HBM if first else VMEM] + [ANY] * len(after),
+        in_specs=[VMEM] * 3 + [HBM if first else VMEM] + [VMEM] * len(heads) + [ANY] * len(after),
         out_specs=[VMEM] * (2 + len(held)),
         out_shape=[pltpu.VMEM((half, count), bf16), jax.ShapeDtypeStruct((outs, half // LANES, LANES), f32)] + held,
         scratch_shapes=[
@@ -276,13 +285,13 @@
             pltpu.VMEM((half, LANES), f32),
             pltpu.VMEM((outs, half), f32),
         ]
-        + [pltpu.SemaphoreType.DMA((count // col,))] * len(held),
+        + [pltpu.SemaphoreType.DMA((count // STEP,))] * len(held),
         compiler_params=pltpu.CompilerParams(vmem_limit_bytes=8 * MIB),
         cost_estimate=pl.CostEstimate(
             flops=8 * half * count * D, bytes_accessed=2 * half * count, transcendentals=2 * half * count
         ),
         name="kernel_values",
-    )(w_half, batch, cen_sq, in_hbm(centers) if first else in_vmem(centers), *after)
+    )(w_half, batch, cen_sq, in_hbm(centers) if first else in_vmem(centers), *heads, *after)
 
 
 def nystrom_kernel(core_ref, cen_ref, sq_ref, hi_ref, lo_ref, own_ref, other_ref, keep_ref, give_ref, acc_ref):
@@ -426,7 +435,7 @@
 
 def finish_kernel(
     core_ref, idx_ref, mine_ref, got_ref, pred_ref, resid_ref, grad_ref, tgt_ref, damp_ref, eig_ref, w_ref, kern_ref,
-    out_hbm, out_pred_ref, sum_ref, moment_ref, out_ref, sems,
+    out_ref, out_pred_ref, sum_ref, moment_ref,
 ):
     half, count = kern_ref.shape
     core = core_ref[0]
@@ -447,32 +456,27 @@
     lines = chips * 2 * blocks
     for place, part in ((core, mine_ref[...].astype(f32)[:, : 2 * blocks]), (1 - core, swap_halves(got[:, : 2 * blocks], 1))):
         moment_ref[pl.ds(pl.multiple_of(place * lines, lines), lines), :] = part.reshape(lines, LANES)
-    coeff = 0.0
-    for n, resid in enumerate((own, other)):
-        for r in range(blocks):
-            moment = moment_ref[pl.ds(n * blocks + r, 2 * chips, stride=2 * blocks), :].astype(bf16)
-            at = slice(r * LANES, (r + 1) * LANES)
-            coeff += lax.dot_general(resid[:, at], moment, NT, preferred_element_type=f32)
-    delta = 2.0 * lax.dot_general(
-        coeff * damp_ref[...], eig_ref[...], NT, precision=lax.Precision.HIGHEST, preferred_element_type=f32
-    )
-    lane = lax.broadcasted_iota(jnp.int32, (outs, LANES), 1)
     col = 1024
-
-    def leave(i):
-        at = slice(i * col, (i + 1) * col)
-        return pltpu.make_async_copy(out_ref.at[:, at], out_hbm.at[:, at], sems.at[i])
-
-    for i in range(count // col):
+    turns = count // col
+    products = [(n, r) for n in range(2) for r in range(blocks)]
+    per = 2 * len(products) // turns
+    coeff, delta = 0.0, None
+    for i in range(turns):
         at = slice(i * col, (i + 1) * col)
         grad = grad_ref[:, at] + jnp.dot(other, kern_ref[:, at], preferred_element_type=f32)
-        shifts = []
-        for k in range(i * (col // LANES), (i + 1) * (col // LANES)):
-            shifts.append(jnp.where(lane == idx_ref[k] - k * LANES, delta[:, k : k + 1], 0.0))
-        out_ref[:, at] = (w_ref[:, at] - 2.0 * grad) + jnp.concatenate(shifts, axis=1)
-        leave(i).start()
-    for i in range(count // col):
-        leave(i).wait()
+        out_ref[:, at] = w_ref[:, at] - 2.0 * grad
+        for n, r in products[i * per : (i + 1) * per]:
+            moment = moment_ref[pl.ds(n * blocks + r, 2 * chips, stride=2 * blocks), :].astype(bf16)
+            resid = (own, other)[n][:, r * LANES : (r + 1) * LANES]
+            coeff += lax.dot_general(resid, moment, NT, preferred_element_type=f32)
+        if (i + 1) * per == len(products):
+            delta = 2.0 * lax.dot_general(
+                coeff * damp_ref[...], eig_ref[...], NT, precision=lax.Precision.HIGHEST, preferred_element_type=f32
+            )
+    lane = lax.broadcasted_iota(jnp.int32, (outs, LANES), 1)
+    for k in range(delta.shape[1]):
+        at = slice(k * LANES, (k + 1) * LANES)
+        out_ref[:, at] += jnp.where(lane == idx_ref[k] - k * LANES, delta[:, k : k + 1], 0.0)
 
 
 def finish(core, nys_index, mine, got, pred, resid, grad, targets, damping, eigvecs, weights, kern):
@@ -480,13 +484,11 @@
     return pl.pallas_call(
         finish_kernel,
         in_specs=[SMEM] * 2 + [VMEM] * 10,
-        out_specs=[HBM, VMEM],
+        out_specs=[VMEM, VMEM],
         out_shape=[jax.ShapeDtypeStruct(weights.shape, f32), jax.ShapeDtypeStruct(targets.shape, f32)],
         scratch_shapes=[
             pltpu.VMEM((chips * PACK, lanes), f32),
             pltpu.VMEM((2 * chips * 2 * kern.shape[0] // LANES, lanes), f32),
-            pltpu.VMEM(weights.shape, f32),
-            pltpu.SemaphoreType.DMA((8,)),
         ],
         compiler_params=pltpu.CompilerParams(vmem_limit_bytes=12 * MIB),
         name="finish",
@@ -510,16 +512,16 @@
     keep, give = pick_rows(place, batch_index, pool, share)
     rows = keep + swap(give, "core")
     rows = exchange(repeat_sum(rows, swap(rows, "zh"), groups), CENTERS)
-    w_half, cen_sq, *nys = prepare(nys_index, weights, eigvecs, centers)
+    w_half, cen_sq, head, *nys = prepare(nys_index, weights, eigvecs, centers)
     core = core[None]
 
-    rows, cen_sq, w_half, nys = lax.optimization_barrier((rows, cen_sq, w_half, nys))
+    rows, cen_sq, w_half, head, nys = lax.optimization_barrier((rows, cen_sq, w_half, head, nys))
     own = rows.reshape(groups * share, D)
     other = swap(own, "core")
 
-    kern_own, pred, held = kernel_values(w_half, centers, own, cen_sq, nys, True)
+    kern_own, pred, held = kernel_values(w_half, centers, own, cen_sq, nys, head)
     moment, give = nystrom_terms(core, nys, own, other)
-    kern_other, pred_give = kernel_values(w_half, held, other, cen_sq, (give, pred), False)
+    kern_other, pred_give = kernel_values(w_half, held, other, cen_sq, (give, pred))
     packed = pack(moment, swap(give, "core"), pred, swap(pred_give, "core"))
     mine = exchange(sum_chips(exchange(packed, CHIPS)), CHIPS)
     got = swap(mine, "core")

time: 102 us -> 100 us (0.980)
  Pallas kernels: 41.3 us -> 39.7 us
    pallas_call x2, Pallas kernels: 21.9 us -> 20.9 us  [kernel_values(): pl.pallas_call(functools.partial(values_kernel, first=first), in_specs=[V...]
  transfers between devices with their start and end apart: 7 -> 7, of which waited for: 4 -> 4; matrix products, arithmetic and copies ran while one was open for 0% -> 0% of each run, Pallas kernels for 30% -> 29%
where the time goes in v7:
time: 100 us; the launch traced here: 99.6 us
  Pallas kernels  39.7 us (40%)
  blocking collectives  32.9 us (33%)
  starting transfers between devices  19.9 us (20%)
  waiting for transfers between devices  6.26 us (6%)
    all_to_all x2, blocking collectives, exchange(): return lax.all_to_all(x, axes, split_axis=0, concat_axis=0, tiled=True)  32.9 us
    pallas_call x2, Pallas kernels, kernel_values(): pl.pallas_call(functools.partial(values_kernel, first=first), in_specs=[V...  20.9 us
    ppermute x6, starting transfers between devices, swap(): return lax.ppermute(x, axis, [(0, 1), (1, 0)])  12.2 us
    all_to_all x1, starting transfers between devices, exchange(): return lax.all_to_all(x, axes, split_axis=0, concat_axis=0, tiled=True)  7.66 us
    pallas_call x1, Pallas kernels, prepare(): pl.pallas_call(prepare_kernel, in_specs=[HBM] * 4, out_specs=[VMEM] * len...  5.9 us
    pallas_call x1, Pallas kernels, finish(): pl.pallas_call(finish_kernel, in_specs=[SMEM] * 2 + [VMEM] * 10, out_spec...  4.63 us
    pallas_call x1, Pallas kernels, pick_rows(): pl.pallas_call(pick_kernel, in_specs=[SMEM, HBM, HBM], out_specs=[VMEM, V...  3.63 us
    all_to_all x1, waiting for transfers between devices, exchange(): return lax.all_to_all(x, axes, split_axis=0, concat_axis=0, tiled=True)  3.38 us
  transfers between devices with their start and end apart: 7, of which 4 were waited for; matrix products, arithmetic and copies ran while one was open for 0% of the time, Pallas kernels for 29%

profile of v7, /device:TPU:1, one launch (start us, length us, event | category | flops | bytes accessed | tf_op | source)
XLA Modules:
  0.0 99.6 jit_solution(12451582690175238340)
XLA Ops:
  0.6 0.1 pad_add_fusion.place_ref
  0.7 3.6 %pick_rows.1 = (bf16[32,256]{1,0:T(8,128)(2,1)S(1)}, bf16[32,256]{1,0:T(8,128)(2,1)S(1)}) custom-call(s32[3]{0:T(128)S(1)} %pad_add_fusion.place_ref, s32[2048]{0:T(1024)} %wanted_ref.1, bf16[8192,256]{1,0:T(8,128)(2,1)} %pool_ref.1), custom_call_target="tpu_custom_call" | custom-call | tf_op jit(solution)/shard_map/pick_rows/pallas_call | solution.py:91
  4.4 1.6 %collective-permute-start = (bf16[32,256]{1,0:T(8,128)(2,1)S(1)}, bf16[32,256]{1,0:T(8,128)(2,1)S(1)}, u32[]{:S(2)}, u32[]{:S(2)}) collective-permute-start(bf16[32,256]{1,0:T(8,128)(2,1)S(1)} %get-tuple-element.30), channel_id=1, source_target_pairs={{0,32},{32,0},{1,33},{33,1},{2,34},{34,2},{3,35},{35,3},{4,36},{36... | collective-permute-start | bytes 49160 | tf_op jit(solution)/shard_map/ppermute | solution.py:499
  5.9 0.8 collective-permute-done
  6.8 3.7 %collective-permute-start.1 = (bf16[32,256]{1,0:T(8,128)(2,1)S(1)}, bf16[32,256]{1,0:T(8,128)(2,1)S(1)}, u32[]{:S(2)}, u32[]{:S(2)}) collective-permute-start(bf16[32,256]{1,0:T(8,128)(2,1)S(1)} %add.15.keep_ref), channel_id=1, source_target_pairs={{0,64},{64,0},{1,65},{65,1},{2,66},{66,2},{3,67},{67,3},{4,68},{68... | collective-permute-start | bytes 49160 | tf_op jit(solution)/shard_map/ppermute | solution.py:499
  10.5 1.1 %collective-permute-done.1.got_ref = bf16[32,256]{1,0:T(8,128)(2,1)S(1)} collective-permute-done((bf16[32,256]{1,0:T(8,128)(2,1)S(1)}, bf16[32,256]{1,0:T(8,128)(2,1)S(1)}, u32[]{:S(2)}, u32[]{:S(2)}) %collective-permute-start.1) | collective-permute-done | bytes 16416 | tf_op jit(solution)/shard_map/ppermute | solution.py:499
  11.6 0.9 repeat_sum.1
  12.5 7.7 %all-to-all-start = ((bf16[32,32,256]{2,1,0:T(8,128)(2,1)}), bf16[32,32,256]{2,1,0:T(8,128)(2,1)S(1)}, u32[]{:S(2)}, u32[]{:S(2)}) async-start(bf16[32,32,256]{2,1,0:T(8,128)(2,1)} %repeat_sum.1), calls=%async_computation | async-start | bytes 1048576 | tf_op jit(solution)/shard_map/all_to_all | solution.py:503
  20.1 5.9 %prepare.1 = (bf16[16,8192]{1,0:T(8,128)(2,1)S(1)}, f32[1,8192]{1,0:T(1,128)S(1)}, bf16[2048,256]{1,0:T(8,128)(2,1)S(1)}, bf16[64,256]{1,0:T(8,128)(2,1)S(1)}, f...) custom-call(s32[64]{0:T(128)} %idx_ref.1, f32[16,8192]{1,0:T(8,128)} %w_ref.1, ...), custom_call_target="tpu_custom_call" | custom-call | flops 4000000000 | bytes 4194304 | tf_op jit(solution)/shard_map/prepare/pallas_call | solution.py:201
  26.0 3.4 %all-to-all-done = bf16[32,32,256]{2,1,0:T(8,128)(2,1)S(1)} async-done(((bf16[32,32,256]{2,1,0:T(8,128)(2,1)}), bf16[32,32,256]{2,1,0:T(8,128)(2,1)S(1)}, u32[]{:S(2)}, u32[]{:S(2)}) %all-to-all-start) | async-done | bytes 524320 | tf_op jit(solution)/shard_map/all_to_all | solution.py:503
  29.4 3.3 %collective-permute-start.2 = (bf16[1024,256]{1,0:T(8,128)(2,1)S(1)}, bf16[1024,256]{1,0:T(8,128)(2,1)S(1)}, u32[]{:S(2)}, u32[]{:S(2)}) collective-permute-start(bf16[1024,256]{1,0:T(8,128)(2,1)S(1)} %bitcast.5), channel_id=1, source_target_pairs={{0,32},{32,0},{1,33},{33,1},{2,34},{34,2},{3,35},{35,3},{4,36},{36... | collective-permute-start | bytes 1572872 | tf_op jit(solution)/shard_map/ppermute | solution.py:499
  32.7 10.5 %kernel_values.2 = (bf16[1024,8192]{1,0:T(8,128)(2,1)S(1)}, f32[16,8,128]{2,1,0:T(8,128)S(1)}, bf16[8192,256]{1,0:T(8,128)(2,1)S(1)}) custom-call(bf16[16,8192]{1,0:T(8,128)(2,1)S(1)} %get-tuple-element.45.w_ref, bf16[1024,256]{1,0:T(8,128)(2,1)S(1)} %bitcast.6, f32[1,8192]{1,0:T(1,128)S(1)} %get-tuple-element.46.cen_sq_ref, bf16[8192,256]{1,0:T(8,128)(2,1)} %cen_ref.3, ...), custom_call_target="tpu_custom_call" | custom-call | flops 17179869184 | bytes 16777216 | tf_op jit(solution)/shard_map/kernel_values/pallas_call | solution.py:278
  43.1 0.0 collective-permute-done.2.other_ref.batch_ref
  43.2 1.2 %nystrom_terms.1 = (bf16[64,16,128]{2,1,0:T(8,128)(2,1)S(1)}, bf16[64,16,128]{2,1,0:T(8,128)(2,1)S(1)}) custom-call(s32[1]{0:T(128)} %bitcast.core_ref, bf16[64,256]{1,0:T(8,128)(2,1)S(1)} %get-tuple-element.38.cen_ref.refs_1_, f32[1,64]{1,0:T(1,128)S(1)} %get-tuple-element.39.sq_ref.refs_2_, bf16[128,64]{1,0:T(8,128)(2,1)S(1)} %get-tuple-element.40.hi_ref.refs_3_, ...), custom_call_target="tpu_custom_call" | custom-call | flops 2000000000 | bytes 1048576 | tf_op jit(solution)/shard_map/nystrom_terms/pallas_call | solution.py:319
  44.3 0.1 collective-permute-start.3
  44.4 0.0 copy-start
  44.4 10.4 %kernel_values.3 = (bf16[1024,8192]{1,0:T(8,128)(2,1)S(1)}, f32[16,8,128]{2,1,0:T(8,128)S(1)}) custom-call(bf16[16,8192]{1,0:T(8,128)(2,1)S(1)} %get-tuple-element.45.w_ref, bf16[1024,256]{1,0:T(8,128)(2,1)S(1)} %collective-permute-done.2.other_ref.batch_ref, f32[1,8192]{1,0:T(1,128)S(1)} %get-tuple-element.46.cen_sq_ref, ...), custom_call_target="tpu_custom_call" | custom-call | flops 17179869184 | bytes 16777216 | tf_op jit(solution)/shard_map/kernel_values/pallas_call | solution.py:278
  54.9 0.6 collective-permute-start.4
  55.4 0.9 collective-permute-done.4.pred_in_ref
  56.3 0.0 collective-permute-done.3.moment_in_ref
  56.4 0.2 pack.1
  56.5 18.7 %all_to_all.15.part_ref = bf16[64,24,128]{2,1,0:T(8,128)(2,1)S(1)} all-to-all(bf16[64,24,128]{2,1,0:T(8,128)(2,1)S(1)} %pack.1), channel_id=1, replica_groups=mesh['zh'=2,'core'=2,'y'=4,'zl'=2,'x'=4] {'zh','y','zl','x'}, dimensions={0} | all-to-all | bytes 786432 | tf_op jit(solution)/shard_map/all_to_all | solution.py:503
  75.2 0.1 sum_chips.1
  75.3 14.2 %all_to_all.16.mine_ref = bf16[64,24,128]{2,1,0:T(8,128)(2,1)S(1)} all-to-all(bf16[64,24,128]{2,1,0:T(8,128)(2,1)S(1)} %sum_chips.1), channel_id=1, replica_groups=mesh['zh'=2,'core'=2,'y'=4,'zl'=2,'x'=4] {'zh','y','zl','x'}, dimensions={0} | all-to-all | bytes 786432 | tf_op jit(solution)/shard_map/all_to_all | solution.py:503
  89.5 3.1 %collective-permute-start.5 = (bf16[64,24,128]{2,1,0:T(8,128)(2,1)S(1)}, bf16[64,24,128]{2,1,0:T(8,128)(2,1)S(1)}, u32[]{:S(2)}, u32[]{:S(2)}) collective-permute-start(bf16[64,24,128]{2,1,0:T(8,128)(2,1)S(1)} %all_to_all.16.mine_ref), channel_id=1, source_target_pairs={{0,32},{32,0},{1,33},{33,1},{2,34},{34,2},{3,35},{35,3},{4,36},{36... | collective-permute-start | bytes 1179656 | tf_op jit(solution)/shard_map/ppermute | solution.py:499
  92.5 0.0 copy-done
  92.6 0.0 copy-start.4
  92.6 2.4 %own_grad.1 = (f32[16,1024]{1,0:T(8,128)S(1)}, bf16[16,1024]{1,0:T(8,128)(2,1)S(1)}, f32[16,8192]{1,0:T(8,128)S(1)}) custom-call(s32[1]{0:T(128)} %bitcast.core_ref, bf16[64,24,128]{2,1,0:T(8,128)(2,1)S(1)} %all_to_all.16.mine_ref, f32[16,2048]{1,0:T(8,128)S(1)} %copy-done, bf16[1024,8192]{1,0:T(8,128)(2,1)S(1)} %get-tuple-element.51.kern_ref), custom_call_target="tpu_custom_call" | custom-call | flops 4294967296 | bytes 16777216 | tf_op jit(solution)/shard_map/own_grad/pallas_call | solution.py:420
  95.0 0.0 collective-permute-done.5.got_ref
  95.0 0.0 copy-done.1
  95.0 0.0 copy-done.2
  95.0 4.6 %finish.1 = (f32[16,8192]{1,0:T(8,128)}, f32[16,2048]{1,0:T(8,128)}) custom-call(s32[1]{0:T(128)} %bitcast.core_ref, s32[64]{0:T(128)S(1)} %copy-done.3, bf16[64,24,128]{2,1,0:T(8,128)(2,1)S(1)} %all_to_all.16.mine_ref, bf16[64,24,128]{2,1,0:T(8,128)(2,1)S(1)} %collective-permute-done.5.got_ref, f32[16,1024]{1,0:T(8,128)S(1)} %get-tuple-element.52.pred_ref, ...), custom_call_target="tpu_custom_call" | custom-call | tf_op jit(solution)/shard_map/finish/pallas_call | solution.py:484
  (6 shorter events, 0.0 us)
Async XLA Ops:
  4.4 2.4 %collective-permute-start = (bf16[32,256]{1,0:T(8,128)(2,1)S(1)}, bf16[32,256]{1,0:T(8,128)(2,1)S(1)}, u32[]{:S(2)}, u32[]{:S(2)}) collective-permute-start(bf16[32,256]{1,0:T(8,128)(2,1)S(1)} %get-tuple-element.30), channel_id=1, source_target_pairs={{0,32},{32,0},{1,33},{33,1},{2,34},{34,2},{3,35},{35,3},{4,36},{36... | collective-permute-start | bytes 49160 | tf_op jit(solution)/shard_map/ppermute | solution.py:499
  6.8 4.8 %collective-permute-start.1 = (bf16[32,256]{1,0:T(8,128)(2,1)S(1)}, bf16[32,256]{1,0:T(8,128)(2,1)S(1)}, u32[]{:S(2)}, u32[]{:S(2)}) collective-permute-start(bf16[32,256]{1,0:T(8,128)(2,1)S(1)} %add.15.keep_ref), channel_id=1, source_target_pairs={{0,64},{64,0},{1,65},{65,1},{2,66},{66,2},{3,67},{67,3},{4,68},{68... | collective-permute-start | bytes 49160 | tf_op jit(solution)/shard_map/ppermute | solution.py:499
  12.5 17.0 %all-to-all-start = ((bf16[32,32,256]{2,1,0:T(8,128)(2,1)}), bf16[32,32,256]{2,1,0:T(8,128)(2,1)S(1)}, u32[]{:S(2)}, u32[]{:S(2)}) async-start(bf16[32,32,256]{2,1,0:T(8,128)(2,1)} %repeat_sum.1), calls=%async_computation | async-start | bytes 1048576 | tf_op jit(solution)/shard_map/all_to_all | solution.py:503
  29.4 13.7 %collective-permute-start.2 = (bf16[1024,256]{1,0:T(8,128)(2,1)S(1)}, bf16[1024,256]{1,0:T(8,128)(2,1)S(1)}, u32[]{:S(2)}, u32[]{:S(2)}) collective-permute-start(bf16[1024,256]{1,0:T(8,128)(2,1)S(1)} %bitcast.5), channel_id=1, source_target_pairs={{0,32},{32,0},{1,33},{33,1},{2,34},{34,2},{3,35},{35,3},{4,36},{36... | collective-permute-start | bytes 1572872 | tf_op jit(solution)/shard_map/ppermute | solution.py:499
  44.3 12.0 %collective-permute-start.3 = (bf16[64,16,128]{2,1,0:T(8,128)(2,1)S(1)}, bf16[64,16,128]{2,1,0:T(8,128)(2,1)S(1)}, u32[]{:S(2)}, u32[]{:S(2)}) collective-permute-start(bf16[64,16,128]{2,1,0:T(8,128)(2,1)S(1)} %get-tuple-element.44.refs_0_), channel_id=1, source_target_pairs={{0,32},{32,0},{1,33},{33,1},{2,34},{34,2},{3,35},{35,3},{4,36},{36... | collective-permute-start | bytes 786440 | tf_op jit(solution)/shard_map/ppermute | solution.py:499
  44.4 48.1 %copy-start = (f32[16,2048]{1,0:T(8,128)S(1)}, f32[16,2048]{1,0:T(8,128)}, u32[]{:S(2)}) copy-start(f32[16,2048]{1,0:T(8,128)} %tgt_ref.3) | copy-start | bytes 393220
  54.9 1.5 %collective-permute-start.4 = (f32[16,8,128]{2,1,0:T(8,128)S(1)}, f32[16,8,128]{2,1,0:T(8,128)S(1)}, u32[]{:S(2)}, u32[]{:S(2)}) collective-permute-start(f32[16,8,128]{2,1,0:T(8,128)S(1)} %get-tuple-element.50), channel_id=1, source_target_pairs={{0,32},{32,0},{1,33},{33,1},{2,34},{34,2},{3,35},{35,3},{4,36},{36... | collective-permute-start | bytes 196616 | tf_op jit(solution)/shard_map/ppermute | solution.py:499
  89.5 5.5 %collective-permute-start.5 = (bf16[64,24,128]{2,1,0:T(8,128)(2,1)S(1)}, bf16[64,24,128]{2,1,0:T(8,128)(2,1)S(1)}, u32[]{:S(2)}, u32[]{:S(2)}) collective-permute-start(bf16[64,24,128]{2,1,0:T(8,128)(2,1)S(1)} %all_to_all.16.mine_ref), channel_id=1, source_target_pairs={{0,32},{32,0},{1,33},{33,1},{2,34},{34,2},{3,35},{35,3},{4,36},{36... | collective-permute-start | bytes 1179656 | tf_op jit(solution)/shard_map/ppermute | solution.py:499
  92.5 2.4 %copy-start.1 = (f32[16,8192]{1,0:T(8,128)S(1)}, f32[16,8192]{1,0:T(8,128)}, u32[]{:S(2)}) copy-start(f32[16,8192]{1,0:T(8,128)} %w_ref.1) | copy-start | bytes 1572868
  92.5 2.4 %copy-start.2 = (f32[64,128]{1,0:T(8,128)S(1)}, f32[64,128]{1,0:T(8,128)}, u32[]{:S(2)}) copy-start(f32[64,128]{1,0:T(8,128)} %eig_ref.1) | copy-start | bytes 98308
  92.5 2.4 %copy-start.3 = (s32[64]{0:T(128)S(1)}, s32[64]{0:T(128)}, u32[]{:S(2)}) copy-start(s32[64]{0:T(128)} %idx_ref.1) | copy-start | bytes 772
  92.6 2.4 %copy-start.4 = (f32[128]{0:T(128)S(1)}, f32[128]{0:T(128)}, u32[]{:S(2)}) copy-start(f32[128]{0:T(128)} %param.15) | copy-start | bytes 1540

commit v8 on v7

--- a/solution.py
+++ b/solution.py
@@ -435,7 +435,7 @@
 
 def finish_kernel(
     core_ref, idx_ref, mine_ref, got_ref, pred_ref, resid_ref, grad_ref, tgt_ref, damp_ref, eig_ref, w_ref, kern_ref,
-    out_ref, out_pred_ref, sum_ref, moment_ref,
+    out_ref, out_pred_ref, sum_ref, moment_ref, other_ref,
 ):
     half, count = kern_ref.shape
     core = core_ref[0]
@@ -445,34 +445,32 @@
     got = got_ref[...].astype(f32)
     sum_ref[...] = got.reshape(sum_ref.shape)
     out_pred_ref[:, pl.ds(pl.multiple_of(core * half, half), half)] = pred_ref[...]
-    resids = []
     for r in range(blocks):
         at = pl.ds(pl.multiple_of((1 - core) * half + r * LANES, LANES), LANES)
         pred = read_pred(sum_ref, r, outs, 2 * blocks)
         out_pred_ref[:, at] = pred
-        resids.append((pred - tgt_ref[:, at]).astype(bf16))
-    other = jnp.concatenate(resids, axis=1)
-    own = resid_ref[...]
+        other_ref[:, r * LANES : (r + 1) * LANES] = (pred - tgt_ref[:, at]).astype(bf16)
     lines = chips * 2 * blocks
     for place, part in ((core, mine_ref[...].astype(f32)[:, : 2 * blocks]), (1 - core, swap_halves(got[:, : 2 * blocks], 1))):
         moment_ref[pl.ds(pl.multiple_of(place * lines, lines), lines), :] = part.reshape(lines, LANES)
-    col = 1024
-    turns = count // col
-    products = [(n, r) for n in range(2) for r in range(blocks)]
-    per = 2 * len(products) // turns
-    coeff, delta = 0.0, None
-    for i in range(turns):
-        at = slice(i * col, (i + 1) * col)
-        grad = grad_ref[:, at] + jnp.dot(other, kern_ref[:, at], preferred_element_type=f32)
+    col = 2048
+
+    def step(i, carry):
+        at = pl.ds(pl.multiple_of(i * col, col), col)
+        grad = grad_ref[:, at] + jnp.dot(other_ref[...], kern_ref[:, at], preferred_element_type=f32)
         out_ref[:, at] = w_ref[:, at] - 2.0 * grad
-        for n, r in products[i * per : (i + 1) * per]:
+        return carry
+
+    lax.fori_loop(0, count // col, step, 0)
+    coeff = 0.0
+    for n, ref in enumerate((resid_ref, other_ref)):
+        for r in range(blocks):
             moment = moment_ref[pl.ds(n * blocks + r, 2 * chips, stride=2 * blocks), :].astype(bf16)
-            resid = (own, other)[n][:, r * LANES : (r + 1) * LANES]
-            coeff += lax.dot_general(resid, moment, NT, preferred_element_type=f32)
-        if (i + 1) * per == len(products):
-            delta = 2.0 * lax.dot_general(
-                coeff * damp_ref[...], eig_ref[...], NT, precision=lax.Precision.HIGHEST, preferred_element_type=f32
-            )
+            at = slice(r * LANES, (r + 1) * LANES)
+            coeff += lax.dot_general(ref[:, at], moment, NT, preferred_element_type=f32)
+    delta = 2.0 * lax.dot_general(
+        coeff * damp_ref[...], eig_ref[...], NT, precision=lax.Precision.HIGHEST, preferred_element_type=f32
+    )
     lane = lax.broadcasted_iota(jnp.int32, (outs, LANES), 1)
     for k in range(delta.shape[1]):
         at = slice(k * LANES, (k + 1) * LANES)
@@ -489,6 +487,7 @@
         scratch_shapes=[
             pltpu.VMEM((chips * PACK, lanes), f32),
             pltpu.VMEM((2 * chips * 2 * kern.shape[0] // LANES, lanes), f32),
+            pltpu.VMEM(resid.shape, bf16),
         ],
         compiler_params=pltpu.CompilerParams(vmem_limit_bytes=12 * MIB),
         name="finish",

time: 100 us -> 101 us (1.010)
  no operation moved by 1% of the time
where the time goes in v8:
time: 101 us; the launch traced here: 100 us
  Pallas kernels  40.3 us (40%)
  blocking collectives  32.8 us (32%)
  starting transfers between devices  20 us (20%)
  waiting for transfers between devices  6.26 us (6%)
    all_to_all x2, blocking collectives, exchange(): return lax.all_to_all(x, axes, split_axis=0, concat_axis=0, tiled=True)  32.8 us
    pallas_call x2, Pallas kernels, kernel_values(): pl.pallas_call(functools.partial(values_kernel, first=first), in_specs=[V...  20.9 us
    ppermute x6, starting transfers between devices, swap(): return lax.ppermute(x, axis, [(0, 1), (1, 0)])  12.2 us
    all_to_all x1, starting transfers between devices, exchange(): return lax.all_to_all(x, axes, split_axis=0, concat_axis=0, tiled=True)  7.73 us
    pallas_call x1, Pallas kernels, prepare(): pl.pallas_call(prepare_kernel, in_specs=[HBM] * 4, out_specs=[VMEM] * len...  5.9 us
    pallas_call x1, Pallas kernels, finish(): pl.pallas_call(finish_kernel, in_specs=[SMEM] * 2 + [VMEM] * 10, out_spec...  5.14 us
    pallas_call x1, Pallas kernels, pick_rows(): pl.pallas_call(pick_kernel, in_specs=[SMEM, HBM, HBM], out_specs=[VMEM, V...  3.64 us
    all_to_all x1, waiting for transfers between devices, exchange(): return lax.all_to_all(x, axes, split_axis=0, concat_axis=0, tiled=True)  3.38 us
  transfers between devices with their start and end apart: 7, of which 4 were waited for; matrix products, arithmetic and copies ran while one was open for 0% of the time, Pallas kernels for 29%

profile of v8, /device:TPU:1, one launch (start us, length us, event | category | flops | bytes accessed | tf_op | source)
XLA Modules:
  0.0 100.2 jit_solution(1984155498170813553)
XLA Ops:
  0.6 0.1 pad_add_fusion.place_ref
  0.7 3.6 %pick_rows.1 = (bf16[32,256]{1,0:T(8,128)(2,1)S(1)}, bf16[32,256]{1,0:T(8,128)(2,1)S(1)}) custom-call(s32[3]{0:T(128)S(1)} %pad_add_fusion.place_ref, s32[2048]{0:T(1024)} %wanted_ref.1, bf16[8192,256]{1,0:T(8,128)(2,1)} %pool_ref.1), custom_call_target="tpu_custom_call" | custom-call | tf_op jit(solution)/shard_map/pick_rows/pallas_call | solution.py:91
  4.4 1.6 %collective-permute-start = (bf16[32,256]{1,0:T(8,128)(2,1)S(1)}, bf16[32,256]{1,0:T(8,128)(2,1)S(1)}, u32[]{:S(2)}, u32[]{:S(2)}) collective-permute-start(bf16[32,256]{1,0:T(8,128)(2,1)S(1)} %get-tuple-element.30), channel_id=1, source_target_pairs={{0,32},{32,0},{1,33},{33,1},{2,34},{34,2},{3,35},{35,3},{4,36},{36... | collective-permute-start | bytes 49160 | tf_op jit(solution)/shard_map/ppermute | solution.py:498
  5.9 0.8 collective-permute-done
  6.8 3.7 %collective-permute-start.1 = (bf16[32,256]{1,0:T(8,128)(2,1)S(1)}, bf16[32,256]{1,0:T(8,128)(2,1)S(1)}, u32[]{:S(2)}, u32[]{:S(2)}) collective-permute-start(bf16[32,256]{1,0:T(8,128)(2,1)S(1)} %add.15.keep_ref), channel_id=1, source_target_pairs={{0,64},{64,0},{1,65},{65,1},{2,66},{66,2},{3,67},{67,3},{4,68},{68... | collective-permute-start | bytes 49160 | tf_op jit(solution)/shard_map/ppermute | solution.py:498
  10.5 1.1 %collective-permute-done.1.got_ref = bf16[32,256]{1,0:T(8,128)(2,1)S(1)} collective-permute-done((bf16[32,256]{1,0:T(8,128)(2,1)S(1)}, bf16[32,256]{1,0:T(8,128)(2,1)S(1)}, u32[]{:S(2)}, u32[]{:S(2)}) %collective-permute-start.1) | collective-permute-done | bytes 16416 | tf_op jit(solution)/shard_map/ppermute | solution.py:498
  11.6 0.9 repeat_sum.1
  12.5 7.7 %all-to-all-start = ((bf16[32,32,256]{2,1,0:T(8,128)(2,1)}), bf16[32,32,256]{2,1,0:T(8,128)(2,1)S(1)}, u32[]{:S(2)}, u32[]{:S(2)}) async-start(bf16[32,32,256]{2,1,0:T(8,128)(2,1)} %repeat_sum.1), calls=%async_computation | async-start | bytes 1048576 | tf_op jit(solution)/shard_map/all_to_all | solution.py:502
  20.2 5.9 %prepare.1 = (bf16[16,8192]{1,0:T(8,128)(2,1)S(1)}, f32[1,8192]{1,0:T(1,128)S(1)}, bf16[2048,256]{1,0:T(8,128)(2,1)S(1)}, bf16[64,256]{1,0:T(8,128)(2,1)S(1)}, f...) custom-call(s32[64]{0:T(128)} %idx_ref.1, f32[16,8192]{1,0:T(8,128)} %w_ref.1, ...), custom_call_target="tpu_custom_call" | custom-call | flops 4000000000 | bytes 4194304 | tf_op jit(solution)/shard_map/prepare/pallas_call | solution.py:201
  26.1 3.4 %all-to-all-done = bf16[32,32,256]{2,1,0:T(8,128)(2,1)S(1)} async-done(((bf16[32,32,256]{2,1,0:T(8,128)(2,1)}), bf16[32,32,256]{2,1,0:T(8,128)(2,1)S(1)}, u32[]{:S(2)}, u32[]{:S(2)}) %all-to-all-start) | async-done | bytes 524320 | tf_op jit(solution)/shard_map/all_to_all | solution.py:502
  29.5 3.3 %collective-permute-start.2 = (bf16[1024,256]{1,0:T(8,128)(2,1)S(1)}, bf16[1024,256]{1,0:T(8,128)(2,1)S(1)}, u32[]{:S(2)}, u32[]{:S(2)}) collective-permute-start(bf16[1024,256]{1,0:T(8,128)(2,1)S(1)} %bitcast.5), channel_id=1, source_target_pairs={{0,32},{32,0},{1,33},{33,1},{2,34},{34,2},{3,35},{35,3},{4,36},{36... | collective-permute-start | bytes 1572872 | tf_op jit(solution)/shard_map/ppermute | solution.py:498
  32.7 10.5 %kernel_values.2 = (bf16[1024,8192]{1,0:T(8,128)(2,1)S(1)}, f32[16,8,128]{2,1,0:T(8,128)S(1)}, bf16[8192,256]{1,0:T(8,128)(2,1)S(1)}) custom-call(bf16[16,8192]{1,0:T(8,128)(2,1)S(1)} %get-tuple-element.45.w_ref, bf16[1024,256]{1,0:T(8,128)(2,1)S(1)} %bitcast.6, f32[1,8192]{1,0:T(1,128)S(1)} %get-tuple-element.46.cen_sq_ref, bf16[8192,256]{1,0:T(8,128)(2,1)} %cen_ref.3, ...), custom_call_target="tpu_custom_call" | custom-call | flops 17179869184 | bytes 16777216 | tf_op jit(solution)/shard_map/kernel_values/pallas_call | solution.py:278
  43.2 0.0 collective-permute-done.2.other_ref.batch_ref
  43.2 1.2 %nystrom_terms.1 = (bf16[64,16,128]{2,1,0:T(8,128)(2,1)S(1)}, bf16[64,16,128]{2,1,0:T(8,128)(2,1)S(1)}) custom-call(s32[1]{0:T(128)} %bitcast.core_ref, bf16[64,256]{1,0:T(8,128)(2,1)S(1)} %get-tuple-element.38.cen_ref.refs_1_, f32[1,64]{1,0:T(1,128)S(1)} %get-tuple-element.39.sq_ref.refs_2_, bf16[128,64]{1,0:T(8,128)(2,1)S(1)} %get-tuple-element.40.hi_ref.refs_3_, ...), custom_call_target="tpu_custom_call" | custom-call | flops 2000000000 | bytes 1048576 | tf_op jit(solution)/shard_map/nystrom_terms/pallas_call | solution.py:319
  44.4 0.1 collective-permute-start.3
  44.5 0.0 copy-start
  44.5 10.4 %kernel_values.3 = (bf16[1024,8192]{1,0:T(8,128)(2,1)S(1)}, f32[16,8,128]{2,1,0:T(8,128)S(1)}) custom-call(bf16[16,8192]{1,0:T(8,128)(2,1)S(1)} %get-tuple-element.45.w_ref, bf16[1024,256]{1,0:T(8,128)(2,1)S(1)} %collective-permute-done.2.other_ref.batch_ref, f32[1,8192]{1,0:T(1,128)S(1)} %get-tuple-element.46.cen_sq_ref, ...), custom_call_target="tpu_custom_call" | custom-call | flops 17179869184 | bytes 16777216 | tf_op jit(solution)/shard_map/kernel_values/pallas_call | solution.py:278
  55.0 0.6 collective-permute-start.4
  55.5 0.9 collective-permute-done.4.pred_in_ref
  56.4 0.0 collective-permute-done.3.moment_in_ref
  56.4 0.2 pack.1
  56.6 18.6 %all_to_all.15.part_ref = bf16[64,24,128]{2,1,0:T(8,128)(2,1)S(1)} all-to-all(bf16[64,24,128]{2,1,0:T(8,128)(2,1)S(1)} %pack.1), channel_id=1, replica_groups=mesh['zh'=2,'core'=2,'y'=4,'zl'=2,'x'=4] {'zh','y','zl','x'}, dimensions={0} | all-to-all | bytes 786432 | tf_op jit(solution)/shard_map/all_to_all | solution.py:502
  75.2 0.1 sum_chips.1
  75.3 14.2 %all_to_all.16.mine_ref = bf16[64,24,128]{2,1,0:T(8,128)(2,1)S(1)} all-to-all(bf16[64,24,128]{2,1,0:T(8,128)(2,1)S(1)} %sum_chips.1), channel_id=1, replica_groups=mesh['zh'=2,'core'=2,'y'=4,'zl'=2,'x'=4] {'zh','y','zl','x'}, dimensions={0} | all-to-all | bytes 786432 | tf_op jit(solution)/shard_map/all_to_all | solution.py:502
  89.5 3.1 %collective-permute-start.5 = (bf16[64,24,128]{2,1,0:T(8,128)(2,1)S(1)}, bf16[64,24,128]{2,1,0:T(8,128)(2,1)S(1)}, u32[]{:S(2)}, u32[]{:S(2)}) collective-permute-start(bf16[64,24,128]{2,1,0:T(8,128)(2,1)S(1)} %all_to_all.16.mine_ref), channel_id=1, source_target_pairs={{0,32},{32,0},{1,33},{33,1},{2,34},{34,2},{3,35},{35,3},{4,36},{36... | collective-permute-start | bytes 1179656 | tf_op jit(solution)/shard_map/ppermute | solution.py:498
  92.6 0.0 copy-done
  92.6 0.0 copy-start.4
  92.6 2.4 %own_grad.1 = (f32[16,1024]{1,0:T(8,128)S(1)}, bf16[16,1024]{1,0:T(8,128)(2,1)S(1)}, f32[16,8192]{1,0:T(8,128)S(1)}) custom-call(s32[1]{0:T(128)} %bitcast.core_ref, bf16[64,24,128]{2,1,0:T(8,128)(2,1)S(1)} %all_to_all.16.mine_ref, f32[16,2048]{1,0:T(8,128)S(1)} %copy-done, bf16[1024,8192]{1,0:T(8,128)(2,1)S(1)} %get-tuple-element.51.kern_ref), custom_call_target="tpu_custom_call" | custom-call | flops 4294967296 | bytes 16777216 | tf_op jit(solution)/shard_map/own_grad/pallas_call | solution.py:420
  95.0 0.0 collective-permute-done.5.got_ref
  95.0 0.0 copy-done.1
  95.0 0.0 copy-done.2
  95.0 5.1 %finish.1 = (f32[16,8192]{1,0:T(8,128)}, f32[16,2048]{1,0:T(8,128)}) custom-call(s32[1]{0:T(128)} %bitcast.core_ref, s32[64]{0:T(128)S(1)} %copy-done.3, bf16[64,24,128]{2,1,0:T(8,128)(2,1)S(1)} %all_to_all.16.mine_ref, bf16[64,24,128]{2,1,0:T(8,128)(2,1)S(1)} %collective-permute-done.5.got_ref, f32[16,1024]{1,0:T(8,128)S(1)} %get-tuple-element.52.pred_ref, ...), custom_call_target="tpu_custom_call" | custom-call | tf_op jit(solution)/shard_map/finish/pallas_call | solution.py:482
  (6 shorter events, 0.0 us)
Async XLA Ops:
  4.4 2.4 %collective-permute-start = (bf16[32,256]{1,0:T(8,128)(2,1)S(1)}, bf16[32,256]{1,0:T(8,128)(2,1)S(1)}, u32[]{:S(2)}, u32[]{:S(2)}) collective-permute-start(bf16[32,256]{1,0:T(8,128)(2,1)S(1)} %get-tuple-element.30), channel_id=1, source_target_pairs={{0,32},{32,0},{1,33},{33,1},{2,34},{34,2},{3,35},{35,3},{4,36},{36... | collective-permute-start | bytes 49160 | tf_op jit(solution)/shard_map/ppermute | solution.py:498
  6.8 4.8 %collective-permute-start.1 = (bf16[32,256]{1,0:T(8,128)(2,1)S(1)}, bf16[32,256]{1,0:T(8,128)(2,1)S(1)}, u32[]{:S(2)}, u32[]{:S(2)}) collective-permute-start(bf16[32,256]{1,0:T(8,128)(2,1)S(1)} %add.15.keep_ref), channel_id=1, source_target_pairs={{0,64},{64,0},{1,65},{65,1},{2,66},{66,2},{3,67},{67,3},{4,68},{68... | collective-permute-start | bytes 49160 | tf_op jit(solution)/shard_map/ppermute | solution.py:498
  12.5 17.0 %all-to-all-start = ((bf16[32,32,256]{2,1,0:T(8,128)(2,1)}), bf16[32,32,256]{2,1,0:T(8,128)(2,1)S(1)}, u32[]{:S(2)}, u32[]{:S(2)}) async-start(bf16[32,32,256]{2,1,0:T(8,128)(2,1)} %repeat_sum.1), calls=%async_computation | async-start | bytes 1048576 | tf_op jit(solution)/shard_map/all_to_all | solution.py:502
  29.5 13.7 %collective-permute-start.2 = (bf16[1024,256]{1,0:T(8,128)(2,1)S(1)}, bf16[1024,256]{1,0:T(8,128)(2,1)S(1)}, u32[]{:S(2)}, u32[]{:S(2)}) collective-permute-start(bf16[1024,256]{1,0:T(8,128)(2,1)S(1)} %bitcast.5), channel_id=1, source_target_pairs={{0,32},{32,0},{1,33},{33,1},{2,34},{34,2},{3,35},{35,3},{4,36},{36... | collective-permute-start | bytes 1572872 | tf_op jit(solution)/shard_map/ppermute | solution.py:498
  44.4 12.0 %collective-permute-start.3 = (bf16[64,16,128]{2,1,0:T(8,128)(2,1)S(1)}, bf16[64,16,128]{2,1,0:T(8,128)(2,1)S(1)}, u32[]{:S(2)}, u32[]{:S(2)}) collective-permute-start(bf16[64,16,128]{2,1,0:T(8,128)(2,1)S(1)} %get-tuple-element.44.refs_0_), channel_id=1, source_target_pairs={{0,32},{32,0},{1,33},{33,1},{2,34},{34,2},{3,35},{35,3},{4,36},{36... | collective-permute-start | bytes 786440 | tf_op jit(solution)/shard_map/ppermute | solution.py:498
  44.5 48.1 %copy-start = (f32[16,2048]{1,0:T(8,128)S(1)}, f32[16,2048]{1,0:T(8,128)}, u32[]{:S(2)}) copy-start(f32[16,2048]{1,0:T(8,128)} %tgt_ref.3) | copy-start | bytes 393220
  55.0 1.5 %collective-permute-start.4 = (f32[16,8,128]{2,1,0:T(8,128)S(1)}, f32[16,8,128]{2,1,0:T(8,128)S(1)}, u32[]{:S(2)}, u32[]{:S(2)}) collective-permute-start(f32[16,8,128]{2,1,0:T(8,128)S(1)} %get-tuple-element.50), channel_id=1, source_target_pairs={{0,32},{32,0},{1,33},{33,1},{2,34},{34,2},{3,35},{35,3},{4,36},{36... | collective-permute-start | bytes 196616 | tf_op jit(solution)/shard_map/ppermute | solution.py:498
  89.5 5.5 %collective-permute-start.5 = (bf16[64,24,128]{2,1,0:T(8,128)(2,1)S(1)}, bf16[64,24,128]{2,1,0:T(8,128)(2,1)S(1)}, u32[]{:S(2)}, u32[]{:S(2)}) collective-permute-start(bf16[64,24,128]{2,1,0:T(8,128)(2,1)S(1)} %all_to_all.16.mine_ref), channel_id=1, source_target_pairs={{0,32},{32,0},{1,33},{33,1},{2,34},{34,2},{3,35},{35,3},{4,36},{36... | collective-permute-start | bytes 1179656 | tf_op jit(solution)/shard_map/ppermute | solution.py:498
  92.6 2.4 %copy-start.1 = (f32[16,8192]{1,0:T(8,128)S(1)}, f32[16,8192]{1,0:T(8,128)}, u32[]{:S(2)}) copy-start(f32[16,8192]{1,0:T(8,128)} %w_ref.1) | copy-start | bytes 1572868
  92.6 2.4 %copy-start.2 = (f32[64,128]{1,0:T(8,128)S(1)}, f32[64,128]{1,0:T(8,128)}, u32[]{:S(2)}) copy-start(f32[64,128]{1,0:T(8,128)} %eig_ref.1) | copy-start | bytes 98308
  92.6 2.4 %copy-start.3 = (s32[64]{0:T(128)S(1)}, s32[64]{0:T(128)}, u32[]{:S(2)}) copy-start(s32[64]{0:T(128)} %idx_ref.1) | copy-start | bytes 772
  92.6 2.4 %copy-start.4 = (f32[128]{0:T(128)S(1)}, f32[128]{0:T(128)}, u32[]{:S(2)}) copy-start(f32[128]{0:T(128)} %param.15) | copy-start | bytes 1540

commit v9 on v7

--- a/solution.py
+++ b/solution.py
@@ -218,7 +218,7 @@
     )(in_hbm(nys_index), in_hbm(weights), in_hbm(eigvecs), in_hbm(centers))
 
 
-def values_kernel(w_ref, batch_ref, cen_sq_ref, cen_ref, *refs, first):
+def values_kernel(w_ref, batch_ref, cen_sq_ref, cen_ref, *refs, first, start, joined):
     if first:
         kern_ref, pred_ref, held_ref, rows_ref, sq_ref, acc_ref, sems = refs[-7:]
     else:
@@ -235,7 +235,7 @@
     if first:
         fetch(1).start()
         held_ref[:col, :] = refs[0][...]
-    rows = batch_ref[...]
+    rows = batch_ref[start : start + batch, :]
     wide = rows.astype(f32)
     rows_ref[...] = rows * (-2)
     sq_ref[...] = jnp.broadcast_to(jnp.sum(wide * wide, axis=1, keepdims=True), (batch, LANES))
@@ -266,20 +266,27 @@
         return carry
 
     lax.fori_loop(0, steps, step, 0)
+    before = 0
+    if joined:
+        before = refs[0].shape[1]
+        for r in range(before):
+            pred_ref[:, r, :] = refs[0][:, r, :]
     for r in range(batch // LANES):
-        pred_ref[:, r, :] = acc_ref[:, r * LANES : (r + 1) * LANES]
-
-
-def kernel_values(w_half, centers, batch, cen_sq, after, head=None):
-    half, count, outs = batch.shape[0], centers.shape[0], w_half.shape[0]
+        pred_ref[:, before + r, :] = acc_ref[:, r * LANES : (r + 1) * LANES]
+
+
+def kernel_values(w_half, centers, batch, cen_sq, after, rows, head=None, joined=None):
+    half, count, outs = rows[1] - rows[0], centers.shape[0], w_half.shape[0]
+    blocks = half // LANES + (0 if joined is None else joined.shape[1])
     first = head is not None
     heads = [in_vmem(head)] if first else []
+    heads += [] if joined is None else [joined]
     held = [pltpu.VMEM(centers.shape, bf16)] if first else []
     return pl.pallas_call(
-        functools.partial(values_kernel, first=first),
+        functools.partial(values_kernel, first=first, start=rows[0], joined=joined is not None),
         in_specs=[VMEM] * 3 + [HBM if first else VMEM] + [VMEM] * len(heads) + [ANY] * len(after),
         out_specs=[VMEM] * (2 + len(held)),
-        out_shape=[pltpu.VMEM((half, count), bf16), jax.ShapeDtypeStruct((outs, half // LANES, LANES), f32)] + held,
+        out_shape=[pltpu.VMEM((half, count), bf16), jax.ShapeDtypeStruct((outs, blocks, LANES), f32)] + held,
         scratch_shapes=[
             pltpu.VMEM((half, D), bf16),
             pltpu.VMEM((half, LANES), f32),
@@ -397,8 +404,9 @@
     return (part(0) + part(1)) + part(2)
 
 
-def grad_kernel(core_ref, mine_ref, tgt_ref, kern_ref, pred_ref, resid_ref, grad_ref, sum_ref):
-    half, count = kern_ref.shape
+def grad_kernel(core_ref, mine_ref, tgt_ref, kern_ref, last_ref, pred_ref, resid_ref, grad_ref, sum_ref):
+    part, count = kern_ref.shape
+    half = part + last_ref.shape[0]
     blocks = half // LANES
     sum_ref[...] = mine_ref[...].astype(f32).reshape(sum_ref.shape)
     for r in range(blocks):
@@ -411,15 +419,16 @@
     col = 1024
     for i in range(count // col):
         at = slice(i * col, (i + 1) * col)
-        grad_ref[:, at] = jnp.dot(resid, kern_ref[:, at], preferred_element_type=f32)
-
-
-def own_grad(core, mine, targets, kern):
-    half, count = kern.shape
+        grad = jnp.dot(resid[:, :part], kern_ref[:, at], preferred_element_type=f32)
+        grad_ref[:, at] = grad + jnp.dot(resid[:, part:], last_ref[:, at], preferred_element_type=f32)
+
+
+def own_grad(core, mine, targets, kern, last):
+    half, count = kern.shape[0] + last.shape[0], kern.shape[1]
     outs = targets.shape[0]
     return pl.pallas_call(
         grad_kernel,
-        in_specs=[SMEM] + [VMEM] * 3,
+        in_specs=[SMEM] + [VMEM] * 4,
         out_specs=[VMEM] * 3,
         out_shape=[
             jax.ShapeDtypeStruct((outs, half), f32),
@@ -430,7 +439,7 @@
         compiler_params=pltpu.CompilerParams(vmem_limit_bytes=8 * MIB),
         cost_estimate=pl.CostEstimate(flops=512 * half * count, bytes_accessed=2 * half * count, transcendentals=0),
         name="own_grad",
-    )(core, mine, targets, in_vmem(kern))
+    )(core, mine, targets, in_vmem(kern), in_vmem(last))
 
 
 def finish_kernel(
@@ -519,13 +528,15 @@
     own = rows.reshape(groups * share, D)
     other = swap(own, "core")
 
-    kern_own, pred, held = kernel_values(w_half, centers, own, cen_sq, nys, head)
+    half = total // 2
+    kern_first, pred, held = kernel_values(w_half, centers, own, cen_sq, nys, (0, half // 2), head)
     moment, give = nystrom_terms(core, nys, own, other)
-    kern_other, pred_give = kernel_values(w_half, held, other, cen_sq, (give, pred))
+    kern_other, pred_give = kernel_values(w_half, held, other, cen_sq, (give, pred), (0, half))
+    kern_last, pred = kernel_values(w_half, held, own, cen_sq, (pred_give,), (half // 2, half), None, pred)
     packed = pack(moment, swap(give, "core"), pred, swap(pred_give, "core"))
     mine = exchange(sum_chips(exchange(packed, CHIPS)), CHIPS)
     got = swap(mine, "core")
-    pred, resid, grad = own_grad(core, mine, targets, kern_own)
+    pred, resid, grad = own_grad(core, mine, targets, kern_first, kern_last)
     return tuple(
         finish(core, nys_index, mine, got, pred, resid, grad, targets, damping, eigvecs, weights, kern_other)
     )

time: 100 us -> 101 us (1.010)
  Pallas kernels: 39.7 us -> 41.2 us
    pallas_call x3 -> x4, Pallas kernels: 23.3 us -> 24.6 us  [the longest x3 22.2 us: kernel_values(): pl.pallas_call(functools.partial(values_kernel, first=first, start=rows[0...]
  transfers between devices with their start and end apart: 7 -> 7, of which waited for: 4 -> 3; matrix products, arithmetic and copies ran while one was open for 0% -> 0% of each run, Pallas kernels for 29% -> 30%
where the time goes in v9:
time: 101 us; the launch traced here: 100 us
  Pallas kernels  41.2 us (41%)
  blocking collectives  33.4 us (33%)
  starting transfers between devices  19.4 us (19%)
  waiting for transfers between devices  5.36 us (5%)
    all_to_all x2, blocking collectives, exchange(): return lax.all_to_all(x, axes, split_axis=0, concat_axis=0, tiled=True)  33.4 us
    pallas_call x3, Pallas kernels, kernel_values(): pl.pallas_call(functools.partial(values_kernel, first=first, start=rows[0...  22.2 us
    ppermute x6, starting transfers between devices, swap(): return lax.ppermute(x, axis, [(0, 1), (1, 0)])  11.8 us
    all_to_all x1, starting transfers between devices, exchange(): return lax.all_to_all(x, axes, split_axis=0, concat_axis=0, tiled=True)  7.59 us
    pallas_call x1, Pallas kernels, prepare(): pl.pallas_call(prepare_kernel, in_specs=[HBM] * 4, out_specs=[VMEM] * len...  5.9 us
    pallas_call x1, Pallas kernels, finish(): pl.pallas_call(finish_kernel, in_specs=[SMEM] * 2 + [VMEM] * 10, out_spec...  4.65 us
    pallas_call x1, Pallas kernels, pick_rows(): pl.pallas_call(pick_kernel, in_specs=[SMEM, HBM, HBM], out_specs=[VMEM, V...  3.77 us
    all_to_all x1, waiting for transfers between devices, exchange(): return lax.all_to_all(x, axes, split_axis=0, concat_axis=0, tiled=True)  3.38 us
  transfers between devices with their start and end apart: 7, of which 3 were waited for; matrix products, arithmetic and copies ran while one was open for 0% of the time, Pallas kernels for 30%

profile of v9, /device:TPU:1, one launch (start us, length us, event | category | flops | bytes accessed | tf_op | source)
XLA Modules:
  0.0 100.2 jit_solution(12184208442452128636)
XLA Ops:
  0.6 0.1 pad_add_fusion.place_ref
  0.7 3.8 %pick_rows.1 = (bf16[32,256]{1,0:T(8,128)(2,1)S(1)}, bf16[32,256]{1,0:T(8,128)(2,1)S(1)}) custom-call(s32[3]{0:T(128)S(1)} %pad_add_fusion.place_ref, s32[2048]{0:T(1024)} %wanted_ref.1, bf16[8192,256]{1,0:T(8,128)(2,1)} %pool_ref.1), custom_call_target="tpu_custom_call" | custom-call | tf_op jit(solution)/shard_map/pick_rows/pallas_call | solution.py:91
  4.5 1.3 %collective-permute-start = (bf16[32,256]{1,0:T(8,128)(2,1)S(1)}, bf16[32,256]{1,0:T(8,128)(2,1)S(1)}, u32[]{:S(2)}, u32[]{:S(2)}) collective-permute-start(bf16[32,256]{1,0:T(8,128)(2,1)S(1)} %get-tuple-element.32), channel_id=1, source_target_pairs={{0,32},{32,0},{1,33},{33,1},{2,34},{34,2},{3,35},{35,3},{4,36},{36... | collective-permute-start | bytes 49160 | tf_op jit(solution)/shard_map/ppermute | solution.py:508
  5.8 0.8 collective-permute-done
  6.7 3.9 %collective-permute-start.1 = (bf16[32,256]{1,0:T(8,128)(2,1)S(1)}, bf16[32,256]{1,0:T(8,128)(2,1)S(1)}, u32[]{:S(2)}, u32[]{:S(2)}) collective-permute-start(bf16[32,256]{1,0:T(8,128)(2,1)S(1)} %add.15.keep_ref), channel_id=1, source_target_pairs={{0,64},{64,0},{1,65},{65,1},{2,66},{66,2},{3,67},{67,3},{4,68},{68... | collective-permute-start | bytes 49160 | tf_op jit(solution)/shard_map/ppermute | solution.py:508
  10.5 1.1 %collective-permute-done.1.got_ref = bf16[32,256]{1,0:T(8,128)(2,1)S(1)} collective-permute-done((bf16[32,256]{1,0:T(8,128)(2,1)S(1)}, bf16[32,256]{1,0:T(8,128)(2,1)S(1)}, u32[]{:S(2)}, u32[]{:S(2)}) %collective-permute-start.1) | collective-permute-done | bytes 16416 | tf_op jit(solution)/shard_map/ppermute | solution.py:508
  11.6 0.9 repeat_sum.1
  12.5 7.6 %all-to-all-start = ((bf16[32,32,256]{2,1,0:T(8,128)(2,1)}), bf16[32,32,256]{2,1,0:T(8,128)(2,1)S(1)}, u32[]{:S(2)}, u32[]{:S(2)}) async-start(bf16[32,32,256]{2,1,0:T(8,128)(2,1)} %repeat_sum.1), calls=%async_computation | async-start | bytes 1048576 | tf_op jit(solution)/shard_map/all_to_all | solution.py:512
  20.1 5.9 %prepare.1 = (bf16[16,8192]{1,0:T(8,128)(2,1)S(1)}, f32[1,8192]{1,0:T(1,128)S(1)}, bf16[2048,256]{1,0:T(8,128)(2,1)S(1)}, bf16[64,256]{1,0:T(8,128)(2,1)S(1)}, f...) custom-call(s32[64]{0:T(128)} %idx_ref.1, f32[16,8192]{1,0:T(8,128)} %w_ref.1, ...), custom_call_target="tpu_custom_call" | custom-call | flops 4000000000 | bytes 4194304 | tf_op jit(solution)/shard_map/prepare/pallas_call | solution.py:201
  26.0 3.4 %all-to-all-done = bf16[32,32,256]{2,1,0:T(8,128)(2,1)S(1)} async-done(((bf16[32,32,256]{2,1,0:T(8,128)(2,1)}), bf16[32,32,256]{2,1,0:T(8,128)(2,1)S(1)}, u32[]{:S(2)}, u32[]{:S(2)}) %all-to-all-start) | async-done | bytes 524320 | tf_op jit(solution)/shard_map/all_to_all | solution.py:512
  29.4 3.3 %collective-permute-start.2 = (bf16[1024,256]{1,0:T(8,128)(2,1)S(1)}, bf16[1024,256]{1,0:T(8,128)(2,1)S(1)}, u32[]{:S(2)}, u32[]{:S(2)}) collective-permute-start(bf16[1024,256]{1,0:T(8,128)(2,1)S(1)} %bitcast.5), channel_id=1, source_target_pairs={{0,32},{32,0},{1,33},{33,1},{2,34},{34,2},{3,35},{35,3},{4,36},{36... | collective-permute-start | bytes 1572872 | tf_op jit(solution)/shard_map/ppermute | solution.py:508
  32.6 5.9 %kernel_values.3 = (bf16[512,8192]{1,0:T(8,128)(2,1)S(1)}, f32[16,4,128]{2,1,0:T(4,128)S(1)}, bf16[8192,256]{1,0:T(8,128)(2,1)S(1)}) custom-call(bf16[16,8192]{1,0:T(8,128)(2,1)S(1)} %get-tuple-element.47.w_ref, bf16[1024,256]{1,0:T(8,128)(2,1)S(1)} %bitcast.6, f32[1,8192]{1,0:T(1,128)S(1)} %get-tuple-element.48.cen_sq_ref, bf16[8192,256]{1,0:T(8,128)(2,1)} %cen_ref.3, ...), custom_call_target="tpu_custom_call" | custom-call | flops 8589934592 | bytes 8388608 | tf_op jit(solution)/shard_map/kernel_values/pallas_call | solution.py:285
  38.6 0.0 collective-permute-done.2.other_ref.batch_ref
  38.6 1.2 %nystrom_terms.1 = (bf16[64,16,128]{2,1,0:T(8,128)(2,1)S(1)}, bf16[64,16,128]{2,1,0:T(8,128)(2,1)S(1)}) custom-call(s32[1]{0:T(128)} %bitcast.core_ref, bf16[64,256]{1,0:T(8,128)(2,1)S(1)} %get-tuple-element.40.cen_ref.refs_1_, f32[1,64]{1,0:T(1,128)S(1)} %get-tuple-element.41.sq_ref.refs_2_, bf16[128,64]{1,0:T(8,128)(2,1)S(1)} %get-tuple-element.42.hi_ref.refs_3_, ...), custom_call_target="tpu_custom_call" | custom-call | flops 2000000000 | bytes 1048576 | tf_op jit(solution)/shard_map/nystrom_terms/pallas_call | solution.py:326
  39.8 0.1 collective-permute-start.3
  39.9 10.4 %kernel_values.4 = (bf16[1024,8192]{1,0:T(8,128)(2,1)S(1)}, f32[16,8,128]{2,1,0:T(8,128)S(1)}) custom-call(bf16[16,8192]{1,0:T(8,128)(2,1)S(1)} %get-tuple-element.47.w_ref, bf16[1024,256]{1,0:T(8,128)(2,1)S(1)} %collective-permute-done.2.other_ref.batch_ref, f32[1,8192]{1,0:T(1,128)S(1)} %get-tuple-element.48.cen_sq_ref, ...), custom_call_target="tpu_custom_call" | custom-call | flops 17179869184 | bytes 16777216 | tf_op jit(solution)/shard_map/kernel_values/pallas_call | solution.py:285
  50.3 0.0 copy-start
  50.3 0.6 collective-permute-start.4
  50.8 5.9 %kernel_values.5 = (bf16[512,8192]{1,0:T(8,128)(2,1)S(1)}, f32[16,8,128]{2,1,0:T(8,128)S(1)}) custom-call(bf16[16,8192]{1,0:T(8,128)(2,1)S(1)} %get-tuple-element.47.w_ref, bf16[1024,256]{1,0:T(8,128)(2,1)S(1)} %bitcast.8, f32[1,8192]{1,0:T(1,128)S(1)} %get-tuple-element.48.cen_sq_ref, bf16[8192,256]{1,0:T(8,128)(2,1)S(1)} %get-tuple-element.50.cen_ref, ...), custom_call_target="tpu_custom_call" | custom-call | flops 8589934592 | bytes 8388608 | tf_op jit(solution)/shard_map/kernel_values/pallas_call | solution.py:285
  56.7 0.0 collective-permute-done.4.pred_in_ref
  56.7 0.0 collective-permute-done.3.moment_in_ref
  56.8 0.2 pack.1
  56.9 19.2 %all_to_all.15.part_ref = bf16[64,24,128]{2,1,0:T(8,128)(2,1)S(1)} all-to-all(bf16[64,24,128]{2,1,0:T(8,128)(2,1)S(1)} %pack.1), channel_id=1, replica_groups=mesh['zh'=2,'core'=2,'y'=4,'zl'=2,'x'=4] {'zh','y','zl','x'}, dimensions={0} | all-to-all | bytes 786432 | tf_op jit(solution)/shard_map/all_to_all | solution.py:512
  76.1 0.1 sum_chips.1
  76.2 14.2 %all_to_all.16.mine_ref = bf16[64,24,128]{2,1,0:T(8,128)(2,1)S(1)} all-to-all(bf16[64,24,128]{2,1,0:T(8,128)(2,1)S(1)} %sum_chips.1), channel_id=1, replica_groups=mesh['zh'=2,'core'=2,'y'=4,'zl'=2,'x'=4] {'zh','y','zl','x'}, dimensions={0} | all-to-all | bytes 786432 | tf_op jit(solution)/shard_map/all_to_all | solution.py:512
  90.4 2.7 %collective-permute-start.5 = (bf16[64,24,128]{2,1,0:T(8,128)(2,1)S(1)}, bf16[64,24,128]{2,1,0:T(8,128)(2,1)S(1)}, u32[]{:S(2)}, u32[]{:S(2)}) collective-permute-start(bf16[64,24,128]{2,1,0:T(8,128)(2,1)S(1)} %all_to_all.16.mine_ref), channel_id=1, source_target_pairs={{0,32},{32,0},{1,33},{33,1},{2,34},{34,2},{3,35},{35,3},{4,36},{36... | collective-permute-start | bytes 1179656 | tf_op jit(solution)/shard_map/ppermute | solution.py:508
  93.2 0.0 copy-done
  93.2 0.0 copy-start.4
  93.2 2.4 %own_grad.1 = (f32[16,1024]{1,0:T(8,128)S(1)}, bf16[16,1024]{1,0:T(8,128)(2,1)S(1)}, f32[16,8192]{1,0:T(8,128)S(1)}) custom-call(s32[1]{0:T(128)} %bitcast.core_ref, bf16[64,24,128]{2,1,0:T(8,128)(2,1)S(1)} %all_to_all.16.mine_ref, f32[16,2048]{1,0:T(8,128)S(1)} %copy-done, bf16[512,8192]{1,0:T(8,128)(2,1)S(1)} %get-tuple-element.54.kern_ref, ...), custom_call_target="tpu_custom_call" | custom-call | flops 4294967296 | bytes 16777216 | tf_op jit(solution)/shard_map/own_grad/pallas_call | solution.py:429
  95.5 0.0 collective-permute-done.5.got_ref
  95.6 0.0 copy-done.1
  95.6 4.6 %finish.1 = (f32[16,8192]{1,0:T(8,128)}, f32[16,2048]{1,0:T(8,128)}) custom-call(s32[1]{0:T(128)} %bitcast.core_ref, s32[64]{0:T(128)S(1)} %copy-done.3, bf16[64,24,128]{2,1,0:T(8,128)(2,1)S(1)} %all_to_all.16.mine_ref, bf16[64,24,128]{2,1,0:T(8,128)(2,1)S(1)} %collective-permute-done.5.got_ref, f32[16,1024]{1,0:T(8,128)S(1)} %get-tuple-element.56.pred_ref, ...), custom_call_target="tpu_custom_call" | custom-call | tf_op jit(solution)/shard_map/finish/pallas_call | solution.py:493
  (7 shorter events, 0.0 us)
Async XLA Ops:
  4.5 2.2 %collective-permute-start = (bf16[32,256]{1,0:T(8,128)(2,1)S(1)}, bf16[32,256]{1,0:T(8,128)(2,1)S(1)}, u32[]{:S(2)}, u32[]{:S(2)}) collective-permute-start(bf16[32,256]{1,0:T(8,128)(2,1)S(1)} %get-tuple-element.32), channel_id=1, source_target_pairs={{0,32},{32,0},{1,33},{33,1},{2,34},{34,2},{3,35},{35,3},{4,36},{36... | collective-permute-start | bytes 49160 | tf_op jit(solution)/shard_map/ppermute | solution.py:508
  6.7 5.0 %collective-permute-start.1 = (bf16[32,256]{1,0:T(8,128)(2,1)S(1)}, bf16[32,256]{1,0:T(8,128)(2,1)S(1)}, u32[]{:S(2)}, u32[]{:S(2)}) collective-permute-start(bf16[32,256]{1,0:T(8,128)(2,1)S(1)} %add.15.keep_ref), channel_id=1, source_target_pairs={{0,64},{64,0},{1,65},{65,1},{2,66},{66,2},{3,67},{67,3},{4,68},{68... | collective-permute-start | bytes 49160 | tf_op jit(solution)/shard_map/ppermute | solution.py:508
  12.5 16.9 %all-to-all-start = ((bf16[32,32,256]{2,1,0:T(8,128)(2,1)}), bf16[32,32,256]{2,1,0:T(8,128)(2,1)S(1)}, u32[]{:S(2)}, u32[]{:S(2)}) async-start(bf16[32,32,256]{2,1,0:T(8,128)(2,1)} %repeat_sum.1), calls=%async_computation | async-start | bytes 1048576 | tf_op jit(solution)/shard_map/all_to_all | solution.py:512
  29.4 9.2 %collective-permute-start.2 = (bf16[1024,256]{1,0:T(8,128)(2,1)S(1)}, bf16[1024,256]{1,0:T(8,128)(2,1)S(1)}, u32[]{:S(2)}, u32[]{:S(2)}) collective-permute-start(bf16[1024,256]{1,0:T(8,128)(2,1)S(1)} %bitcast.5), channel_id=1, source_target_pairs={{0,32},{32,0},{1,33},{33,1},{2,34},{34,2},{3,35},{35,3},{4,36},{36... | collective-permute-start | bytes 1572872 | tf_op jit(solution)/shard_map/ppermute | solution.py:508
  39.8 17.0 %collective-permute-start.3 = (bf16[64,16,128]{2,1,0:T(8,128)(2,1)S(1)}, bf16[64,16,128]{2,1,0:T(8,128)(2,1)S(1)}, u32[]{:S(2)}, u32[]{:S(2)}) collective-permute-start(bf16[64,16,128]{2,1,0:T(8,128)(2,1)S(1)} %get-tuple-element.46.refs_0_), channel_id=1, source_target_pairs={{0,32},{32,0},{1,33},{33,1},{2,34},{34,2},{3,35},{35,3},{4,36},{36... | collective-permute-start | bytes 786440 | tf_op jit(solution)/shard_map/ppermute | solution.py:508
  50.3 42.9 %copy-start = (f32[16,2048]{1,0:T(8,128)S(1)}, f32[16,2048]{1,0:T(8,128)}, u32[]{:S(2)}) copy-start(f32[16,2048]{1,0:T(8,128)} %tgt_ref.3) | copy-start | bytes 393220
  50.3 6.5 %collective-permute-start.4 = (f32[16,8,128]{2,1,0:T(8,128)S(1)}, f32[16,8,128]{2,1,0:T(8,128)S(1)}, u32[]{:S(2)}, u32[]{:S(2)}) collective-permute-start(f32[16,8,128]{2,1,0:T(8,128)S(1)} %get-tuple-element.52.refs_1_), channel_id=1, source_target_pairs={{0,32},{32,0},{1,33},{33,1},{2,34},{34,2},{3,35},{35,3},{4,36},{36... | collective-permute-start | bytes 196616 | tf_op jit(solution)/shard_map/ppermute | solution.py:508
  90.4 5.1 %collective-permute-start.5 = (bf16[64,24,128]{2,1,0:T(8,128)(2,1)S(1)}, bf16[64,24,128]{2,1,0:T(8,128)(2,1)S(1)}, u32[]{:S(2)}, u32[]{:S(2)}) collective-permute-start(bf16[64,24,128]{2,1,0:T(8,128)(2,1)S(1)} %all_to_all.16.mine_ref), channel_id=1, source_target_pairs={{0,32},{32,0},{1,33},{33,1},{2,34},{34,2},{3,35},{35,3},{4,36},{36... | collective-permute-start | bytes 1179656 | tf_op jit(solution)/shard_map/ppermute | solution.py:508
  93.2 2.4 %copy-start.1 = (f32[16,8192]{1,0:T(8,128)S(1)}, f32[16,8192]{1,0:T(8,128)}, u32[]{:S(2)}) copy-start(f32[16,8192]{1,0:T(8,128)} %w_ref.1) | copy-start | bytes 1572868
  93.2 2.4 %copy-start.2 = (f32[64,128]{1,0:T(8,128)S(1)}, f32[64,128]{1,0:T(8,128)}, u32[]{:S(2)}) copy-start(f32[64,128]{1,0:T(8,128)} %eig_ref.1) | copy-start | bytes 98308
  93.2 2.4 %copy-start.3 = (s32[64]{0:T(128)S(1)}, s32[64]{0:T(128)}, u32[]{:S(2)}) copy-start(s32[64]{0:T(128)} %idx_ref.1) | copy-start | bytes 772
  93.2 2.4 %copy-start.4 = (f32[128]{0:T(128)S(1)}, f32[128]{0:T(128)}, u32[]{:S(2)}) copy-start(f32[128]{0:T(128)} %param.15) | copy-start | bytes 1540

commit v10 on v7

--- a/solution.py
+++ b/solution.py
@@ -52,7 +52,9 @@
 
     def local(n):
         of = jnp.where(n < share, core, 1 - core)
-        return index_ref[of * half + first + jnp.where(n < share, n, n - share)] - mine * rows
+        spot = jnp.where(n < share, n, n - share)
+        spot = jnp.where(spot < share // 2, spot, spot - share // 2 + half // 2)
+        return index_ref[of * half + first + spot] - mine * rows
 
     def copy(n, at):
         return pltpu.make_async_copy(pool_ref.at[pl.ds(pl.multiple_of(at, group), group), :], held_ref.at[n], sems.at[n])
@@ -508,10 +510,13 @@
     core = lax.axis_index("core").astype(jnp.int32)
     groups = lax.axis_size(CENTERS)
     share = total // (2 * groups)
-    place = jnp.stack([lax.axis_index(LOADER), core, lax.axis_index(CENTERS) * share]).astype(jnp.int32)
+    place = jnp.stack([lax.axis_index(LOADER), core, lax.axis_index(CENTERS) * (share // 2)]).astype(jnp.int32)
     keep, give = pick_rows(place, batch_index, pool, share)
     rows = keep + swap(give, "core")
-    rows = exchange(repeat_sum(rows, swap(rows, "zh"), groups), CENTERS)
+    z = lax.axis_index("zh")
+    mine = lax.dynamic_slice_in_dim(rows, z * (share // 2), share // 2)
+    theirs = lax.dynamic_slice_in_dim(rows, (1 - z) * (share // 2), share // 2)
+    rows = exchange(repeat_sum(mine, swap(theirs, "zh"), lax.axis_size(CHIPS)), CHIPS)
     w_half, cen_sq, head, *nys = prepare(nys_index, weights, eigvecs, centers)
     core = core[None]
 

time: 100 us -> 101 us (1.010)
  blocking collectives: 32.9 us -> 29.4 us
  starting transfers between devices: 19.9 us -> 22.4 us
  waiting for transfers between devices: 6.26 us -> 8.25 us
    all_to_all x2, blocking collectives: 32.9 us -> 29.4 us  [exchange(): return lax.all_to_all(x, axes, split_axis=0, concat_axis=0, tiled=True)]
    all_to_all x1, starting transfers between devices: 7.66 us -> 10.4 us  [exchange(): return lax.all_to_all(x, axes, split_axis=0, concat_axis=0, tiled=True)]
    all_to_all x1, waiting for transfers between devices: 3.38 us -> 5.46 us  [exchange(): return lax.all_to_all(x, axes, split_axis=0, concat_axis=0, tiled=True)]
where the time goes in v10:
time: 101 us
  Pallas kernels  39.8 us (39%)
  blocking collectives  29.4 us (29%)
  starting transfers between devices  22.4 us (22%)
  waiting for transfers between devices  8.25 us (8%)
    all_to_all x2, blocking collectives, exchange(): return lax.all_to_all(x, axes, split_axis=0, concat_axis=0, tiled=True)  29.4 us
    pallas_call x2, Pallas kernels, kernel_values(): pl.pallas_call(functools.partial(values_kernel, first=first), in_specs=[V...  20.9 us
    ppermute x6, starting transfers between devices, swap(): return lax.ppermute(x, axis, [(0, 1), (1, 0)])  11.9 us
    all_to_all x1, starting transfers between devices, exchange(): return lax.all_to_all(x, axes, split_axis=0, concat_axis=0, tiled=True)  10.4 us
    pallas_call x1, Pallas kernels, prepare(): pl.pallas_call(prepare_kernel, in_specs=[HBM] * 4, out_specs=[VMEM] * len...  5.9 us
    all_to_all x1, waiting for transfers between devices, exchange(): return lax.all_to_all(x, axes, split_axis=0, concat_axis=0, tiled=True)  5.46 us
    pallas_call x1, Pallas kernels, finish(): pl.pallas_call(finish_kernel, in_specs=[SMEM] * 2 + [VMEM] * 10, out_spec...  4.63 us
    pallas_call x1, Pallas kernels, pick_rows(): pl.pallas_call(pick_kernel, in_specs=[SMEM, HBM, HBM], out_specs=[VMEM, V...  3.73 us
  transfers between devices with their start and end apart: 7, of which 4 were waited for; matrix products, arithmetic and copies ran while one was open for 0% of the time, Pallas kernels for 29%

profile of v10, /device:TPU:1, one launch (start us, length us, event | category | flops | bytes accessed | tf_op | source)
XLA Modules:
  0.0 100.7 jit_solution(10232259013004113338)
XLA Ops:
  0.6 0.1 pad_add_fusion.place_ref
  0.7 3.7 %pick_rows.1 = (bf16[32,256]{1,0:T(8,128)(2,1)S(1)}, bf16[32,256]{1,0:T(8,128)(2,1)S(1)}) custom-call(s32[3]{0:T(128)S(1)} %pad_add_fusion.place_ref, s32[2048]{0:T(1024)} %wanted_ref.1, bf16[8192,256]{1,0:T(8,128)(2,1)} %pool_ref.1), custom_call_target="tpu_custom_call" | custom-call | tf_op jit(solution)/shard_map/pick_rows/pallas_call | solution.py:93
  4.5 1.5 %collective-permute-start = (bf16[32,256]{1,0:T(8,128)(2,1)S(1)}, bf16[32,256]{1,0:T(8,128)(2,1)S(1)}, u32[]{:S(2)}, u32[]{:S(2)}) collective-permute-start(bf16[32,256]{1,0:T(8,128)(2,1)S(1)} %get-tuple-element.30), channel_id=1, source_target_pairs={{0,32},{32,0},{1,33},{33,1},{2,34},{34,2},{3,35},{35,3},{4,36},{36... | collective-permute-start | bytes 49160 | tf_op jit(solution)/shard_map/ppermute | solution.py:501
  6.0 0.8 collective-permute-done
  6.9 3.7 %collective-permute-start.1 = (bf16[16,256]{1,0:T(8,128)(2,1)S(1)}, bf16[16,256]{1,0:T(8,128)(2,1)S(1)}, u32[]{:S(2)}, u32[]{:S(2)}) collective-permute-start(bf16[16,256]{1,0:T(8,128)(2,1)S(1)} %get-tuple-element.56), channel_id=1, source_target_pairs={{0,64},{64,0},{1,65},{65,1},{2,66},{66,2},{3,67},{67,3},{4,68},{68... | collective-permute-start | bytes 24584 | tf_op jit(solution)/shard_map/ppermute | solution.py:501
  10.6 1.0 %collective-permute-done.1.got_ref = bf16[16,256]{1,0:T(8,128)(2,1)S(1)} collective-permute-done((bf16[16,256]{1,0:T(8,128)(2,1)S(1)}, bf16[16,256]{1,0:T(8,128)(2,1)S(1)}, u32[]{:S(2)}, u32[]{:S(2)}) %collective-permute-start.1) | collective-permute-done | bytes 8224 | tf_op jit(solution)/shard_map/ppermute | solution.py:501
  11.6 0.8 repeat_sum.1
  12.5 10.4 %all-to-all-start = ((bf16[64,16,256]{2,1,0:T(8,128)(2,1)}), bf16[64,16,256]{2,1,0:T(8,128)(2,1)S(1)}, u32[]{:S(2)}, u32[]{:S(2)}) async-start(bf16[64,16,256]{2,1,0:T(8,128)(2,1)} %repeat_sum.1), calls=%async_computation | async-start | bytes 1048576 | tf_op jit(solution)/shard_map/all_to_all | solution.py:505
  22.9 5.9 %prepare.1 = (bf16[16,8192]{1,0:T(8,128)(2,1)S(1)}, f32[1,8192]{1,0:T(1,128)S(1)}, bf16[2048,256]{1,0:T(8,128)(2,1)S(1)}, bf16[64,256]{1,0:T(8,128)(2,1)S(1)}, f...) custom-call(s32[64]{0:T(128)} %idx_ref.1, f32[16,8192]{1,0:T(8,128)} %w_ref.1, ...), custom_call_target="tpu_custom_call" | custom-call | flops 4000000000 | bytes 4194304 | tf_op jit(solution)/shard_map/prepare/pallas_call | solution.py:203
  28.8 5.5 %all-to-all-done = bf16[64,16,256]{2,1,0:T(8,128)(2,1)S(1)} async-done(((bf16[64,16,256]{2,1,0:T(8,128)(2,1)}), bf16[64,16,256]{2,1,0:T(8,128)(2,1)S(1)}, u32[]{:S(2)}, u32[]{:S(2)}) %all-to-all-start) | async-done | bytes 524320 | tf_op jit(solution)/shard_map/all_to_all | solution.py:505
  34.3 3.0 %collective-permute-start.2 = (bf16[1024,256]{1,0:T(8,128)(2,1)S(1)}, bf16[1024,256]{1,0:T(8,128)(2,1)S(1)}, u32[]{:S(2)}, u32[]{:S(2)}) collective-permute-start(bf16[1024,256]{1,0:T(8,128)(2,1)S(1)} %bitcast.5), channel_id=1, source_target_pairs={{0,32},{32,0},{1,33},{33,1},{2,34},{34,2},{3,35},{35,3},{4,36},{36... | collective-permute-start | bytes 1572872 | tf_op jit(solution)/shard_map/ppermute | solution.py:501
  37.2 10.5 %kernel_values.2 = (bf16[1024,8192]{1,0:T(8,128)(2,1)S(1)}, f32[16,8,128]{2,1,0:T(8,128)S(1)}, bf16[8192,256]{1,0:T(8,128)(2,1)S(1)}) custom-call(bf16[16,8192]{1,0:T(8,128)(2,1)S(1)} %get-tuple-element.45.w_ref, bf16[1024,256]{1,0:T(8,128)(2,1)S(1)} %bitcast.6, f32[1,8192]{1,0:T(1,128)S(1)} %get-tuple-element.46.cen_sq_ref, bf16[8192,256]{1,0:T(8,128)(2,1)} %cen_ref.3, ...), custom_call_target="tpu_custom_call" | custom-call | flops 17179869184 | bytes 16777216 | tf_op jit(solution)/shard_map/kernel_values/pallas_call | solution.py:280
  47.7 0.0 collective-permute-done.2.other_ref.batch_ref
  47.7 1.2 %nystrom_terms.1 = (bf16[64,16,128]{2,1,0:T(8,128)(2,1)S(1)}, bf16[64,16,128]{2,1,0:T(8,128)(2,1)S(1)}) custom-call(s32[1]{0:T(128)} %bitcast.core_ref, bf16[64,256]{1,0:T(8,128)(2,1)S(1)} %get-tuple-element.38.cen_ref.refs_1_, f32[1,64]{1,0:T(1,128)S(1)} %get-tuple-element.39.sq_ref.refs_2_, bf16[128,64]{1,0:T(8,128)(2,1)S(1)} %get-tuple-element.40.hi_ref.refs_3_, ...), custom_call_target="tpu_custom_call" | custom-call | flops 2000000000 | bytes 1048576 | tf_op jit(solution)/shard_map/nystrom_terms/pallas_call | solution.py:321
  48.9 0.1 collective-permute-start.3
  49.0 0.0 copy-start
  49.0 10.4 %kernel_values.3 = (bf16[1024,8192]{1,0:T(8,128)(2,1)S(1)}, f32[16,8,128]{2,1,0:T(8,128)S(1)}) custom-call(bf16[16,8192]{1,0:T(8,128)(2,1)S(1)} %get-tuple-element.45.w_ref, bf16[1024,256]{1,0:T(8,128)(2,1)S(1)} %collective-permute-done.2.other_ref.batch_ref, f32[1,8192]{1,0:T(1,128)S(1)} %get-tuple-element.46.cen_sq_ref, ...), custom_call_target="tpu_custom_call" | custom-call | flops 17179869184 | bytes 16777216 | tf_op jit(solution)/shard_map/kernel_values/pallas_call | solution.py:280
  59.4 0.6 collective-permute-start.4
  60.0 0.9 collective-permute-done.4.pred_in_ref
  60.9 0.0 collective-permute-done.3.moment_in_ref
  60.9 0.2 pack.1
  61.1 15.2 %all_to_all.15.part_ref = bf16[64,24,128]{2,1,0:T(8,128)(2,1)S(1)} all-to-all(bf16[64,24,128]{2,1,0:T(8,128)(2,1)S(1)} %pack.1), channel_id=1, replica_groups=mesh['zh'=2,'core'=2,'y'=4,'zl'=2,'x'=4] {'zh','y','zl','x'}, dimensions={0} | all-to-all | bytes 786432 | tf_op jit(solution)/shard_map/all_to_all | solution.py:505
  76.3 0.1 sum_chips.1
  76.4 14.2 %all_to_all.16.mine_ref = bf16[64,24,128]{2,1,0:T(8,128)(2,1)S(1)} all-to-all(bf16[64,24,128]{2,1,0:T(8,128)(2,1)S(1)} %sum_chips.1), channel_id=1, replica_groups=mesh['zh'=2,'core'=2,'y'=4,'zl'=2,'x'=4] {'zh','y','zl','x'}, dimensions={0} | all-to-all | bytes 786432 | tf_op jit(solution)/shard_map/all_to_all | solution.py:505
  90.6 3.1 %collective-permute-start.5 = (bf16[64,24,128]{2,1,0:T(8,128)(2,1)S(1)}, bf16[64,24,128]{2,1,0:T(8,128)(2,1)S(1)}, u32[]{:S(2)}, u32[]{:S(2)}) collective-permute-start(bf16[64,24,128]{2,1,0:T(8,128)(2,1)S(1)} %all_to_all.16.mine_ref), channel_id=1, source_target_pairs={{0,32},{32,0},{1,33},{33,1},{2,34},{34,2},{3,35},{35,3},{4,36},{36... | collective-permute-start | bytes 1179656 | tf_op jit(solution)/shard_map/ppermute | solution.py:501
  93.6 0.0 copy-done
  93.6 0.0 copy-start.4
  93.6 2.4 %own_grad.1 = (f32[16,1024]{1,0:T(8,128)S(1)}, bf16[16,1024]{1,0:T(8,128)(2,1)S(1)}, f32[16,8192]{1,0:T(8,128)S(1)}) custom-call(s32[1]{0:T(128)} %bitcast.core_ref, bf16[64,24,128]{2,1,0:T(8,128)(2,1)S(1)} %all_to_all.16.mine_ref, f32[16,2048]{1,0:T(8,128)S(1)} %copy-done, bf16[1024,8192]{1,0:T(8,128)(2,1)S(1)} %get-tuple-element.51.kern_ref), custom_call_target="tpu_custom_call" | custom-call | flops 4294967296 | bytes 16777216 | tf_op jit(solution)/shard_map/own_grad/pallas_call | solution.py:422
  96.0 0.0 collective-permute-done.5.got_ref
  96.0 0.0 copy-done.1
  96.0 0.0 copy-done.2
  96.1 4.6 %finish.1 = (f32[16,8192]{1,0:T(8,128)}, f32[16,2048]{1,0:T(8,128)}) custom-call(s32[1]{0:T(128)} %bitcast.core_ref, s32[64]{0:T(128)S(1)} %copy-done.3, bf16[64,24,128]{2,1,0:T(8,128)(2,1)S(1)} %all_to_all.16.mine_ref, bf16[64,24,128]{2,1,0:T(8,128)(2,1)S(1)} %collective-permute-done.5.got_ref, f32[16,1024]{1,0:T(8,128)S(1)} %get-tuple-element.52.pred_ref, ...), custom_call_target="tpu_custom_call" | custom-call | tf_op jit(solution)/shard_map/finish/pallas_call | solution.py:486
  (7 shorter events, 0.0 us)
Async XLA Ops:
  4.5 2.4 %collective-permute-start = (bf16[32,256]{1,0:T(8,128)(2,1)S(1)}, bf16[32,256]{1,0:T(8,128)(2,1)S(1)}, u32[]{:S(2)}, u32[]{:S(2)}) collective-permute-start(bf16[32,256]{1,0:T(8,128)(2,1)S(1)} %get-tuple-element.30), channel_id=1, source_target_pairs={{0,32},{32,0},{1,33},{33,1},{2,34},{34,2},{3,35},{35,3},{4,36},{36... | collective-permute-start | bytes 49160 | tf_op jit(solution)/shard_map/ppermute | solution.py:501
  6.9 4.8 %collective-permute-start.1 = (bf16[16,256]{1,0:T(8,128)(2,1)S(1)}, bf16[16,256]{1,0:T(8,128)(2,1)S(1)}, u32[]{:S(2)}, u32[]{:S(2)}) collective-permute-start(bf16[16,256]{1,0:T(8,128)(2,1)S(1)} %get-tuple-element.56), channel_id=1, source_target_pairs={{0,64},{64,0},{1,65},{65,1},{2,66},{66,2},{3,67},{67,3},{4,68},{68... | collective-permute-start | bytes 24584 | tf_op jit(solution)/shard_map/ppermute | solution.py:501
  12.5 21.8 %all-to-all-start = ((bf16[64,16,256]{2,1,0:T(8,128)(2,1)}), bf16[64,16,256]{2,1,0:T(8,128)(2,1)S(1)}, u32[]{:S(2)}, u32[]{:S(2)}) async-start(bf16[64,16,256]{2,1,0:T(8,128)(2,1)} %repeat_sum.1), calls=%async_computation | async-start | bytes 1048576 | tf_op jit(solution)/shard_map/all_to_all | solution.py:505
  34.3 13.4 %collective-permute-start.2 = (bf16[1024,256]{1,0:T(8,128)(2,1)S(1)}, bf16[1024,256]{1,0:T(8,128)(2,1)S(1)}, u32[]{:S(2)}, u32[]{:S(2)}) collective-permute-start(bf16[1024,256]{1,0:T(8,128)(2,1)S(1)} %bitcast.5), channel_id=1, source_target_pairs={{0,32},{32,0},{1,33},{33,1},{2,34},{34,2},{3,35},{35,3},{4,36},{36... | collective-permute-start | bytes 1572872 | tf_op jit(solution)/shard_map/ppermute | solution.py:501
  48.9 12.0 %collective-permute-start.3 = (bf16[64,16,128]{2,1,0:T(8,128)(2,1)S(1)}, bf16[64,16,128]{2,1,0:T(8,128)(2,1)S(1)}, u32[]{:S(2)}, u32[]{:S(2)}) collective-permute-start(bf16[64,16,128]{2,1,0:T(8,128)(2,1)S(1)} %get-tuple-element.44.refs_0_), channel_id=1, source_target_pairs={{0,32},{32,0},{1,33},{33,1},{2,34},{34,2},{3,35},{35,3},{4,36},{36... | collective-permute-start | bytes 786440 | tf_op jit(solution)/shard_map/ppermute | solution.py:501
  49.0 44.6 %copy-start = (f32[16,2048]{1,0:T(8,128)S(1)}, f32[16,2048]{1,0:T(8,128)}, u32[]{:S(2)}) copy-start(f32[16,2048]{1,0:T(8,128)} %tgt_ref.3) | copy-start | bytes 393220
  59.4 1.5 %collective-permute-start.4 = (f32[16,8,128]{2,1,0:T(8,128)S(1)}, f32[16,8,128]{2,1,0:T(8,128)S(1)}, u32[]{:S(2)}, u32[]{:S(2)}) collective-permute-start(f32[16,8,128]{2,1,0:T(8,128)S(1)} %get-tuple-element.50), channel_id=1, source_target_pairs={{0,32},{32,0},{1,33},{33,1},{2,34},{34,2},{3,35},{35,3},{4,36},{36... | collective-permute-start | bytes 196616 | tf_op jit(solution)/shard_map/ppermute | solution.py:501
  90.6 5.5 %collective-permute-start.5 = (bf16[64,24,128]{2,1,0:T(8,128)(2,1)S(1)}, bf16[64,24,128]{2,1,0:T(8,128)(2,1)S(1)}, u32[]{:S(2)}, u32[]{:S(2)}) collective-permute-start(bf16[64,24,128]{2,1,0:T(8,128)(2,1)S(1)} %all_to_all.16.mine_ref), channel_id=1, source_target_pairs={{0,32},{32,0},{1,33},{33,1},{2,34},{34,2},{3,35},{35,3},{4,36},{36... | collective-permute-start | bytes 1179656 | tf_op jit(solution)/shard_map/ppermute | solution.py:501
  93.6 2.4 %copy-start.1 = (f32[16,8192]{1,0:T(8,128)S(1)}, f32[16,8192]{1,0:T(8,128)}, u32[]{:S(2)}) copy-start(f32[16,8192]{1,0:T(8,128)} %w_ref.1) | copy-start | bytes 1572868
  93.6 2.4 %copy-start.2 = (f32[64,128]{1,0:T(8,128)S(1)}, f32[64,128]{1,0:T(8,128)}, u32[]{:S(2)}) copy-start(f32[64,128]{1,0:T(8,128)} %eig_ref.1) | copy-start | bytes 98308
  93.6 2.4 %copy-start.3 = (s32[64]{0:T(128)S(1)}, s32[64]{0:T(128)}, u32[]{:S(2)}) copy-start(s32[64]{0:T(128)} %idx_ref.1) | copy-start | bytes 772
  93.6 2.4 %copy-start.4 = (f32[128]{0:T(128)S(1)}, f32[128]{0:T(128)}, u32[]{:S(2)}) copy-start(f32[128]{0:T(128)} %param.15) | copy-start | bytes 1540

commit v11 on v7

--- a/solution.py
+++ b/solution.py
@@ -13,6 +13,7 @@
 MIB = 2**20
 LOADER = ("zh", "core")
 CENTERS = ("y", "zl", "x")
+PLANE = ("y", "x")
 ALL = LOADER + CENTERS
 CHIPS = ("zh",) + CENTERS
 PACK = 24
@@ -105,19 +106,24 @@
     )(place, in_hbm(batch_index), in_hbm(pool))
 
 
-def repeat_kernel(keep_ref, got_ref, out_ref):
-    out_ref[...] = jnp.broadcast_to((keep_ref[...] + got_ref[...])[None], out_ref.shape)
-
-
-def repeat_sum(keep, got, times):
+def repeat_kernel(z_ref, mine_ref, far_ref, near_ref, across_ref, out_ref):
+    share = mine_ref.shape[0]
+    for place, refs in ((z_ref[0], (mine_ref, far_ref)), (1 - z_ref[0], (near_ref, across_ref))):
+        at = pl.ds(pl.multiple_of(place * share, share), share)
+        rows = refs[0][...] + refs[1][...]
+        out_ref[:, at, :] = jnp.broadcast_to(rows[None], (out_ref.shape[0],) + rows.shape)
+
+
+def repeat_sum(z, parts, times):
+    share, width = parts[0].shape
     return pl.pallas_call(
         repeat_kernel,
-        in_specs=[VMEM, VMEM],
+        in_specs=[SMEM] + [VMEM] * 4,
         out_specs=VMEM,
-        out_shape=jax.ShapeDtypeStruct((times,) + keep.shape, bf16),
+        out_shape=jax.ShapeDtypeStruct((times, 2 * share, width), bf16),
         compiler_params=pltpu.CompilerParams(vmem_limit_bytes=4 * MIB),
         name="repeat_sum",
-    )(keep, got)
+    )(z, *parts)
 
 
 def row_norms(rows):
@@ -508,10 +514,13 @@
     core = lax.axis_index("core").astype(jnp.int32)
     groups = lax.axis_size(CENTERS)
     share = total // (2 * groups)
-    place = jnp.stack([lax.axis_index(LOADER), core, lax.axis_index(CENTERS) * share]).astype(jnp.int32)
+    z = lax.axis_index("zl").astype(jnp.int32)
+    place = jnp.stack([lax.axis_index(LOADER), core, lax.axis_index(PLANE) * 2 * share + z * share]).astype(jnp.int32)
     keep, give = pick_rows(place, batch_index, pool, share)
     rows = keep + swap(give, "core")
-    rows = exchange(repeat_sum(rows, swap(rows, "zh"), groups), CENTERS)
+    across = lax.ppermute(rows, ("zh", "zl"), [(n, 3 - n) for n in range(4)])
+    parts = (rows, swap(rows, "zh"), swap(rows, "zl"), across)
+    rows = exchange(repeat_sum(z[None], parts, lax.axis_size(PLANE)), PLANE)
     w_half, cen_sq, head, *nys = prepare(nys_index, weights, eigvecs, centers)
     core = core[None]
 

time: 100 us -> 99 us (0.990)
  blocking collectives: 32.9 us -> 29.4 us
  waiting for transfers between devices: 6.26 us -> 8.95 us
    all_to_all x2, blocking collectives: 32.9 us -> 29.4 us  [exchange(): return lax.all_to_all(x, axes, split_axis=0, concat_axis=0, tiled=True)]
    ppermute x0 -> x1, waiting for transfers between devices: none -> 1.76 us  [body(): across = lax.ppermute(rows, ('zh', 'zl'), [(n, 3 - n) for n in range(4)])]
    ppermute x6 -> x7, waiting for transfers between devices: 2.88 us -> 3.79 us  [swap(): return lax.ppermute(x, axis, [(0, 1), (1, 0)])]
    ppermute x6 -> x7, starting transfers between devices: 12.2 us -> 12.6 us  [swap(): return lax.ppermute(x, axis, [(0, 1), (1, 0)])]
  transfers between devices with their start and end apart: 7 -> 9, of which waited for: 4 -> 6; matrix products, arithmetic and copies ran while one was open for 0% -> 0% of each run, Pallas kernels for 29% -> 30%
where the time goes in v11:
time: 99 us; the launch traced here: 98.5 us
  Pallas kernels  39.8 us (40%)
  blocking collectives  29.4 us (30%)
  starting transfers between devices  19.4 us (20%)
  waiting for transfers between devices  8.95 us (9%)
    all_to_all x2, blocking collectives, exchange(): return lax.all_to_all(x, axes, split_axis=0, concat_axis=0, tiled=True)  29.4 us
    pallas_call x2, Pallas kernels, kernel_values(): pl.pallas_call(functools.partial(values_kernel, first=first), in_specs=[V...  20.9 us
    ppermute x7, starting transfers between devices, swap(): return lax.ppermute(x, axis, [(0, 1), (1, 0)])  12.6 us
    all_to_all x1, starting transfers between devices, exchange(): return lax.all_to_all(x, axes, split_axis=0, concat_axis=0, tiled=True)  6.8 us
    pallas_call x1, Pallas kernels, prepare(): pl.pallas_call(prepare_kernel, in_specs=[HBM] * 4, out_specs=[VMEM] * len...  5.9 us
    pallas_call x1, Pallas kernels, finish(): pl.pallas_call(finish_kernel, in_specs=[SMEM] * 2 + [VMEM] * 10, out_spec...  4.63 us
    ppermute x7, waiting for transfers between devices, swap(): return lax.ppermute(x, axis, [(0, 1), (1, 0)])  3.79 us
    pallas_call x1, Pallas kernels, pick_rows(): pl.pallas_call(pick_kernel, in_specs=[SMEM, HBM, HBM], out_specs=[VMEM, V...  3.72 us
  transfers between devices with their start and end apart: 9, of which 6 were waited for; matrix products, arithmetic and copies ran while one was open for 0% of the time, Pallas kernels for 30%

profile of v11, /device:TPU:1, one launch (start us, length us, event | category | flops | bytes accessed | tf_op | source)
XLA Modules:
  0.0 98.5 jit_solution(2390290867958585072)
XLA Ops:
  0.6 0.1 pad_add_fusion.place_ref
  0.7 3.7 %pick_rows.1 = (bf16[32,256]{1,0:T(8,128)(2,1)S(1)}, bf16[32,256]{1,0:T(8,128)(2,1)S(1)}) custom-call(s32[3]{0:T(128)S(1)} %pad_add_fusion.place_ref, s32[2048]{0:T(1024)} %wanted_ref.1, bf16[8192,256]{1,0:T(8,128)(2,1)} %pool_ref.1), custom_call_target="tpu_custom_call" | custom-call | tf_op jit(solution)/shard_map/pick_rows/pallas_call | solution.py:92
  4.4 1.4 %collective-permute-start = (bf16[32,256]{1,0:T(8,128)(2,1)S(1)}, bf16[32,256]{1,0:T(8,128)(2,1)S(1)}, u32[]{:S(2)}, u32[]{:S(2)}) collective-permute-start(bf16[32,256]{1,0:T(8,128)(2,1)S(1)} %get-tuple-element.30), channel_id=1, source_target_pairs={{0,32},{32,0},{1,33},{33,1},{2,34},{34,2},{3,35},{35,3},{4,36},{36... | collective-permute-start | bytes 49160 | tf_op jit(solution)/shard_map/ppermute | solution.py:505
  5.9 0.8 collective-permute-done
  6.7 3.8 %collective-permute-start.1 = (bf16[32,256]{1,0:T(8,128)(2,1)S(1)}, bf16[32,256]{1,0:T(8,128)(2,1)S(1)}, u32[]{:S(2)}, u32[]{:S(2)}) collective-permute-start(bf16[32,256]{1,0:T(8,128)(2,1)S(1)} %add.15.mine_ref), channel_id=1, source_target_pairs={{0,64},{64,0},{1,65},{65,1},{2,66},{66,2},{3,67},{67,3},{4,68},{68... | collective-permute-start | bytes 49160 | tf_op jit(solution)/shard_map/ppermute | solution.py:505
  10.5 0.7 collective-permute-start.2
  11.2 0.5 collective-permute-done.1.far_ref
  11.7 1.6 %collective-permute-done.2.near_ref = bf16[32,256]{1,0:T(8,128)(2,1)S(1)} collective-permute-done((bf16[32,256]{1,0:T(8,128)(2,1)S(1)}, bf16[32,256]{1,0:T(8,128)(2,1)S(1)}, u32[]{:S(2)}, u32[]{:S(2)}) %collective-permute-start.2) | collective-permute-done | bytes 16416 | tf_op jit(solution)/shard_map/ppermute | solution.py:505
  13.2 1.8 %collective-permute-done.3.across_ref = bf16[32,256]{1,0:T(8,128)(2,1)S(1)} collective-permute-done((bf16[32,256]{1,0:T(8,128)(2,1)S(1)}, bf16[32,256]{1,0:T(8,128)(2,1)S(1)}, u32[]{:S(2)}, u32[]{:S(2)}) %collective-permute-start.3) | collective-permute-done | bytes 16416 | tf_op jit(solution)/shard_map/ppermute | solution.py:521
  15.0 0.8 repeat_sum.1
  15.8 6.8 %all-to-all-start = ((bf16[16,64,256]{2,1,0:T(8,128)(2,1)}), bf16[16,64,256]{2,1,0:T(8,128)(2,1)S(1)}, u32[]{:S(2)}, u32[]{:S(2)}) async-start(bf16[16,64,256]{2,1,0:T(8,128)(2,1)} %repeat_sum.1), calls=%async_computation | async-start | bytes 1048576 | tf_op jit(solution)/shard_map/all_to_all | solution.py:509
  22.7 5.9 %prepare.1 = (bf16[16,8192]{1,0:T(8,128)(2,1)S(1)}, f32[1,8192]{1,0:T(1,128)S(1)}, bf16[2048,256]{1,0:T(8,128)(2,1)S(1)}, bf16[64,256]{1,0:T(8,128)(2,1)S(1)}, f...) custom-call(s32[64]{0:T(128)} %idx_ref.1, f32[16,8192]{1,0:T(8,128)} %w_ref.1, ...), custom_call_target="tpu_custom_call" | custom-call | flops 4000000000 | bytes 4194304 | tf_op jit(solution)/shard_map/prepare/pallas_call | solution.py:207
  28.6 3.4 %all-to-all-done = bf16[16,64,256]{2,1,0:T(8,128)(2,1)S(1)} async-done(((bf16[16,64,256]{2,1,0:T(8,128)(2,1)}), bf16[16,64,256]{2,1,0:T(8,128)(2,1)S(1)}, u32[]{:S(2)}, u32[]{:S(2)}) %all-to-all-start) | async-done | bytes 524320 | tf_op jit(solution)/shard_map/all_to_all | solution.py:509
  32.0 3.2 %collective-permute-start.4 = (bf16[1024,256]{1,0:T(8,128)(2,1)S(1)}, bf16[1024,256]{1,0:T(8,128)(2,1)S(1)}, u32[]{:S(2)}, u32[]{:S(2)}) collective-permute-start(bf16[1024,256]{1,0:T(8,128)(2,1)S(1)} %bitcast.6), channel_id=1, source_target_pairs={{0,32},{32,0},{1,33},{33,1},{2,34},{34,2},{3,35},{35,3},{4,36},{36... | collective-permute-start | bytes 1572872 | tf_op jit(solution)/shard_map/ppermute | solution.py:505
  35.1 10.5 %kernel_values.2 = (bf16[1024,8192]{1,0:T(8,128)(2,1)S(1)}, f32[16,8,128]{2,1,0:T(8,128)S(1)}, bf16[8192,256]{1,0:T(8,128)(2,1)S(1)}) custom-call(bf16[16,8192]{1,0:T(8,128)(2,1)S(1)} %get-tuple-element.45.w_ref, bf16[1024,256]{1,0:T(8,128)(2,1)S(1)} %bitcast.7, f32[1,8192]{1,0:T(1,128)S(1)} %get-tuple-element.46.cen_sq_ref, bf16[8192,256]{1,0:T(8,128)(2,1)} %cen_ref.3, ...), custom_call_target="tpu_custom_call" | custom-call | flops 17179869184 | bytes 16777216 | tf_op jit(solution)/shard_map/kernel_values/pallas_call | solution.py:284
  45.6 0.0 collective-permute-done.4.other_ref.batch_ref
  45.6 1.2 %nystrom_terms.1 = (bf16[64,16,128]{2,1,0:T(8,128)(2,1)S(1)}, bf16[64,16,128]{2,1,0:T(8,128)(2,1)S(1)}) custom-call(s32[1]{0:T(128)} %bitcast.core_ref, bf16[64,256]{1,0:T(8,128)(2,1)S(1)} %get-tuple-element.38.cen_ref.refs_1_, f32[1,64]{1,0:T(1,128)S(1)} %get-tuple-element.39.sq_ref.refs_2_, bf16[128,64]{1,0:T(8,128)(2,1)S(1)} %get-tuple-element.40.hi_ref.refs_3_, ...), custom_call_target="tpu_custom_call" | custom-call | flops 2000000000 | bytes 1048576 | tf_op jit(solution)/shard_map/nystrom_terms/pallas_call | solution.py:325
  46.8 0.1 collective-permute-start.5
  46.9 0.0 copy-start
  46.9 10.4 %kernel_values.3 = (bf16[1024,8192]{1,0:T(8,128)(2,1)S(1)}, f32[16,8,128]{2,1,0:T(8,128)S(1)}) custom-call(bf16[16,8192]{1,0:T(8,128)(2,1)S(1)} %get-tuple-element.45.w_ref, bf16[1024,256]{1,0:T(8,128)(2,1)S(1)} %collective-permute-done.4.other_ref.batch_ref, f32[1,8192]{1,0:T(1,128)S(1)} %get-tuple-element.46.cen_sq_ref, ...), custom_call_target="tpu_custom_call" | custom-call | flops 17179869184 | bytes 16777216 | tf_op jit(solution)/shard_map/kernel_values/pallas_call | solution.py:284
  57.4 0.6 collective-permute-start.6
  57.9 0.9 collective-permute-done.6.pred_in_ref
  58.8 0.0 collective-permute-done.5.moment_in_ref
  58.8 0.2 pack.1
  59.0 15.1 %all_to_all.15.part_ref = bf16[64,24,128]{2,1,0:T(8,128)(2,1)S(1)} all-to-all(bf16[64,24,128]{2,1,0:T(8,128)(2,1)S(1)} %pack.1), channel_id=1, replica_groups=mesh['zh'=2,'core'=2,'y'=4,'zl'=2,'x'=4] {'zh','y','zl','x'}, dimensions={0} | all-to-all | bytes 786432 | tf_op jit(solution)/shard_map/all_to_all | solution.py:509
  74.1 0.1 sum_chips.1
  74.2 14.3 %all_to_all.16.mine_ref = bf16[64,24,128]{2,1,0:T(8,128)(2,1)S(1)} all-to-all(bf16[64,24,128]{2,1,0:T(8,128)(2,1)S(1)} %sum_chips.1), channel_id=1, replica_groups=mesh['zh'=2,'core'=2,'y'=4,'zl'=2,'x'=4] {'zh','y','zl','x'}, dimensions={0} | all-to-all | bytes 786432 | tf_op jit(solution)/shard_map/all_to_all | solution.py:509
  88.5 2.9 %collective-permute-start.7 = (bf16[64,24,128]{2,1,0:T(8,128)(2,1)S(1)}, bf16[64,24,128]{2,1,0:T(8,128)(2,1)S(1)}, u32[]{:S(2)}, u32[]{:S(2)}) collective-permute-start(bf16[64,24,128]{2,1,0:T(8,128)(2,1)S(1)} %all_to_all.16.mine_ref), channel_id=1, source_target_pairs={{0,32},{32,0},{1,33},{33,1},{2,34},{34,2},{3,35},{35,3},{4,36},{36... | collective-permute-start | bytes 1179656 | tf_op jit(solution)/shard_map/ppermute | solution.py:505
  91.5 0.0 copy-start.4
  91.5 2.4 %own_grad.1 = (f32[16,1024]{1,0:T(8,128)S(1)}, bf16[16,1024]{1,0:T(8,128)(2,1)S(1)}, f32[16,8192]{1,0:T(8,128)S(1)}) custom-call(s32[1]{0:T(128)} %bitcast.core_ref, bf16[64,24,128]{2,1,0:T(8,128)(2,1)S(1)} %all_to_all.16.mine_ref, f32[16,2048]{1,0:T(8,128)S(1)} %copy-done, bf16[1024,8192]{1,0:T(8,128)(2,1)S(1)} %get-tuple-element.51.kern_ref), custom_call_target="tpu_custom_call" | custom-call | flops 4294967296 | bytes 16777216 | tf_op jit(solution)/shard_map/own_grad/pallas_call | solution.py:426
  93.9 0.0 copy-done.2
  93.9 4.6 %finish.1 = (f32[16,8192]{1,0:T(8,128)}, f32[16,2048]{1,0:T(8,128)}) custom-call(s32[1]{0:T(128)} %bitcast.core_ref, s32[64]{0:T(128)S(1)} %copy-done.3, bf16[64,24,128]{2,1,0:T(8,128)(2,1)S(1)} %all_to_all.16.mine_ref, bf16[64,24,128]{2,1,0:T(8,128)(2,1)S(1)} %collective-permute-done.7.got_ref, f32[16,1024]{1,0:T(8,128)S(1)} %get-tuple-element.52.pred_ref, ...), custom_call_target="tpu_custom_call" | custom-call | tf_op jit(solution)/shard_map/finish/pallas_call | solution.py:490
  (10 shorter events, 0.0 us)
Async XLA Ops:
  4.4 2.3 %collective-permute-start = (bf16[32,256]{1,0:T(8,128)(2,1)S(1)}, bf16[32,256]{1,0:T(8,128)(2,1)S(1)}, u32[]{:S(2)}, u32[]{:S(2)}) collective-permute-start(bf16[32,256]{1,0:T(8,128)(2,1)S(1)} %get-tuple-element.30), channel_id=1, source_target_pairs={{0,32},{32,0},{1,33},{33,1},{2,34},{34,2},{3,35},{35,3},{4,36},{36... | collective-permute-start | bytes 49160 | tf_op jit(solution)/shard_map/ppermute | solution.py:505
  6.7 4.9 %collective-permute-start.1 = (bf16[32,256]{1,0:T(8,128)(2,1)S(1)}, bf16[32,256]{1,0:T(8,128)(2,1)S(1)}, u32[]{:S(2)}, u32[]{:S(2)}) collective-permute-start(bf16[32,256]{1,0:T(8,128)(2,1)S(1)} %add.15.mine_ref), channel_id=1, source_target_pairs={{0,64},{64,0},{1,65},{65,1},{2,66},{66,2},{3,67},{67,3},{4,68},{68... | collective-permute-start | bytes 49160 | tf_op jit(solution)/shard_map/ppermute | solution.py:505
  10.5 2.7 %collective-permute-start.2 = (bf16[32,256]{1,0:T(8,128)(2,1)S(1)}, bf16[32,256]{1,0:T(8,128)(2,1)S(1)}, u32[]{:S(2)}, u32[]{:S(2)}) collective-permute-start(bf16[32,256]{1,0:T(8,128)(2,1)S(1)} %add.15.mine_ref), channel_id=1, source_target_pairs={{0,4},{4,0},{1,5},{5,1},{2,6},{6,2},{3,7},{7,3},{8,12},{12,8},{9,1... | collective-permute-start | bytes 49160 | tf_op jit(solution)/shard_map/ppermute | solution.py:505
  11.2 3.8 %collective-permute-start.3 = (bf16[32,256]{1,0:T(8,128)(2,1)S(1)}, bf16[32,256]{1,0:T(8,128)(2,1)S(1)}, u32[]{:S(2)}, u32[]{:S(2)}) collective-permute-start(bf16[32,256]{1,0:T(8,128)(2,1)S(1)} %add.15.mine_ref), channel_id=1, source_target_pairs={{0,68},{4,64},{64,4},{68,0},{1,69},{5,65},{65,5},{69,1},{2,70},{6,... | collective-permute-start | bytes 49160 | tf_op jit(solution)/shard_map/ppermute | solution.py:521
  15.8 16.1 %all-to-all-start = ((bf16[16,64,256]{2,1,0:T(8,128)(2,1)}), bf16[16,64,256]{2,1,0:T(8,128)(2,1)S(1)}, u32[]{:S(2)}, u32[]{:S(2)}) async-start(bf16[16,64,256]{2,1,0:T(8,128)(2,1)} %repeat_sum.1), calls=%async_computation | async-start | bytes 1048576 | tf_op jit(solution)/shard_map/all_to_all | solution.py:509
  32.0 13.7 %collective-permute-start.4 = (bf16[1024,256]{1,0:T(8,128)(2,1)S(1)}, bf16[1024,256]{1,0:T(8,128)(2,1)S(1)}, u32[]{:S(2)}, u32[]{:S(2)}) collective-permute-start(bf16[1024,256]{1,0:T(8,128)(2,1)S(1)} %bitcast.6), channel_id=1, source_target_pairs={{0,32},{32,0},{1,33},{33,1},{2,34},{34,2},{3,35},{35,3},{4,36},{36... | collective-permute-start | bytes 1572872 | tf_op jit(solution)/shard_map/ppermute | solution.py:505
  46.8 12.0 %collective-permute-start.5 = (bf16[64,16,128]{2,1,0:T(8,128)(2,1)S(1)}, bf16[64,16,128]{2,1,0:T(8,128)(2,1)S(1)}, u32[]{:S(2)}, u32[]{:S(2)}) collective-permute-start(bf16[64,16,128]{2,1,0:T(8,128)(2,1)S(1)} %get-tuple-element.44.refs_0_), channel_id=1, source_target_pairs={{0,32},{32,0},{1,33},{33,1},{2,34},{34,2},{3,35},{35,3},{4,36},{36... | collective-permute-start | bytes 786440 | tf_op jit(solution)/shard_map/ppermute | solution.py:505
  46.9 44.5 %copy-start = (f32[16,2048]{1,0:T(8,128)S(1)}, f32[16,2048]{1,0:T(8,128)}, u32[]{:S(2)}) copy-start(f32[16,2048]{1,0:T(8,128)} %tgt_ref.3) | copy-start | bytes 393220
  57.4 1.5 %collective-permute-start.6 = (f32[16,8,128]{2,1,0:T(8,128)S(1)}, f32[16,8,128]{2,1,0:T(8,128)S(1)}, u32[]{:S(2)}, u32[]{:S(2)}) collective-permute-start(f32[16,8,128]{2,1,0:T(8,128)S(1)} %get-tuple-element.50), channel_id=1, source_target_pairs={{0,32},{32,0},{1,33},{33,1},{2,34},{34,2},{3,35},{35,3},{4,36},{36... | collective-permute-start | bytes 196616 | tf_op jit(solution)/shard_map/ppermute | solution.py:505
  88.5 5.3 %collective-permute-start.7 = (bf16[64,24,128]{2,1,0:T(8,128)(2,1)S(1)}, bf16[64,24,128]{2,1,0:T(8,128)(2,1)S(1)}, u32[]{:S(2)}, u32[]{:S(2)}) collective-permute-start(bf16[64,24,128]{2,1,0:T(8,128)(2,1)S(1)} %all_to_all.16.mine_ref), channel_id=1, source_target_pairs={{0,32},{32,0},{1,33},{33,1},{2,34},{34,2},{3,35},{35,3},{4,36},{36... | collective-permute-start | bytes 1179656 | tf_op jit(solution)/shard_map/ppermute | solution.py:505
  91.5 2.4 %copy-start.1 = (f32[16,8192]{1,0:T(8,128)S(1)}, f32[16,8192]{1,0:T(8,128)}, u32[]{:S(2)}) copy-start(f32[16,8192]{1,0:T(8,128)} %w_ref.1) | copy-start | bytes 1572868
  91.5 2.4 %copy-start.2 = (f32[64,128]{1,0:T(8,128)S(1)}, f32[64,128]{1,0:T(8,128)}, u32[]{:S(2)}) copy-start(f32[64,128]{1,0:T(8,128)} %eig_ref.1) | copy-start | bytes 98308
  91.5 2.4 %copy-start.3 = (s32[64]{0:T(128)S(1)}, s32[64]{0:T(128)}, u32[]{:S(2)}) copy-start(s32[64]{0:T(128)} %idx_ref.1) | copy-start | bytes 772
  91.5 2.4 %copy-start.4 = (f32[128]{0:T(128)S(1)}, f32[128]{0:T(128)}, u32[]{:S(2)}) copy-start(f32[128]{0:T(128)} %param.15) | copy-start | bytes 1540
